TPU v7x, 128 devices: a whole 4x4x4 slice. The times are simulated.
128 devices in a mesh: section: 2 (over x_hi), dp: 64 (over y, x_lo, z, core).
Axes of the slice: x: 4 (x_hi: 2, x_lo: 2; x = x_hi * 2 + x_lo), y: 4, z: 4, core: 2. Of those that a mesh axis runs over, the one named last changes fastest.
Arguments:
- inputs: bfloat16 [2, 8192, 960], P(None, 'dp'), may hold values from -40 to 40
- segment_ids: int32 [2, 8192], P(None, 'dp'), may hold values from 0 to 127, never falling along the last dimension, each value on 1 to 128 neighbouring positions
- qkv_weight: bfloat16 [2, 960, 1600], P('section', 'dp'), may hold values from -0.1875 to 0.1875
- out_weight: bfloat16 [2, 960, 960], P('section', 'dp'), may hold values from -0.75 to 0.75
- gate_up_weight: bfloat16 [2, 960, 5120], P('section', 'dp'), may hold values from -0.1875 to 0.1875
- down_weight: bfloat16 [2, 2560, 960], P('section', 'dp'), may hold values from -0.125 to 0.125
- norm_gains: bfloat16 [2, 960, 2], P('section', 'dp'), may hold values from 0.099609375 to 1.8984375
- cotangent: bfloat16 [2, 8192, 960], P(None, 'dp'), may hold values from -6 to 6
Outputs:
- section_outputs: bfloat16 [2, 2, 8192, 960], P('section', None, 'dp')
- section_input_grads: bfloat16 [2, 2, 8192, 960], P('section', None, 'dp')
- qkv_grad: float32 [2, 960, 1600], P('section', 'dp')
- out_grad: float32 [2, 960, 960], P('section', 'dp')
- gate_up_grad: float32 [2, 960, 5120], P('section', 'dp')
- down_grad: float32 [2, 2560, 960], P('section', 'dp')
- gains_grad: float32 [2, 960, 2], P('section', 'dp')
Inputs may be any that keep to these rules, and one draw needn't show every extreme that they name: `segment_ids`: within each micro-batch the document numbers never fall along the tokens, and each number names 1 to 128 tokens in a row.
All inputs are finite; a program needn't handle non-finite values.
Results may differ from a plain program's by a relative error of at most 0.02.
Values may be sent and summed in bfloat16 or wider, within the bound.
No kernel may reach another device: no remote copies, remote signals or barrier semaphores. Data moves between devices by JAX's collectives and lax.ppermute only.
A program may use at most 256 MiB of HBM per device.

v0:
```python
import jax
import jax.numpy as jnp
from jax import lax
from jax.sharding import PartitionSpec as P

D = 960
H = 15
KV = 5
HD = 64
FF = 2560


EPSILON = 1e-05
ROPE_BASE = 100000.0


def shifted(block, axis, distance):
    devices = range(lax.axis_size(axis))
    route = [(i - distance, i) for i in devices if i - distance in devices]
    return lax.ppermute(block, axis, route)


def rope_tables(length):
    position = jnp.arange(length, dtype=jnp.float32)[:, None]
    frequency = ROPE_BASE ** (-jnp.arange(0, HD, 2, dtype=jnp.float32) / HD)
    angle = position * frequency[None, :]
    return (jnp.cos(angle), jnp.sin(angle))


def rotate(vector, cosine_table, sine_table):
    halfway = vector.shape[-1] // 2
    first_half = vector[..., :halfway]
    second_half = vector[..., halfway:]
    cosine = cosine_table[:, None, :]
    sine_part = sine_table[:, None, :]
    return jnp.concatenate(
        [
            first_half * cosine - second_half * sine_part,
            second_half * cosine + first_half * sine_part,
        ],
        -1,
    )


def unrotate(vector, cosine_table, sine_table):
    halfway = vector.shape[-1] // 2
    first_half = vector[..., :halfway]
    second_half = vector[..., halfway:]
    cosine = cosine_table[:, None, :]
    sine_part = sine_table[:, None, :]
    return jnp.concatenate(
        [
            first_half * cosine + second_half * sine_part,
            second_half * cosine - first_half * sine_part,
        ],
        -1,
    )


def normalize(vector, gain):
    return vector * lax.rsqrt(jnp.mean(vector * vector, axis=-1, keepdims=True) + EPSILON) * gain


def swiglu(gate_part, up_part):
    return jax.nn.silu(gate_part) * up_part


def attention_scores(queries, keys_rot, allowed):
    scores = jnp.einsum(
        "qkgd,tkd->kgqt", queries, keys_rot, preferred_element_type=jnp.float32
    ) * HD ** (-0.5)
    return jnp.where(allowed, scores, -1000000000.0)


def layer_forward(layer_in, seg_row, weights):
    qkv_mat, out_mat, gate_up_mat, down_mat, gain_pair = weights
    length = layer_in.shape[0]
    cosine_table, sine_table = rope_tables(length)
    gains_full = gain_pair.astype(jnp.float32)
    stream = layer_in.astype(jnp.float32)
    hidden_one = normalize(stream, gains_full[:, 0]).astype(jnp.bfloat16)
    projected = jnp.dot(hidden_one, qkv_mat, preferred_element_type=jnp.float32)
    queries = rotate(projected[:, :D].reshape(length, H, HD), cosine_table, sine_table)
    queries = queries.astype(jnp.bfloat16).reshape(length, KV, H // KV, HD)
    keys_rot = rotate(
        projected[:, D : D + KV * HD].reshape(length, KV, HD), cosine_table, sine_table
    ).astype(jnp.bfloat16)
    values = projected[:, D + KV * HD :].reshape(length, KV, HD).astype(jnp.bfloat16)
    positions = jnp.arange(length)
    allowed = (seg_row[:, None] == seg_row[None, :]) & (positions[:, None] >= positions[None, :])
    scores = attention_scores(queries, keys_rot, allowed)
    row_max = jnp.max(scores, axis=-1, keepdims=True)
    exp_scores = jnp.exp(scores - row_max)
    row_total = jnp.sum(exp_scores, axis=-1, keepdims=True)
    attn_probs = exp_scores / row_total
    log_total = row_max + jnp.log(row_total)
    attended = jnp.einsum(
        "kgqt,tkd->qkgd",
        attn_probs.astype(jnp.bfloat16),
        values,
        preferred_element_type=jnp.float32,
    )
    attended = attended.reshape(length, D).astype(jnp.bfloat16)
    middle = stream + jnp.dot(attended, out_mat, preferred_element_type=jnp.float32)
    hidden_two = normalize(middle, gains_full[:, 1]).astype(jnp.bfloat16)
    gate_up = jnp.dot(hidden_two, gate_up_mat, preferred_element_type=jnp.float32)
    activated = swiglu(gate_up[:, :FF], gate_up[:, FF:]).astype(jnp.bfloat16)
    layer_out = middle + jnp.dot(activated, down_mat, preferred_element_type=jnp.float32)
    kept = (
        stream,
        hidden_one,
        queries,
        keys_rot,
        values,
        allowed,
        log_total,
        attended,
        middle,
        hidden_two,
        gate_up,
        activated,
    )
    return (kept, layer_out)


def layer_backward(kept, grad_out, weights):
    qkv_mat, out_mat, gate_up_mat, down_mat, gain_pair = weights
    (
        stream,
        hidden_one,
        queries,
        keys_rot,
        values,
        allowed,
        log_total,
        attended,
        middle,
        hidden_two,
        gate_up,
        activated,
    ) = kept
    length = stream.shape[0]
    cosine_table, sine_table = rope_tables(length)
    gains_full = gain_pair.astype(jnp.float32)
    grad_down = grad_out.astype(jnp.bfloat16)
    grad_act = jnp.dot(grad_down, down_mat.T, preferred_element_type=jnp.float32)
    unused, swiglu_back = jax.vjp(swiglu, gate_up[:, :FF], gate_up[:, FF:])
    grad_gate, grad_upper = swiglu_back(grad_act)
    grad_gate_up = jnp.concatenate([grad_gate, grad_upper], -1).astype(jnp.bfloat16)
    grad_two = jnp.dot(grad_gate_up, gate_up_mat.T, preferred_element_type=jnp.float32)
    unused, norm_back_two = jax.vjp(normalize, middle, gains_full[:, 1])
    grad_norm_two, gain_two = norm_back_two(grad_two)
    grad_middle = grad_out + grad_norm_two
    grad_attn = grad_middle.astype(jnp.bfloat16)
    grad_mixed = jnp.dot(grad_attn, out_mat.T, preferred_element_type=jnp.float32).astype(
        jnp.bfloat16
    )
    grad_mixed = grad_mixed.reshape(length, KV, H // KV, HD)
    scores = attention_scores(queries, keys_rot, allowed)
    attn_probs = jnp.exp(scores - log_total)
    grad_probs = jnp.einsum(
        "qkgd,tkd->kgqt", grad_mixed, values, preferred_element_type=jnp.float32
    )
    grad_scores = attn_probs * (
        grad_probs - jnp.sum(grad_probs * attn_probs, axis=-1, keepdims=True)
    )
    grad_scores = grad_scores.astype(jnp.bfloat16)
    grad_queries = jnp.einsum(
        "kgqt,tkd->qkgd", grad_scores, keys_rot, preferred_element_type=jnp.float32
    ) * HD ** (-0.5)
    grad_keys = jnp.einsum(
        "kgqt,qkgd->tkd", grad_scores, queries, preferred_element_type=jnp.float32
    ) * HD ** (-0.5)
    grad_values = jnp.einsum(
        "kgqt,qkgd->tkd",
        attn_probs.astype(jnp.bfloat16),
        grad_mixed,
        preferred_element_type=jnp.float32,
    )
    grad_queries = grad_queries.astype(jnp.bfloat16).reshape(length, H, HD).astype(jnp.float32)
    grad_keys = grad_keys.astype(jnp.bfloat16).astype(jnp.float32)
    grad_q_pre = (
        unrotate(grad_queries, cosine_table, sine_table).astype(jnp.bfloat16).reshape(length, D)
    )
    grad_k_pre = (
        unrotate(grad_keys, cosine_table, sine_table).astype(jnp.bfloat16).reshape(length, KV * HD)
    )
    grad_v_pre = grad_values.astype(jnp.bfloat16).reshape(length, KV * HD)
    grad_proj = jnp.concatenate([grad_q_pre, grad_k_pre, grad_v_pre], -1)
    grad_one = jnp.dot(grad_proj, qkv_mat.T, preferred_element_type=jnp.float32)
    unused, norm_back_one = jax.vjp(normalize, stream, gains_full[:, 0])
    grad_norm_one, gain_one = norm_back_one(grad_one)
    grad_in = grad_middle + grad_norm_one
    pieces = (
        hidden_one,
        grad_proj,
        attended,
        grad_attn,
        hidden_two,
        grad_gate_up,
        activated,
        grad_down,
        jnp.stack([gain_one, gain_two], -1),
    )
    return (grad_in, pieces)


def contract(left_rows, right_rows):
    return lax.dot_general(
        left_rows, right_rows, (((0,), (0,)), ((), ())), preferred_element_type=jnp.float32
    )


def grad_terms(stacked, gain_sum):
    return (
        contract(stacked[0], stacked[1])[None],
        contract(stacked[2], stacked[3])[None],
        contract(stacked[4], stacked[5])[None],
        contract(stacked[6], stacked[7])[None],
        gain_sum[None],
    )


def per_device(
    inputs, segment_ids, qkv_weight, out_weight, gate_up_weight, down_weight, norm_gains, cotangent
):
    batches = inputs.shape[0]
    is_first = lax.axis_index("section") == 0
    gathered = (
        lax.all_gather(qkv_weight, "dp", axis=1, tiled=True),
        lax.all_gather(out_weight, "dp", axis=1, tiled=True),
        lax.all_gather(gate_up_weight, "dp", axis=1, tiled=True),
        lax.all_gather(down_weight, "dp", axis=1, tiled=True),
        lax.all_gather(norm_gains, "dp", axis=1, tiled=True),
    )
    weights = tuple((piece[0] for piece in gathered))
    received = jnp.zeros(inputs.shape[1:], jnp.bfloat16)
    saved = []
    produced = []
    for turn in range(batches + 1):
        own_input = inputs[min(turn, batches - 1)]
        layer_in = jnp.where(is_first, own_input, received)
        seg_row = jnp.where(
            is_first, segment_ids[min(turn, batches - 1)], segment_ids[max(turn - 1, 0)]
        )
        kept, layer_out = layer_forward(layer_in, seg_row, weights)
        layer_out = layer_out.astype(jnp.bfloat16)
        saved.append(kept)
        produced.append(layer_out)
        if turn < batches:
            received = shifted(layer_out, "section", 1)
    section_outputs = jnp.stack(
        [
            jnp.where(is_first, produced[position], produced[position + 1])
            for position in range(batches)
        ]
    )[None]
    gathered_back = (
        lax.all_gather(qkv_weight, "dp", axis=1, tiled=True),
        lax.all_gather(out_weight, "dp", axis=1, tiled=True),
        lax.all_gather(gate_up_weight, "dp", axis=1, tiled=True),
        lax.all_gather(down_weight, "dp", axis=1, tiled=True),
        lax.all_gather(norm_gains, "dp", axis=1, tiled=True),
    )
    weights_back = tuple((piece[0] for piece in gathered_back))
    received = jnp.zeros(inputs.shape[1:], jnp.bfloat16)
    returned = []
    collected = []
    owned = None
    for turn in range(batches + 1):
        if turn < batches:
            own_grad = cotangent[turn]
        else:
            own_grad = jnp.zeros(inputs.shape[1:], jnp.bfloat16)
        grad_out = jnp.where(is_first, received, own_grad).astype(jnp.float32)
        kept = jax.tree.map(
            lambda for_first, for_second: jnp.where(is_first, for_first, for_second),
            saved[max(turn - 1, 0)],
            saved[min(turn + 1, batches)],
        )
        grad_in, pieces = layer_backward(kept, grad_out, weights_back)
        grad_in = grad_in.astype(jnp.bfloat16)
        returned.append(grad_in)
        collected.append(pieces)
        if turn < batches:
            received = shifted(grad_in, "section", -1)
    section_input_grads = jnp.stack(
        [
            jnp.where(is_first, returned[position + 1], returned[position])
            for position in range(batches)
        ]
    )[None]
    stacked = [jnp.concatenate([pieces[member] for pieces in collected], 0) for member in range(8)]
    gain_sum = collected[0][8]
    for pieces in collected[1:]:
        gain_sum = gain_sum + pieces[8]
    owned = lax.psum_scatter(grad_terms(stacked, gain_sum), "dp", scatter_dimension=1, tiled=True)
    return (section_outputs, section_input_grads, owned[0], owned[1], owned[2], owned[3], owned[4])


def solution(mesh):
    in_specs = (
        P(None, "dp", None),
        P(None, "dp"),
        P("section", "dp", None),
        P("section", "dp", None),
        P("section", "dp", None),
        P("section", "dp", None),
        P("section", "dp", None),
        P(None, "dp", None),
    )
    out_specs = (
        P("section", None, "dp", None),
        P("section", None, "dp", None),
        P("section", "dp", None),
        P("section", "dp", None),
        P("section", "dp", None),
        P("section", "dp", None),
        P("section", "dp", None),
    )
    return jax.shard_map(
        per_device, mesh=mesh, in_specs=in_specs, out_specs=out_specs, check_vma=False
    )
```

profile of v0, /device:TPU:0, one launch (start us, length us, event | category | flops | bytes accessed | tf_op | source)
XLA Modules:
  0.0 2363.4 jit_solution(15730589190905274555)
XLA Ops:
  7.2 1.5 copy.55
  8.8 1.5 copy.53
  10.4 1.9 copy.56
  13.7 85.3 %all_gather.20 = bf16[1,960,2]{2,0,1:T(2,128)(2,1)S(1)} all-gather(bf16[1,15,2]{2,0,1:T(2,128)(2,1)S(1)} %copy.52), channel_id=1, replica_groups=mesh['section'=2,'dp'=64] {'dp'}, dimensions={1}, use_global_device_ids=true | all-gather | bytes 3900 | tf_op jit(solution)/shard_map/all_gather | solution.py:234
  101.1 17.6 all-gather.7.cloned.1.call-done
  118.7 2.9 copy.106
  121.6 107.3 %all-gather.5.cloned.1.call-done = bf16[1,960,1600]{2,0,1:T(2,128)(2,1)} async-done(((bf16[1,15,1600]{2,0,1:T(2,128)(2,1)}), bf16[1,960,1600]{2,0,1:T(2,128)(2,1)}) %all-gather.5.cloned.1.call-update) | async-done | bytes 3072016 | tf_op jit(solution)/shard_map/all_gather | solution.py:230
  228.8 3.3 copy.105
  232.2 1.6 fusion.45
  235.7 0.9 multiply_reduce_fusion.23
  236.7 120.1 %all-gather.9.cloned.1.call-done = bf16[1,960,5120]{2,0,1:T(2,128)(2,1)} async-done(((bf16[1,15,5120]{2,0,1:T(2,128)(2,1)}), bf16[1,960,5120]{2,0,1:T(2,128)(2,1)}) %all-gather.9.cloned.1.call-update) | async-done | bytes 9830416 | tf_op jit(solution)/shard_map/all_gather | solution.py:232
  356.7 10.9 copy.107
  367.6 3.8 copy-done
  371.4 3.1 fusion.10
  374.6 90.7 %all-gather.11.cloned.1.call-done = bf16[1,2560,960]{2,1,0:T(8,128)(2,1)} async-done(((bf16[1,40,960]{2,1,0:T(8,128)(2,1)}), bf16[1,2560,960]{2,1,0:T(8,128)(2,1)}) %all-gather.11.cloned.1.call-update) | async-done | bytes 4915216 | tf_op jit(solution)/shard_map/all_gather | solution.py:233
  465.3 5.3 fusion.144
  470.5 5.1 collective-permute-start
  475.7 5.3 collective-permute-done
  481.2 1.6 fusion.43
  484.5 0.9 multiply_reduce_fusion.20
  485.5 0.9 broadcast_select_fusion.14
  486.4 1.7 broadcast_select_fusion.2
  488.3 2.3 fusion.84
  490.6 3.4 multiply_reduce_fusion.7
  496.8 2.1 broadcast_select_fusion.5
  498.9 1.8 fusion.141
  500.7 5.9 collective-permute-start.1
  507.1 4.2 collective-permute-done.1
  511.4 2.6 multiply_reduce_fusion.8
  514.5 1.6 fusion.41
  518.0 1.2 broadcast_select_fusion.8
  519.2 2.4 multiply_reduce_fusion.12
  521.6 1.0 broadcast_select_fusion.13
  522.6 5.2 broadcast_select_fusion
  529.7 1.7 collective-permute-start.2
  531.9 7.8 collective-permute-done.2
  539.7 2.3 fusion.87
  542.0 3.4 multiply_reduce_fusion.5
  548.0 1.7 multiply_reduce_fusion.6
  549.8 1.3 select_bitcast_fusion
  551.1 1.4 collective-permute-start.3
  552.6 8.2 collective-permute-done.3
  561.6 5.2 convolution_bitcast_fusion.1
  566.8 22.1 copy.71
  589.9 1.3 fusion.81
  591.3 5.4 fusion.90
  596.8 7.6 multiply_reduce_fusion.3
  607.7 1.1 copy-done.4
  608.8 1.1 multiply_reduce_fusion.4
  611.3 1.9 convolution_bitcast_fusion.2
  613.3 10.7 copy.68
  624.0 1.2 convolution_bitcast_fusion.3
  625.2 6.0 copy.69
  632.9 13.5 convolution_bitcast_fusion
  646.4 24.9 %copy.70 = f32[1,960,5120]{2,0,1:T(1,128)} copy(f32[1,960,5120]{2,1,0:T(8,128)} %convolution_bitcast_fusion) | data formatting | bytes 39321600 | tf_op jit(solution)/shard_map/broadcast_in_dim | solution.py:218
  674.0 4.3 fusion.180
  679.1 140.6 %all-reduce.4 = f32[1,960,2]{1,2,0:T(2,128)S(1)} all-reduce(f32[1,960,2]{1,2,0:T(2,128)S(1)} %fusion.280), channel_id=6, replica_groups=mesh['section'=2,'dp'=64] {'dp'}, use_global_device_ids=true, to_apply=%region_37.38.clone | all-reduce | flops 1920 | bytes 15360
  821.2 343.4 %all-reduce.12.cloned.1.call-done = f32[1,2560,960]{2,0,1:T(1,128)} async-done(((f32[1,2560,960]{2,0,1:T(1,128)}), f32[1,2560,960]{2,0,1:T(1,128)}) %all-reduce.12.cloned.1.call-update) | async-done | bytes 9830416
  1164.5 0.9 constant_dynamic-slice_fusion.1
  1166.2 580.5 %all-reduce.14.cloned.1.call-done = (f32[1,960,1600]{2,0,1:T(1,128)}, f32[1,960,960]{2,0,1:T(1,128)}) async-done(((f32[1,960,1600]{2,0,1:T(1,128)}, f32[1,960,960]{2,0,1:T(1,128)}), (f32[1,960,1600]{2,0,1:T(1,128)}, f32[1,960,960]{2,0,1:T(1,128)})) %all-reduce.14.cloned.1.call-update) | async-done | bytes 9830416
  1746.7 1.5 constant_dynamic-slice_fusion.3
  1748.1 1.5 constant_dynamic-slice_fusion.4
  1749.7 604.8 %all-reduce.10.cloned.1.call-done = f32[1,960,5120]{2,0,1:T(1,128)} async-done(((f32[1,960,5120]{2,0,1:T(1,128)}), f32[1,960,5120]{2,0,1:T(1,128)}) %all-reduce.10.cloned.1.call-update) | async-done | bytes 19660816
  2354.4 1.7 constant_dynamic-slice_fusion.2
  (450 shorter events, 29.5 us)
Async XLA Ops:
  7.2 92.3 %copy-start.5 = (bf16[2,128,960]{1,2,0:T(8,128)(2,1)S(1)}, bf16[2,128,960]{1,2,0:T(8,128)(2,1)}, u32[]{:S(2)}) copy-start(bf16[2,128,960]{1,2,0:T(8,128)(2,1)} %param.8) | copy-start | bytes 1474564
  7.2 111.5 %all-gather.7.cloned.1.call-start = ((), (), s32[]{:S(2)}) async-start(), calls=%async_computation.1 | async-start | bytes 3993600 | tf_op jit(solution)/shard_map/all_gather | solution.py:231
  8.7 91.5 %copy-start.125 = (s32[2,128]{1,0:T(2,128)S(1)}, s32[2,128]{1,0:T(2,128)}, u32[]{:S(2)}) copy-start(s32[2,128]{1,0:T(2,128)} %param.9) | copy-start | bytes 3076
  8.7 220.1 %all-gather.5.cloned.1.call-start = ((), (), s32[]{:S(2)}) async-start(), calls=%async_computation | async-start | bytes 6489600 | tf_op jit(solution)/shard_map/all_gather | solution.py:230
  10.3 346.4 %all-gather.9.cloned.1.call-start = ((), (), s32[]{:S(2)}) async-start(), calls=%async_computation.2 | async-start | bytes 19968000 | tf_op jit(solution)/shard_map/all_gather | solution.py:232
  12.3 453.0 %all-gather.11.cloned.1.call-start = ((), (), s32[]{:S(2)}) async-start(), calls=%async_computation.3 | async-start | bytes 5324800 | tf_op jit(solution)/shard_map/all_gather | solution.py:233
  12.9 1151.7 %all-reduce.12.cloned.1.call-start = ((), (), s32[]{:S(2)}) async-start(), calls=%async_computation.5 | async-start | bytes 20971520
  100.1 267.5 %copy-start.43 = (f32[960]{0:T(1024)}, f32[960]{0:T(1024)S(1)}, u32[]{:S(2)}) copy-start(f32[960]{0:T(1024)S(1)} %get-tuple-element.42) | copy-start | bytes 11524
  100.1 381.1 %copy-start.78 = (f32[960]{0:T(1024)}, f32[960]{0:T(1024)S(1)}, u32[]{:S(2)}) copy-start(f32[960]{0:T(1024)S(1)} %get-tuple-element.43) | copy-start | bytes 11524
  100.2 132.0 %copy-start.122 = (f32[128]{0:T(128)}, f32[128]{0:T(128)S(1)}, u32[]{:S(2)}) copy-start(f32[128]{0:T(128)S(1)} %add_rsqrt_fusion.5) | copy-start | bytes 1540
  236.6 131.0 %copy-start.118 = (f32[128]{0:T(128)}, f32[128]{0:T(128)S(1)}, u32[]{:S(2)}) copy-start(f32[128]{0:T(128)S(1)} %add_rsqrt_fusion.4) | copy-start | bytes 1540
  367.6 3.8 copy-start
  374.6 101.1 %copy-start.25 = (bf16[2,128,960]{1,2,0:T(8,128)(2,1)S(1)}, bf16[2,128,960]{1,2,0:T(8,128)(2,1)}, u32[]{:S(2)}) copy-start(bf16[2,128,960]{1,2,0:T(8,128)(2,1)} %param.15) | copy-start | bytes 1474564
  465.3 16.0 copy-start.3
  465.3 21.1 slice-start
  465.3 21.1 slice-start.1
  470.5 12.3 copy-start.69
  470.5 10.4 collective-permute-start
  475.7 12.5 copy-start.32
  481.2 17.7 copy-start.138
  483.1 13.1 copy-start.81
  483.1 13.1 copy-start.84
  483.1 13.4 copy-start.47
  483.1 13.4 copy-start.50
  485.4 8.6 copy-start.10
  488.2 5.9 copy-start.132
  490.6 3.4 copy-start.154
  490.6 3.5 copy-start.26
  498.9 12.5 copy-start.145
  500.7 13.2 copy-start.21
  500.7 10.7 copy-start.79
  500.7 10.7 collective-permute-start.1
  506.7 7.2 copy-start.107
  506.8 7.1 copy-start.71
  507.1 6.8 copy-start.103
  514.5 35.3 %copy-start.120 = (f32[128]{0:T(128)}, f32[128]{0:T(128)S(1)}, u32[]{:S(2)}) copy-start(f32[128]{0:T(128)S(1)} %get-tuple-element.149) | copy-start | bytes 1540
  516.1 30.6 %copy-start.41 = (bf16[128,320]{0,1:T(8,128)(2,1)}, bf16[128,320]{0,1:T(8,128)(2,1)S(1)}, u32[]{:S(2)}) copy-start(bf16[128,320]{0,1:T(8,128)(2,1)S(1)} %slice.397) | copy-start | bytes 245764
  528.6 24.0 %copy-start.6 = (bf16[128,2560]{1,0:T(8,128)(2,1)}, bf16[128,2560]{1,0:T(8,128)(2,1)S(1)}, u32[]{:S(2)}) copy-start(bf16[128,2560]{1,0:T(8,128)(2,1)S(1)} %get-tuple-element.52) | copy-start | bytes 1966084
  529.7 10.1 copy-start.18
  529.7 10.0 collective-permute-start.2
  551.1 9.7 copy-start.36
  551.1 10.5 copy-start.17
  551.1 10.5 copy-start.33
  551.1 9.7 collective-permute-start.3
  560.8 6.0 copy-start.19
  589.0 1157.7 %all-reduce.14.cloned.1.call-start = ((), (), s32[]{:S(2)}) async-start(), calls=%async_computation.6 | async-start | bytes 20643840
  591.3 5.5 copy-start.9
  591.3 5.5 copy-start.45
  596.8 7.7 copy-start.160
  596.8 7.7 copy-start.161
  596.8 7.7 copy-start.141
  596.8 7.7 copy-start.20
  613.2 10.7 copy-start.29
  613.2 10.7 copy-start.31
  613.2 10.7 copy-start.147
  613.3 10.7 copy-start.148
  613.3 10.7 copy-start.149
  631.2 1723.2 %all-reduce.10.cloned.1.call-start = ((), (), s32[]{:S(2)}) async-start(), calls=%async_computation.4 | async-start | bytes 39321600
  673.9 5.2 copy-start.126
  673.9 5.1 copy-start.127
  673.9 5.1 copy-start.128
  673.9 5.1 copy-start.129
  674.0 5.1 copy-start.130
  674.0 146.4 %copy-start.38 = (bf16[1,128,960]{1,2,0:T(8,128)(2,1)S(1)}, bf16[1,128,960]{1,2,0:T(8,128)(2,1)}, u32[]{:S(2)}) copy-start(bf16[1,128,960]{1,2,0:T(8,128)(2,1)} %get-tuple-element.57) | copy-start | bytes 737284
  (114 other events, 175.1 us)
Sparse Core Ops, SparseCore 0:
  10.3 108.3 all-gather.6
  121.0 107.8 all-gather.4
  231.1 125.5 all-gather.8
  358.3 106.9 all-gather.10
  589.1 575.3 all-reduce.11
  1167.0 579.6 all-reduce.13
  1749.2 605.1 all-reduce.9
where the time goes:
time: 2370 us; the launch traced here: 2360 us
  waiting for transfers between devices  1890 us (80%)
  blocking collectives  226 us (10%)
  local copies, waits for them, and re-layouts  107 us (5%)
  matrix products  92.9 us (4%)
    unnamed x10, waiting for transfers between devices  1530 us
    unnamed x1, blocking collectives  141 us
    all_gather x1, waiting for transfers between devices, per_device(): lax.all_gather(gate_up_weight, 'dp', axis=1, tiled=True)  120 us
    all_gather x1, waiting for transfers between devices, per_device(): lax.all_gather(qkv_weight, 'dp', axis=1, tiled=True)  107 us
    all_gather x1, waiting for transfers between devices, per_device(): lax.all_gather(down_weight, 'dp', axis=1, tiled=True)  90.7 us
    all_gather x1, blocking collectives, per_device(): lax.all_gather(norm_gains, 'dp', axis=1, tiled=True)  85.3 us
  transfers between devices with their start and end apart: 11, of which 11 were waited for; matrix products, arithmetic and copies ran while one was open for 5% of the time, Pallas kernels for 0%

commit v1 on v0

v1 whole, which is shorter than its diff:
```python
import jax
import jax.numpy as jnp
from jax import lax
from jax.experimental import pallas as pl
from jax.experimental.pallas import tpu as pltpu
from jax.sharding import PartitionSpec as P

D = 960
H = 15
KV = 5
HD = 64
FF = 2560
QKV = D + 2 * KV * HD
N_DP = 64
ROWS = D // N_DP
PAD = 16
FROWS = FF // N_DP
LANES = 128
QKV_PAD = 1664
OUT_PAD = 1024

BF16 = jnp.bfloat16
F32 = jnp.float32


def place(y, x, z, core):
    return ((y % 4 * 2 + x % 2) * 4 + z % 4) * 2 + core % 2


def route(kind, step):
    pairs = []
    for source in range(N_DP):
        y, x, z, core = source // 16, source // 8 % 2, source // 2 % 4, source % 2
        if kind == "core":
            target = place(y, x, z, core + 1)
        elif kind == "x":
            target = place(y, x + 1, z, core)
        elif (kind == "wide") == (core == 0):
            target = place(y, x, z + step, core)
        else:
            target = place(y + step, x, z, core)
        pairs.append((source, target))
    return pairs


def send(block, kind, step=1):
    return lax.ppermute(block, "dp", route(kind, step))


def total(*terms):
    result = terms[0].astype(F32)
    for term in terms[1:]:
        result = result + term.astype(F32)
    return result


def ring_scatter(blocks, kind):
    half = blocks.shape[1] // 2
    from_left = send(blocks[2, :half], kind, 1)
    from_right = send(blocks[2, half:], kind, -1)
    onward = jnp.concatenate([total(blocks[1, :half], from_left).astype(BF16), blocks[1, half:]], 0)
    back = jnp.concatenate([blocks[3, :half], total(blocks[3, half:], from_right).astype(BF16)], 0)
    from_left = send(onward, kind, 1)
    from_right = send(back, kind, -1)
    return total(blocks[0], from_left, from_right).astype(BF16)


def scatter_sum(for_other, for_own):
    blocks = total(for_own, send(for_other, "core")).astype(BF16)
    blocks = ring_scatter(blocks.reshape((4, 8) + blocks.shape[1:]), "wide")
    blocks = ring_scatter(blocks.reshape((4, 2) + blocks.shape[1:]), "narrow")
    return total(blocks[0], send(blocks[1], "x"))


def ring_gather(block, kind):
    half = block.shape[0] // 2
    from_left = send(block, kind, 1)
    from_right = send(block, kind, -1)
    far_left = send(from_left[:half], kind, 1)
    far_right = send(from_right[half:], kind, -1)
    return [block, from_right, far_left, far_right, from_left]


def gather_rows(shard):
    block = jnp.stack([shard, send(shard, "x")], 0)
    block = jnp.concatenate(ring_gather(block, "narrow"), 0)
    pieces = ring_gather(block, "wide")
    others = [send(piece, "core") for piece in pieces]
    return jnp.concatenate(pieces + others, 0)


def block_order():
    index = lax.axis_index("dp")
    y, x, z, core = index // 16, index // 8 % 2, index // 2 % 4, index % 2
    position = jnp.arange(N_DP)
    core_step, wide, narrow, x_step = position // 32, position // 8 % 4, position // 2 % 4, position % 2
    core_there = (core + core_step) % 2
    z_step = jnp.where(core_there == 0, wide, narrow)
    y_step = jnp.where(core_there == 0, narrow, wide)
    return (((y + y_step) % 4 * 2 + (x + x_step) % 2) * 4 + (z + z_step) % 4) * 2 + core_there


def placement(order):
    column = jnp.arange(N_DP * PAD)
    inner = column % PAD
    row = jnp.where(inner < ROWS, jnp.repeat(order, PAD) * ROWS + inner, -1)
    return (jnp.arange(D)[:, None] == row[None, :]).astype(BF16)


def reorder_kernel(scatter, order_ref, blocks_ref, out_ref):
    def one(step, carry):
        there = order_ref[step]
        if scatter:
            out_ref[there] = blocks_ref[step]
        else:
            out_ref[step] = blocks_ref[there]
        return carry

    lax.fori_loop(0, N_DP, one, 0)


def reorder(blocks, order, scatter):
    return pl.pallas_call(
        lambda *refs: reorder_kernel(scatter, *refs),
        out_shape=jax.ShapeDtypeStruct(blocks.shape, blocks.dtype),
        in_specs=[
            pl.BlockSpec(memory_space=pltpu.SMEM),
            pl.BlockSpec(memory_space=pltpu.VMEM),
        ],
        out_specs=pl.BlockSpec(memory_space=pltpu.VMEM),
        compiler_params=pltpu.CompilerParams(vmem_limit_bytes=32 * 1024 * 1024),
    )(order, blocks)


def dot(left, right):
    return jnp.dot(left, right, preferred_element_type=F32)


def dot_t(left, right):
    return lax.dot_general(left, right, (((1,), (1,)), ((), ())), preferred_element_type=F32)


EPSILON = 1e-05
ROPE_BASE = 100000.0


def shifted(block, axis, distance):
    devices = range(lax.axis_size(axis))
    pairs = [(i - distance, i) for i in devices if i - distance in devices]
    return lax.ppermute(block, axis, pairs)


def rope_tables(length):
    position = jnp.arange(length, dtype=jnp.float32)[:, None]
    frequency = ROPE_BASE ** (-jnp.arange(0, HD, 2, dtype=jnp.float32) / HD)
    angle = position * frequency[None, :]
    return (jnp.cos(angle), jnp.sin(angle))


def rotate(vector, cosine_table, sine_table):
    halfway = vector.shape[-1] // 2
    first_half = vector[..., :halfway]
    second_half = vector[..., halfway:]
    cosine = cosine_table[:, None, :]
    sine_part = sine_table[:, None, :]
    return jnp.concatenate(
        [
            first_half * cosine - second_half * sine_part,
            second_half * cosine + first_half * sine_part,
        ],
        -1,
    )


def unrotate(vector, cosine_table, sine_table):
    halfway = vector.shape[-1] // 2
    first_half = vector[..., :halfway]
    second_half = vector[..., halfway:]
    cosine = cosine_table[:, None, :]
    sine_part = sine_table[:, None, :]
    return jnp.concatenate(
        [
            first_half * cosine + second_half * sine_part,
            second_half * cosine - first_half * sine_part,
        ],
        -1,
    )


def normalize(vector, gain):
    return vector * lax.rsqrt(jnp.mean(vector * vector, axis=-1, keepdims=True) + EPSILON) * gain


def swiglu(gate_part, up_part):
    return jax.nn.silu(gate_part) * up_part


def attention_scores(queries, keys_rot, allowed):
    scores = jnp.einsum(
        "qkgd,tkd->kgqt", queries, keys_rot, preferred_element_type=jnp.float32
    ) * HD ** (-0.5)
    return jnp.where(allowed, scores, -1000000000.0)


def layer_forward(layer_in, seg_row, weights):
    attn_mat, gate_up_mat, down_mat, gains_full, spread = weights
    length = layer_in.shape[0]
    cosine_table, sine_table = rope_tables(length)
    stream = layer_in.astype(F32)
    hidden_one = normalize(stream, gains_full[0]).astype(BF16)
    hidden_one = dot(hidden_one, spread).astype(BF16)
    projected = dot(hidden_one, attn_mat[:, :QKV_PAD])[:, :QKV]
    queries = rotate(projected[:, :D].reshape(length, H, HD), cosine_table, sine_table)
    queries = queries.astype(BF16).reshape(length, KV, H // KV, HD)
    keys_rot = rotate(
        projected[:, D : D + KV * HD].reshape(length, KV, HD), cosine_table, sine_table
    ).astype(BF16)
    values = projected[:, D + KV * HD :].reshape(length, KV, HD).astype(BF16)
    positions = jnp.arange(length)
    allowed = (seg_row[:, None] == seg_row[None, :]) & (positions[:, None] >= positions[None, :])
    scores = attention_scores(queries, keys_rot, allowed)
    row_max = jnp.max(scores, axis=-1, keepdims=True)
    exp_scores = jnp.exp(scores - row_max)
    row_total = jnp.sum(exp_scores, axis=-1, keepdims=True)
    attn_probs = exp_scores / row_total
    log_total = row_max + jnp.log(row_total)
    attended = jnp.einsum(
        "kgqt,tkd->qkgd",
        attn_probs.astype(BF16),
        values,
        preferred_element_type=F32,
    )
    attended = dot(attended.reshape(length, D).astype(BF16), spread).astype(BF16)
    middle = stream + dot(attended, attn_mat[:, QKV_PAD : QKV_PAD + D])
    hidden_two = normalize(middle, gains_full[1]).astype(BF16)
    hidden_two = dot(hidden_two, spread).astype(BF16)
    gate_up = dot(hidden_two, gate_up_mat)
    activated = swiglu(gate_up[:, :FF], gate_up[:, FF:]).astype(BF16)
    layer_out = middle + dot(activated, down_mat)
    kept = (
        stream,
        hidden_one,
        queries,
        keys_rot,
        values,
        allowed,
        log_total,
        attended,
        middle,
        hidden_two,
        gate_up,
        activated,
    )
    return (kept, layer_out)


def layer_backward(kept, grad_out, weights):
    attn_mat, gate_up_mat, down_mat, gains_full, spread = weights
    (
        stream,
        hidden_one,
        queries,
        keys_rot,
        values,
        allowed,
        log_total,
        attended,
        middle,
        hidden_two,
        gate_up,
        activated,
    ) = kept
    length = stream.shape[0]
    cosine_table, sine_table = rope_tables(length)
    grad_down = grad_out.astype(BF16)
    grad_act = dot_t(grad_down, down_mat)
    unused, swiglu_back = jax.vjp(swiglu, gate_up[:, :FF], gate_up[:, FF:])
    grad_gate, grad_upper = swiglu_back(grad_act)
    grad_gate_up = jnp.concatenate([grad_gate, grad_upper], -1).astype(BF16)
    grad_two = dot_t(dot_t(grad_gate_up, gate_up_mat).astype(BF16), spread)
    unused, norm_back_two = jax.vjp(normalize, middle, gains_full[1])
    grad_norm_two, gain_two = norm_back_two(grad_two)
    grad_middle = grad_out + grad_norm_two
    grad_attn = grad_middle.astype(BF16)
    grad_mixed = dot_t(grad_attn, attn_mat[:, QKV_PAD : QKV_PAD + D]).astype(BF16)
    grad_mixed = dot_t(grad_mixed, spread).astype(BF16)
    grad_mixed = grad_mixed.reshape(length, KV, H // KV, HD)
    scores = attention_scores(queries, keys_rot, allowed)
    attn_probs = jnp.exp(scores - log_total)
    grad_probs = jnp.einsum(
        "qkgd,tkd->kgqt", grad_mixed, values, preferred_element_type=F32
    )
    grad_scores = attn_probs * (
        grad_probs - jnp.sum(grad_probs * attn_probs, axis=-1, keepdims=True)
    )
    grad_scores = grad_scores.astype(BF16)
    grad_queries = jnp.einsum(
        "kgqt,tkd->qkgd", grad_scores, keys_rot, preferred_element_type=F32
    ) * HD ** (-0.5)
    grad_keys = jnp.einsum(
        "kgqt,qkgd->tkd", grad_scores, queries, preferred_element_type=F32
    ) * HD ** (-0.5)
    grad_values = jnp.einsum(
        "kgqt,qkgd->tkd",
        attn_probs.astype(BF16),
        grad_mixed,
        preferred_element_type=F32,
    )
    grad_queries = grad_queries.astype(BF16).reshape(length, H, HD).astype(F32)
    grad_keys = grad_keys.astype(BF16).astype(F32)
    grad_q_pre = unrotate(grad_queries, cosine_table, sine_table).astype(BF16).reshape(length, D)
    grad_k_pre = (
        unrotate(grad_keys, cosine_table, sine_table).astype(BF16).reshape(length, KV * HD)
    )
    grad_v_pre = grad_values.astype(BF16).reshape(length, KV * HD)
    grad_proj = jnp.concatenate([grad_q_pre, grad_k_pre, grad_v_pre], -1)
    grad_one = dot_t(dot_t(grad_proj, attn_mat[:, :QKV]).astype(BF16), spread)
    unused, norm_back_one = jax.vjp(normalize, stream, gains_full[0])
    grad_norm_one, gain_one = norm_back_one(grad_one)
    grad_in = grad_middle + grad_norm_one
    pieces = (
        grad_proj,
        grad_attn,
        grad_gate_up,
        grad_down,
        jnp.stack([gain_one, gain_two], 0),
    )
    return (grad_in, pieces)


def contract(left_rows, right_rows):
    return lax.dot_general(
        left_rows, right_rows, (((0,), (0,)), ((), ())), preferred_element_type=F32
    ).astype(BF16)


def halves(left_rows, right_rows):
    own = contract(left_rows[:, : N_DP * PAD // 2], right_rows)
    other = contract(left_rows[:, N_DP * PAD // 2 :], right_rows)
    return (other, own)


def as_blocks(rows):
    return rows.reshape(N_DP // 2, -1, rows.shape[-1])


def per_device(
    inputs, segment_ids, qkv_weight, out_weight, gate_up_weight, down_weight, norm_gains, cotangent
):
    batches = inputs.shape[0]
    is_first = lax.axis_index("section") == 0
    order = block_order()
    spread = placement(order)
    attn_shard = jnp.concatenate(
        [
            qkv_weight[0],
            norm_gains[0],
            jnp.zeros((ROWS, QKV_PAD - QKV - 2), BF16),
            out_weight[0],
            jnp.zeros((ROWS, OUT_PAD - D), BF16),
        ],
        1,
    )
    attn_mat = gather_rows(jnp.pad(attn_shard, ((0, 1), (0, 0)))).reshape(N_DP * PAD, -1)
    gate_up_mat = gather_rows(jnp.pad(gate_up_weight[0], ((0, 1), (0, 0)))).reshape(N_DP * PAD, -1)
    down_mat = reorder(gather_rows(down_weight[0]), order, True).reshape(FF, D)
    gains_full = lax.dot_general(
        attn_mat[:, QKV : QKV + 2], spread, (((0,), (1,)), ((), ())), preferred_element_type=F32
    )
    weights = (attn_mat, gate_up_mat, down_mat, gains_full, spread)
    received = jnp.zeros(inputs.shape[1:], BF16)
    saved = []
    produced = []
    for turn in range(batches + 1):
        own_input = inputs[min(turn, batches - 1)]
        layer_in = jnp.where(is_first, own_input, received)
        seg_row = jnp.where(
            is_first, segment_ids[min(turn, batches - 1)], segment_ids[max(turn - 1, 0)]
        )
        kept, layer_out = layer_forward(layer_in, seg_row, weights)
        layer_out = layer_out.astype(BF16)
        saved.append(kept)
        produced.append(layer_out)
        if turn < batches:
            received = shifted(layer_out, "section", 1)
    section_outputs = jnp.stack(
        [
            jnp.where(is_first, produced[position], produced[position + 1])
            for position in range(batches)
        ]
    )[None]
    received = jnp.zeros(inputs.shape[1:], BF16)
    returned = []
    collected = []
    for turn in range(batches + 1):
        if turn < batches:
            own_grad = cotangent[turn]
        else:
            own_grad = jnp.zeros(inputs.shape[1:], BF16)
        grad_out = jnp.where(is_first, received, own_grad).astype(F32)
        kept = jax.tree.map(
            lambda for_first, for_second: jnp.where(is_first, for_first, for_second),
            saved[max(turn - 1, 0)],
            saved[min(turn + 1, batches)],
        )
        grad_in, pieces = layer_backward(kept, grad_out, weights)
        grad_in = grad_in.astype(BF16)
        returned.append(grad_in)
        collected.append(pieces)
        if turn < batches:
            received = shifted(grad_in, "section", -1)
    section_input_grads = jnp.stack(
        [
            jnp.where(is_first, returned[position + 1], returned[position])
            for position in range(batches)
        ]
    )[None]

    def lefts(member):
        return jnp.concatenate(
            [jnp.where(is_first, saved[b][member], saved[b + 1][member]) for b in range(batches)], 0
        )

    def rights(member):
        return jnp.concatenate(
            [
                jnp.where(is_first, collected[b + 1][member], collected[b][member])
                for b in range(batches)
            ],
            0,
        )

    down_blocks = contract(lefts(11), rights(3)).reshape(N_DP, FROWS, D)
    down_blocks = reorder(down_blocks, order, False)
    down_grad = scatter_sum(down_blocks[N_DP // 2 :], down_blocks[: N_DP // 2])
    other, own = halves(lefts(9), rights(2))
    gate_up_grad = scatter_sum(as_blocks(other), as_blocks(own))
    gain_sum = collected[0][4]
    for pieces in collected[1:]:
        gain_sum = gain_sum + pieces[4]
    gain_high = gain_sum.astype(BF16)
    gain_low = (gain_sum - gain_high.astype(F32)).astype(BF16)
    gain_rows = lax.dot_general(
        spread, jnp.stack([gain_high, gain_low]), (((0,), (2,)), ((), ())), preferred_element_type=F32
    )
    gain_rows = (gain_rows[:, 0] + gain_rows[:, 1]).astype(BF16)
    qkv_terms = halves(lefts(1), rights(0))
    out_terms = halves(lefts(7), rights(1))
    attn_terms = []
    middle_row = N_DP * PAD // 2
    for term, start in ((0, middle_row), (1, 0)):
        attn_terms.append(
            jnp.concatenate(
                [
                    qkv_terms[term],
                    gain_rows[start : start + middle_row],
                    jnp.zeros((middle_row, QKV_PAD - QKV - 2), BF16),
                    out_terms[term],
                    jnp.zeros((middle_row, OUT_PAD - D), BF16),
                ],
                1,
            )
        )
    attn_grad = scatter_sum(as_blocks(attn_terms[0]), as_blocks(attn_terms[1]))
    return (
        section_outputs,
        section_input_grads,
        attn_grad[None, :ROWS, :QKV],
        attn_grad[None, :ROWS, QKV_PAD : QKV_PAD + D],
        gate_up_grad[None, :ROWS],
        down_grad[None],
        attn_grad[None, :ROWS, QKV : QKV + 2],
    )


def solution(mesh):
    in_specs = (
        P(None, "dp", None),
        P(None, "dp"),
        P("section", "dp", None),
        P("section", "dp", None),
        P("section", "dp", None),
        P("section", "dp", None),
        P("section", "dp", None),
        P(None, "dp", None),
    )
    out_specs = (
        P("section", None, "dp", None),
        P("section", None, "dp", None),
        P("section", "dp", None),
        P("section", "dp", None),
        P("section", "dp", None),
        P("section", "dp", None),
        P("section", "dp", None),
    )
    return jax.shard_map(
        per_device, mesh=mesh, in_specs=in_specs, out_specs=out_specs, check_vma=False
    )
```

time: 2370 us -> 543 us (0.23)
  waiting for transfers between devices: 1890 us -> 121 us
  blocking collectives: 226 us -> 0 us
  starting transfers between devices: 14.6 us -> 96.2 us
  matrix products: 92.9 us -> 157 us
  other arithmetic: 14.1 us -> 54.7 us
    unnamed x10 -> x0, waiting for transfers between devices: 1530 us -> none
    all_gather x4 -> x0, waiting for transfers between devices: 336 us -> none  [the longest x1 120 us: per_device(): lax.all_gather(gate_up_weight, 'dp', axis=1, tiled=True)]
    unnamed x1 -> x0, blocking collectives: 141 us -> none
    ppermute x4 -> x76, waiting for transfers between devices: 25.5 us -> 121 us  [the longest x72 103 us: send(): return lax.ppermute(block, 'dp', route(kind, step))]
    all_gather x1 -> x0, blocking collectives: 85.3 us -> none  [per_device(): lax.all_gather(norm_gains, 'dp', axis=1, tiled=True)]
    ppermute x4 -> x76, starting transfers between devices: 14.1 us -> 96.2 us  [the longest x72 81.8 us: send(): return lax.ppermute(block, 'dp', route(kind, step))]
    dot_general x33 -> x44, matrix products: 66.2 us -> 132 us  [the longest x12 65.8 us: dot_t(): lax.dot_general(left, right, (((1,), (1,)), ((), ())), preferred_element_...]
    broadcast_in_dim x4 -> x6, local copies, waits for them, and re-layouts: 63.6 us -> 1.02 us  [the longest x1 0.93 us: per_device(): gate_up_grad[None, :ROWS]]
  transfers between devices with their start and end apart: 11 -> 76, of which waited for: 11 -> 30; matrix products, arithmetic and copies ran while one was open for 5% -> 22% of each run, Pallas kernels for 0% -> 0%
where the time goes in v1:
time: 543 us; the launch traced here: 533 us
  matrix products  157 us (29%)
  waiting for transfers between devices  121 us (22%)
  local copies, waits for them, and re-layouts  96.9 us (18%)
  starting transfers between devices  96.2 us (18%)
  other arithmetic  54.7 us (10%)
    ppermute x72, waiting for transfers between devices, send(): return lax.ppermute(block, 'dp', route(kind, step))  103 us
    ppermute x72, starting transfers between devices, send(): return lax.ppermute(block, 'dp', route(kind, step))  81.8 us
    dot_general x12, matrix products, dot_t(): lax.dot_general(left, right, (((1,), (1,)), ((), ())), preferred_element_...  65.8 us
    dot_general x21, matrix products, dot(): return jnp.dot(left, right, preferred_element_type=F32)  56.6 us
    unnamed x385, local copies, waits for them, and re-layouts  27.9 us
    concatenate x3, local copies, waits for them, and re-layouts, per_device(): jnp.concatenate([qkv_terms[term], gain_rows[start:start + middle_row], jn...  26.9 us
    ppermute x4, waiting for transfers between devices, shifted(): return lax.ppermute(block, axis, pairs)  18.4 us
    dot_general x7, matrix products, contract(): lax.dot_general(left_rows, right_rows, (((0,), (0,)), ((), ())), preferre...  16.9 us
  transfers between devices with their start and end apart: 76, of which 30 were waited for; matrix products, arithmetic and copies ran while one was open for 22% of the time, Pallas kernels for 0%

profile of v1, /device:TPU:0, one launch (start us, length us, event | category | flops | bytes accessed | tf_op | source)
XLA Modules:
  0.0 532.6 jit_solution(7069201185028958316)
XLA Ops:
  14.9 3.1 collective-permute-start.29
  18.0 3.3 collective-permute-start.1
  22.0 3.3 collective-permute-start.15
  30.8 4.5 collective-permute-done.31
  35.3 4.1 collective-permute-start.33
  42.0 3.4 collective-permute-start.5
  47.7 4.4 collective-permute-done.17
  53.4 3.9 collective-permute-done.18
  60.4 9.1 %collective-permute-done.6 = bf16[8,16,2688]{2,1,0:T(8,128)(2,1)S(1)} collective-permute-done((bf16[8,16,2688]{2,1,0:T(8,128)(2,1)S(1)}, bf16[8,16,2688]{2,1,0:T(8,128)(2,1)S(1)}, u32[]{:S(2)}, u32[]{:S(2)}) %collective-permute-start.6) | collective-permute-done | bytes 688160 | tf_op jit(solution)/shard_map/ppermute | solution.py:47
  69.8 3.2 collective-permute-done.35
  73.1 3.5 collective-permute-done.36
  76.7 3.3 collective-permute-start.8
  80.0 5.0 collective-permute-done.7
  86.5 3.3 collective-permute-start.19
  114.8 3.3 collective-permute-start.22
  119.8 5.7 %collective-permute-done.21 = bf16[4,16,5120]{2,1,0:T(8,128)(2,1)S(1)} collective-permute-done((bf16[4,16,5120]{2,1,0:T(8,128)(2,1)S(1)}, bf16[4,16,5120]{2,1,0:T(8,128)(2,1)S(1)}, u32[]{:S(2)}, u32[]{:S(2)}) %collective-permute-start.21) | collective-permute-done | bytes 655392 | tf_op jit(solution)/shard_map/ppermute | solution.py:47
  135.6 6.3 %fusion.316 = f32[128,5120]{1,0:T(8,128)S(1)} fusion(bf16[128,1024]{1,0:T(8,128)(2,1)S(1)} %fusion.101, bf16[1024,5120]{1,0:T(8,128)(2,1)} %bitcast.522), kind=kOutput, calls=%fused_computation.702 | convolution fusion | flops 1342177280 | bytes 13369344 | tf_op jit(solution)/shard_map/dot_general | solution.py:136
  143.9 4.8 collective-permute-start.42
  148.8 5.2 collective-permute-done.42
  171.1 3.3 multiply_reduce_fusion.20
  176.3 7.7 %broadcast_select_fusion.4 = (f32[128,5120]{1,0:T(8,128)S(1)}, f32[128,5120]{1,0:T(8,128)}) fusion(f32[128,5120]{1,0:T(8,128)S(1)} %fusion.316, pred[]{:T(512)S(6)} %eq.77, bf16[128,1024]{1,0:T(8,128)(2,1)S(1)} %fusion.104, bf16[1024,5120]{1,0:T(8,128)(2,1)} %bitcast.523), kind=kOutput, calls=%fused_computation.139 | convolution fusion | flops 1342832640 | bytes 18612224 | tf_op jit(solution)/shard_map/dot_general | solution.py:136
  184.5 3.3 fusion.75
  187.8 10.2 %multiply_reduce_fusion.7 = (f32[960]{0:T(1024)}, f32[128]{0:T(128)}, f32[128,960]{0,1:T(8,128)}) fusion(f32[128,960]{0,1:T(8,128)} %get-tuple-element.51, f32[128]{0:T(128)} %fusion.275, f32[960]{0:T(1024)S(1)} %bitcast.649, s32[1024]{0:T(1024)S(1)} %copy-done.133, bf16[1024,5120]{1,0:T(8,128)(2,1)} %bitcast.524, ...), kind=kOutput, calls=%fused_computation.297 | convolution fusion | flops 1598307200 | bytes 12792320 | tf_op jit(solution)/shard_map/dot_general | solution.py:140
  201.3 3.9 fusion.111
  215.0 6.6 %collective-permute-start.43 = (bf16[128,960]{0,1:T(8,128)(2,1)}, bf16[128,960]{0,1:T(8,128)(2,1)}, u32[]{:S(2)}, u32[]{:S(2)}) collective-permute-start(bf16[128,960]{0,1:T(8,128)(2,1)} %fusion.109), channel_id=1, source_target_pairs={{0,64},{1,65},{2,66},{3,67},{4,68},{5,69},{6,70},{7,71},{8,72},{9,... | collective-permute-start | bytes 737288 | tf_op jit(solution)/shard_map/ppermute | solution.py:150
  223.0 4.7 fusion.8
  252.4 3.6 multiply_reduce_fusion.12
  257.8 7.6 %broadcast_select_fusion.2 = (f32[128,5120]{1,0:T(8,128)}, f32[128,5120]{1,0:T(8,128)S(1)}, f32[128,5120]{1,0:T(8,128)S(1)}) fusion(f32[128,5120]{1,0:T(8,128)S(1)} %copy-done.4, pred[]{:T(512)S(6)} %eq.77, f32[128,5120]{1,0:T(8,128)S(1)} %fusion.316, bf16[128,1024]{1,0:T(8,128)(2,1)S(1)} %get-tuple-element.223, bf16[1024,5120]{1,0:T(8,128)(2,1)} %bitcast.525), kind=kOutput, calls=%fused_computation.137 | convolution fusion | flops 1343488000 | bytes 23855104 | tf_op jit(solution)/shard_map/dot_general | solution.py:136
  270.9 6.6 %collective-permute-done.44 = bf16[128,960]{0,1:T(8,128)(2,1)S(1)} collective-permute-done((bf16[128,960]{0,1:T(8,128)(2,1)S(1)}, bf16[128,960]{0,1:T(8,128)(2,1)S(1)}, u32[]{:S(2)}, u32[]{:S(2)}) %collective-permute-start.44) | collective-permute-done | bytes 245792 | tf_op jit(solution)/shard_map/ppermute | solution.py:150
  278.3 3.3 fusion.78
  281.6 10.1 %multiply_reduce_fusion.5 = (f32[960]{0:T(1024)}, f32[128]{0:T(128)S(1)}, f32[128,960]{0,1:T(8,128)}) fusion(f32[128,960]{0,1:T(8,128)S(1)} %copy-done.23, f32[128]{0:T(128)S(1)} %fusion.277, f32[960]{0:T(1024)S(1)} %bitcast.652, s32[1024]{0:T(1024)S(1)} %copy-done.135, bf16[1024,5120]{1,0:T(8,128)(2,1)} %bitcast.526, ...), kind=kOutput, calls=%fused_computation.295 | convolution fusion | flops 1598307200 | bytes 12792320 | tf_op jit(solution)/shard_map/dot_general | solution.py:140
  293.7 3.0 fusion.112
  300.1 4.1 multiply_reduce_fusion.6
  308.2 6.6 %collective-permute-done.45 = bf16[128,960]{0,1:T(8,128)(2,1)S(1)} collective-permute-done((bf16[128,960]{0,1:T(8,128)(2,1)S(1)}, bf16[128,960]{0,1:T(8,128)(2,1)S(1)}, u32[]{:S(2)}, u32[]{:S(2)}) %collective-permute-start.45) | collective-permute-done | bytes 245792 | tf_op jit(solution)/shard_map/ppermute | solution.py:150
  314.8 5.8 %fusion.81 = (bf16[128,2560]{1,0:T(8,128)(2,1)}, bf16[128,2560]{1,0:T(8,128)(2,1)}) fusion(f32[128,5120]{1,0:T(8,128)S(1)} %copy-done.20, bf16[2560,960]{1,0:T(8,128)(2,1)} %bitcast.505, bf16[128,960]{0,1:T(8,128)(2,1)S(1)} %collective-permute-done.45, pred[]{:T(512)S(6)} %eq.77), kind=kOutput, calls=%fused_computation.106 | convolution fusion | flops 633856000 | bytes 9093121 | tf_op jit(solution)/shard_map/dot_general | solution.py:140
  320.7 9.5 %multiply_reduce_fusion.3 = (f32[960]{0:T(1024)S(1)}, f32[128]{0:T(128)S(1)}, f32[128,960]{0,1:T(8,128)}) fusion(f32[128,960]{0,1:T(8,128)S(1)} %copy-done.27, f32[128]{0:T(128)S(1)} %copy-done.147, f32[960]{0:T(1024)S(1)} %bitcast.654, s32[1024]{0:T(1024)S(1)} %copy-done.136, bf16[1024,5120]{1,0:T(8,128)(2,1)} %bitcast.527, ...), kind=kOutput, calls=%fused_computation.293 | convolution fusion | flops 1598307200 | bytes 12792320 | tf_op jit(solution)/shard_map/dot_general | solution.py:140
  332.3 3.0 fusion.113
  338.2 5.0 multiply_reduce_fusion.4
  344.0 5.0 convolution_convert_fusion.2
  349.0 7.8 %copy.85 = bf16[2560,960]{1,0:T(8,128)(2,1)} copy(bf16[2560,960]{0,1:T(8,128)(2,1)} %convolution_convert_fusion.2) | data formatting | bytes 9830400 | tf_op jit(solution)/shard_map/convert_element_type | solution.py:334
  366.9 11.9 %concatenate.246 = bf16[512,2688]{0,1:T(8,128)(2,1)S(1)} concatenate(bf16[512,1600]{0,1:T(8,128)(2,1)} %convolution_convert_fusion.3, bf16[512,2]{0,1:T(2,128)(2,1)S(1)} %get-tuple-element.184, bf16[512,62]{0,1:T(8,128)(2,1)} %broadcast.433, bf16[512,960]{0,1:T(8,128)(2,1)} %convolution_convert_fusion.5, bf16[512,64]{0,1:T(8,128)(2,1)} %broadcast.434), dimensions={1} | concatenate | bytes 5505024 | tf_op jit(solution)/shard_map/concatenate | solution.py:453
  382.3 4.7 fusion.124
  391.0 11.9 %concatenate.245 = bf16[512,2688]{0,1:T(8,128)(2,1)S(1)} concatenate(bf16[512,1600]{0,1:T(8,128)(2,1)} %convolution_convert_fusion.4, bf16[512,2]{0,1:T(2,128)(2,1)S(1)} %get-tuple-element.185, bf16[512,62]{0,1:T(8,128)(2,1)} %broadcast.433, bf16[512,960]{0,1:T(8,128)(2,1)} %convolution_convert_fusion.6, bf16[512,64]{0,1:T(8,128)(2,1)} %broadcast.434), dimensions={1} | concatenate | bytes 5505024 | tf_op jit(solution)/shard_map/concatenate | solution.py:453
  402.9 3.5 copy.83
  409.4 3.9 convolution_convert_fusion
  423.9 3.3 collective-permute-start.49
  432.5 3.5 collective-permute-start.50
  435.9 3.0 collective-permute-done.70
  442.2 3.2 collective-permute-start.73
  445.5 3.1 collective-permute-done.71
  454.1 3.7 collective-permute-done.72
  459.8 3.2 collective-permute-start.53
  465.6 4.4 fusion
  470.4 3.2 collective-permute-start.59
  473.6 3.3 collective-permute-start.54
  477.0 7.0 %collective-permute-done.57 = bf16[4,16,5120]{2,1,0:T(8,128)(2,1)S(1)} collective-permute-done((bf16[4,16,5120]{2,1,0:T(8,128)(2,1)S(1)}, bf16[4,16,5120]{2,1,0:T(8,128)(2,1)S(1)}, u32[]{:S(2)}, u32[]{:S(2)}) %collective-permute-start.57) | collective-permute-done | bytes 655392 | tf_op jit(solution)/shard_map/ppermute | solution.py:47
  487.7 14.4 %collective-permute-done.60 = bf16[8,16,5120]{2,1,0:T(8,128)(2,1)S(1)} collective-permute-done((bf16[8,16,5120]{2,1,0:T(8,128)(2,1)S(1)}, bf16[8,16,5120]{2,1,0:T(8,128)(2,1)S(1)}, u32[]{:S(2)}, u32[]{:S(2)}) %collective-permute-start.60) | collective-permute-done | bytes 1310752 | tf_op jit(solution)/shard_map/ppermute | solution.py:47
  502.1 3.0 collective-permute-done.58
  505.9 4.8 collective-permute-start.63
  510.9 3.1 collective-permute-done.61
  514.1 3.4 collective-permute-start.64
  518.3 3.7 collective-permute-done.64
  522.1 3.8 collective-permute-done.62
  528.0 3.4 collective-permute-done.65
  (715 shorter events, 208.3 us)
Async XLA Ops:
  2.3 15.7 %collective-permute-start = (bf16[16,2688]{1,0:T(8,128)(2,1)S(1)}, bf16[16,2688]{1,0:T(8,128)(2,1)S(1)}, u32[]{:S(2)}, u32[]{:S(2)}) collective-permute-start(bf16[16,2688]{1,0:T(8,128)(2,1)S(1)} %get-tuple-element.171), channel_id=1, source_target_pairs={{0,8},{1,9},{2,10},{3,11},{4,12},{5,13},{6,14},{7,15},{8,0},{9,1},... | collective-permute-start | bytes 258056 | tf_op jit(solution)/shard_map/ppermute | solution.py:47
  4.0 10.0 %collective-permute-start.28 = (bf16[40,960]{1,0:T(8,128)(2,1)}, bf16[40,960]{1,0:T(8,128)(2,1)S(1)}, u32[]{:S(2)}, u32[]{:S(2)}) collective-permute-start(bf16[40,960]{1,0:T(8,128)(2,1)} %bitcast.606), channel_id=1, source_target_pairs={{0,8},{1,9},{2,10},{3,11},{4,12},{5,13},{6,14},{7,15},{8,0},{9,1},... | collective-permute-start | bytes 230408 | tf_op jit(solution)/shard_map/ppermute | solution.py:47
  5.4 16.6 %collective-permute-start.14 = (bf16[16,5120]{1,0:T(8,128)(2,1)S(1)}, bf16[16,5120]{1,0:T(8,128)(2,1)S(1)}, u32[]{:S(2)}, u32[]{:S(2)}) collective-permute-start(bf16[16,5120]{1,0:T(8,128)(2,1)S(1)} %get-tuple-element.161), channel_id=1, source_target_pairs={{0,8},{1,9},{2,10},{3,11},{4,12},{5,13},{6,14},{7,15},{8,0},{9,1},... | collective-permute-start | bytes 491528 | tf_op jit(solution)/shard_map/ppermute | solution.py:47
  14.9 11.2 %collective-permute-start.29 = (bf16[2,40,960]{2,1,0:T(8,128)(2,1)S(1)}, bf16[2,40,960]{2,1,0:T(8,128)(2,1)S(1)}, u32[]{:S(2)}, u32[]{:S(2)}) collective-permute-start(bf16[2,40,960]{2,1,0:T(8,128)(2,1)S(1)} %pad_maximum_fusion.49), channel_id=1, source_target_pairs={{0,48},{1,7},{2,50},{3,1},{4,52},{5,3},{6,54},{7,5},{8,56},{9,15},... | collective-permute-start | bytes 460808 | tf_op jit(solution)/shard_map/ppermute | solution.py:47
  18.0 8.1 %collective-permute-start.30 = (bf16[2,40,960]{2,1,0:T(8,128)(2,1)S(1)}, bf16[2,40,960]{2,1,0:T(8,128)(2,1)S(1)}, u32[]{:S(2)}, u32[]{:S(2)}) collective-permute-start(bf16[2,40,960]{2,1,0:T(8,128)(2,1)S(1)} %pad_maximum_fusion.49), channel_id=1, source_target_pairs={{0,16},{1,3},{2,18},{3,5},{4,20},{5,7},{6,22},{7,1},{8,24},{9,11},... | collective-permute-start | bytes 460808 | tf_op jit(solution)/shard_map/ppermute | solution.py:47
  18.0 11.5 %collective-permute-start.1 = (bf16[2,16,2688]{2,1,0:T(8,128)(2,1)S(1)}, bf16[2,16,2688]{2,1,0:T(8,128)(2,1)S(1)}, u32[]{:S(2)}, u32[]{:S(2)}) collective-permute-start(bf16[2,16,2688]{2,1,0:T(8,128)(2,1)S(1)} %pad_maximum_fusion.42), channel_id=1, source_target_pairs={{0,48},{1,7},{2,50},{3,1},{4,52},{5,3},{6,54},{7,5},{8,56},{9,15},... | collective-permute-start | bytes 516104 | tf_op jit(solution)/shard_map/ppermute | solution.py:47
  21.3 6.6 %collective-permute-start.2 = (bf16[2,16,2688]{2,1,0:T(8,128)(2,1)S(1)}, bf16[2,16,2688]{2,1,0:T(8,128)(2,1)S(1)}, u32[]{:S(2)}, u32[]{:S(2)}) collective-permute-start(bf16[2,16,2688]{2,1,0:T(8,128)(2,1)S(1)} %pad_maximum_fusion.42), channel_id=1, source_target_pairs={{0,16},{1,3},{2,18},{3,5},{4,20},{5,7},{6,22},{7,1},{8,24},{9,11},... | collective-permute-start | bytes 516104 | tf_op jit(solution)/shard_map/ppermute | solution.py:47
  22.0 23.4 %collective-permute-start.15 = (bf16[2,16,5120]{2,1,0:T(8,128)(2,1)S(1)}, bf16[2,16,5120]{2,1,0:T(8,128)(2,1)S(1)}, u32[]{:S(2)}, u32[]{:S(2)}) collective-permute-start(bf16[2,16,5120]{2,1,0:T(8,128)(2,1)S(1)} %pad_maximum_fusion.25), channel_id=1, source_target_pairs={{0,48},{1,7},{2,50},{3,1},{4,52},{5,3},{6,54},{7,5},{8,56},{9,15},... | collective-permute-start | bytes 983048 | tf_op jit(solution)/shard_map/ppermute | solution.py:47
  26.1 16.0 %collective-permute-start.16 = (bf16[2,16,5120]{2,1,0:T(8,128)(2,1)S(1)}, bf16[2,16,5120]{2,1,0:T(8,128)(2,1)S(1)}, u32[]{:S(2)}, u32[]{:S(2)}) collective-permute-start(bf16[2,16,5120]{2,1,0:T(8,128)(2,1)S(1)} %pad_maximum_fusion.25), channel_id=1, source_target_pairs={{0,16},{1,3},{2,18},{3,5},{4,20},{5,7},{6,22},{7,1},{8,24},{9,11},... | collective-permute-start | bytes 983048 | tf_op jit(solution)/shard_map/ppermute | solution.py:47
  26.1 9.1 %collective-permute-start.31 = (bf16[1,40,960]{2,1,0:T(8,128)(2,1)S(1)}, bf16[1,40,960]{2,1,0:T(8,128)(2,1)S(1)}, u32[]{:S(2)}, u32[]{:S(2)}) collective-permute-start(bf16[1,40,960]{2,1,0:T(8,128)(2,1)S(1)} %slice.607), channel_id=1, source_target_pairs={{0,16},{1,3},{2,18},{3,5},{4,20},{5,7},{6,22},{7,1},{8,24},{9,11},... | collective-permute-start | bytes 230408 | tf_op jit(solution)/shard_map/ppermute | solution.py:47
  28.0 7.3 %collective-permute-start.32 = (bf16[1,40,960]{2,1,0:T(8,128)(2,1)S(1)}, bf16[1,40,960]{2,1,0:T(8,128)(2,1)S(1)}, u32[]{:S(2)}, u32[]{:S(2)}) collective-permute-start(bf16[1,40,960]{2,1,0:T(8,128)(2,1)S(1)} %slice.608), channel_id=1, source_target_pairs={{0,48},{1,7},{2,50},{3,1},{4,52},{5,3},{6,54},{7,5},{8,56},{9,15},... | collective-permute-start | bytes 230408 | tf_op jit(solution)/shard_map/ppermute | solution.py:47
  29.5 9.9 %collective-permute-start.3 = (bf16[1,16,2688]{2,1,0:T(8,128)(2,1)S(1)}, bf16[1,16,2688]{2,1,0:T(8,128)(2,1)S(1)}, u32[]{:S(2)}, u32[]{:S(2)}) collective-permute-start(bf16[1,16,2688]{2,1,0:T(8,128)(2,1)S(1)} %slice.585), channel_id=1, source_target_pairs={{0,16},{1,3},{2,18},{3,5},{4,20},{5,7},{6,22},{7,1},{8,24},{9,11},... | collective-permute-start | bytes 258056 | tf_op jit(solution)/shard_map/ppermute | solution.py:47
  35.3 24.0 %collective-permute-start.33 = (bf16[8,40,960]{2,1,0:T(8,128)(2,1)S(1)}, bf16[8,40,960]{2,1,0:T(8,128)(2,1)S(1)}, u32[]{:S(2)}, u32[]{:S(2)}) collective-permute-start(bf16[8,40,960]{2,1,0:T(8,128)(2,1)S(1)} %get-tuple-element.148), channel_id=1, source_target_pairs={{0,6},{1,49},{2,0},{3,51},{4,2},{5,53},{6,4},{7,55},{8,14},{9,57},... | collective-permute-start | bytes 1843208 | tf_op jit(solution)/shard_map/ppermute | solution.py:47
  39.4 19.6 %collective-permute-start.34 = (bf16[8,40,960]{2,1,0:T(8,128)(2,1)S(1)}, bf16[8,40,960]{2,1,0:T(8,128)(2,1)S(1)}, u32[]{:S(2)}, u32[]{:S(2)}) collective-permute-start(bf16[8,40,960]{2,1,0:T(8,128)(2,1)S(1)} %get-tuple-element.148), channel_id=1, source_target_pairs={{0,2},{1,17},{2,4},{3,19},{4,6},{5,21},{6,0},{7,23},{8,10},{9,25},... | collective-permute-start | bytes 1843208 | tf_op jit(solution)/shard_map/ppermute | solution.py:47
  40.7 36.0 %collective-permute-start.37 = (bf16[8,40,960]{2,1,0:T(8,128)(2,1)S(1)}, bf16[8,40,960]{2,1,0:T(8,128)(2,1)S(1)}, u32[]{:S(2)}, u32[]{:S(2)}) collective-permute-start(bf16[8,40,960]{2,1,0:T(8,128)(2,1)S(1)} %get-tuple-element.148), channel_id=1, source_target_pairs={{0,1},{1,0},{2,3},{3,2},{4,5},{5,4},{6,7},{7,6},{8,9},{9,8},{10,11... | collective-permute-start | bytes 1843208 | tf_op jit(solution)/shard_map/ppermute | solution.py:47
  42.0 27.5 %collective-permute-start.5 = (bf16[8,16,2688]{2,1,0:T(8,128)(2,1)S(1)}, bf16[8,16,2688]{2,1,0:T(8,128)(2,1)S(1)}, u32[]{:S(2)}, u32[]{:S(2)}) collective-permute-start(bf16[8,16,2688]{2,1,0:T(8,128)(2,1)S(1)} %get-tuple-element.144), channel_id=1, source_target_pairs={{0,6},{1,49},{2,0},{3,51},{4,2},{5,53},{6,4},{7,55},{8,14},{9,57},... | collective-permute-start | bytes 2064392 | tf_op jit(solution)/shard_map/ppermute | solution.py:47
  45.5 6.6 %collective-permute-start.17 = (bf16[1,16,5120]{2,1,0:T(8,128)(2,1)S(1)}, bf16[1,16,5120]{2,1,0:T(8,128)(2,1)S(1)}, u32[]{:S(2)}, u32[]{:S(2)}) collective-permute-start(bf16[1,16,5120]{2,1,0:T(8,128)(2,1)S(1)} %slice.601), channel_id=1, source_target_pairs={{0,16},{1,3},{2,18},{3,5},{4,20},{5,7},{6,22},{7,1},{8,24},{9,11},... | collective-permute-start | bytes 491528 | tf_op jit(solution)/shard_map/ppermute | solution.py:47
  57.4 12.1 %collective-permute-start.6 = (bf16[8,16,2688]{2,1,0:T(8,128)(2,1)S(1)}, bf16[8,16,2688]{2,1,0:T(8,128)(2,1)S(1)}, u32[]{:S(2)}, u32[]{:S(2)}) collective-permute-start(bf16[8,16,2688]{2,1,0:T(8,128)(2,1)S(1)} %get-tuple-element.144), channel_id=1, source_target_pairs={{0,2},{1,17},{2,4},{3,19},{4,6},{5,21},{6,0},{7,23},{8,10},{9,25},... | collective-permute-start | bytes 2064392 | tf_op jit(solution)/shard_map/ppermute | solution.py:47
  59.0 27.2 %collective-permute-start.9 = (bf16[8,16,2688]{2,1,0:T(8,128)(2,1)S(1)}, bf16[8,16,2688]{2,1,0:T(8,128)(2,1)S(1)}, u32[]{:S(2)}, u32[]{:S(2)}) collective-permute-start(bf16[8,16,2688]{2,1,0:T(8,128)(2,1)S(1)} %get-tuple-element.144), channel_id=1, source_target_pairs={{0,1},{1,0},{2,3},{3,2},{4,5},{5,4},{6,7},{7,6},{8,9},{9,8},{10,11... | collective-permute-start | bytes 2064392 | tf_op jit(solution)/shard_map/ppermute | solution.py:47
  59.3 13.8 %collective-permute-start.35 = (bf16[4,40,960]{2,1,0:T(8,128)(2,1)S(1)}, bf16[4,40,960]{2,1,0:T(8,128)(2,1)S(1)}, u32[]{:S(2)}, u32[]{:S(2)}) collective-permute-start(bf16[4,40,960]{2,1,0:T(8,128)(2,1)S(1)} %slice.609), channel_id=1, source_target_pairs={{0,2},{1,17},{2,4},{3,19},{4,6},{5,21},{6,0},{7,23},{8,10},{9,25},... | collective-permute-start | bytes 921608 | tf_op jit(solution)/shard_map/ppermute | solution.py:47
  69.5 7.1 %collective-permute-start.36 = (bf16[4,40,960]{2,1,0:T(8,128)(2,1)S(1)}, bf16[4,40,960]{2,1,0:T(8,128)(2,1)S(1)}, u32[]{:S(2)}, u32[]{:S(2)}) collective-permute-start(bf16[4,40,960]{2,1,0:T(8,128)(2,1)S(1)} %slice.610), channel_id=1, source_target_pairs={{0,6},{1,49},{2,0},{3,51},{4,2},{5,53},{6,4},{7,55},{8,14},{9,57},... | collective-permute-start | bytes 921608 | tf_op jit(solution)/shard_map/ppermute | solution.py:47
  69.6 16.9 %collective-permute-start.38 = (bf16[8,40,960]{2,1,0:T(8,128)(2,1)S(1)}, bf16[8,40,960]{2,1,0:T(8,128)(2,1)S(1)}, u32[]{:S(2)}, u32[]{:S(2)}) collective-permute-start(bf16[8,40,960]{2,1,0:T(8,128)(2,1)S(1)} %collective-permute-done.33), channel_id=1, source_target_pairs={{0,1},{1,0},{2,3},{3,2},{4,5},{5,4},{6,7},{7,6},{8,9},{9,8},{10,11... | collective-permute-start | bytes 1843208 | tf_op jit(solution)/shard_map/ppermute | solution.py:47
  73.0 17.0 %collective-permute-start.41 = (bf16[8,40,960]{2,1,0:T(8,128)(2,1)S(1)}, bf16[8,40,960]{2,1,0:T(8,128)(2,1)S(1)}, u32[]{:S(2)}, u32[]{:S(2)}) collective-permute-start(bf16[8,40,960]{2,1,0:T(8,128)(2,1)S(1)} %collective-permute-done.34), channel_id=1, source_target_pairs={{0,1},{1,0},{2,3},{3,2},{4,5},{5,4},{6,7},{7,6},{8,9},{9,8},{10,11... | collective-permute-start | bytes 1843208 | tf_op jit(solution)/shard_map/ppermute | solution.py:47
  76.6 8.5 %collective-permute-start.7 = (bf16[4,16,2688]{2,1,0:T(8,128)(2,1)S(1)}, bf16[4,16,2688]{2,1,0:T(8,128)(2,1)S(1)}, u32[]{:S(2)}, u32[]{:S(2)}) collective-permute-start(bf16[4,16,2688]{2,1,0:T(8,128)(2,1)S(1)} %slice.587), channel_id=1, source_target_pairs={{0,2},{1,17},{2,4},{3,19},{4,6},{5,21},{6,0},{7,23},{8,10},{9,25},... | collective-permute-start | bytes 1032200 | tf_op jit(solution)/shard_map/ppermute | solution.py:47
  76.7 8.4 %collective-permute-start.8 = (bf16[4,16,2688]{2,1,0:T(8,128)(2,1)S(1)}, bf16[4,16,2688]{2,1,0:T(8,128)(2,1)S(1)}, u32[]{:S(2)}, u32[]{:S(2)}) collective-permute-start(bf16[4,16,2688]{2,1,0:T(8,128)(2,1)S(1)} %slice.588), channel_id=1, source_target_pairs={{0,6},{1,49},{2,0},{3,51},{4,2},{5,53},{6,4},{7,55},{8,14},{9,57},... | collective-permute-start | bytes 1032200 | tf_op jit(solution)/shard_map/ppermute | solution.py:47
  85.1 6.9 %collective-permute-start.10 = (bf16[8,16,2688]{2,1,0:T(8,128)(2,1)S(1)}, bf16[8,16,2688]{2,1,0:T(8,128)(2,1)S(1)}, u32[]{:S(2)}, u32[]{:S(2)}) collective-permute-start(bf16[8,16,2688]{2,1,0:T(8,128)(2,1)S(1)} %collective-permute-done.5), channel_id=1, source_target_pairs={{0,1},{1,0},{2,3},{3,2},{4,5},{5,4},{6,7},{7,6},{8,9},{9,8},{10,11... | collective-permute-start | bytes 2064392 | tf_op jit(solution)/shard_map/ppermute | solution.py:47
  86.5 28.3 %collective-permute-start.19 = (bf16[8,16,5120]{2,1,0:T(8,128)(2,1)}, bf16[8,16,5120]{2,1,0:T(8,128)(2,1)S(1)}, u32[]{:S(2)}, u32[]{:S(2)}) collective-permute-start(bf16[8,16,5120]{2,1,0:T(8,128)(2,1)} %get-tuple-element.121), channel_id=1, source_target_pairs={{0,6},{1,49},{2,0},{3,51},{4,2},{5,53},{6,4},{7,55},{8,14},{9,57},... | collective-permute-start | bytes 3932168 | tf_op jit(solution)/shard_map/ppermute | solution.py:47
  89.8 23.8 %collective-permute-start.20 = (bf16[8,16,5120]{2,1,0:T(8,128)(2,1)}, bf16[8,16,5120]{2,1,0:T(8,128)(2,1)S(1)}, u32[]{:S(2)}, u32[]{:S(2)}) collective-permute-start(bf16[8,16,5120]{2,1,0:T(8,128)(2,1)} %get-tuple-element.121), channel_id=1, source_target_pairs={{0,2},{1,17},{2,4},{3,19},{4,6},{5,21},{6,0},{7,23},{8,10},{9,25},... | collective-permute-start | bytes 3932168 | tf_op jit(solution)/shard_map/ppermute | solution.py:47
  90.0 39.1 %collective-permute-start.23 = (bf16[8,16,5120]{2,1,0:T(8,128)(2,1)}, bf16[8,16,5120]{2,1,0:T(8,128)(2,1)}, u32[]{:S(2)}, u32[]{:S(2)}) collective-permute-start(bf16[8,16,5120]{2,1,0:T(8,128)(2,1)} %get-tuple-element.121), channel_id=1, source_target_pairs={{0,1},{1,0},{2,3},{3,2},{4,5},{5,4},{6,7},{7,6},{8,9},{9,8},{10,11... | collective-permute-start | bytes 3932168 | tf_op jit(solution)/shard_map/ppermute | solution.py:47
  113.7 11.9 %collective-permute-start.21 = (bf16[4,16,5120]{2,1,0:T(8,128)(2,1)S(1)}, bf16[4,16,5120]{2,1,0:T(8,128)(2,1)S(1)}, u32[]{:S(2)}, u32[]{:S(2)}) collective-permute-start(bf16[4,16,5120]{2,1,0:T(8,128)(2,1)S(1)} %slice.603), channel_id=1, source_target_pairs={{0,2},{1,17},{2,4},{3,19},{4,6},{5,21},{6,0},{7,23},{8,10},{9,25},... | collective-permute-start | bytes 1966088 | tf_op jit(solution)/shard_map/ppermute | solution.py:47
  114.8 11.6 %collective-permute-start.22 = (bf16[4,16,5120]{2,1,0:T(8,128)(2,1)S(1)}, bf16[4,16,5120]{2,1,0:T(8,128)(2,1)S(1)}, u32[]{:S(2)}, u32[]{:S(2)}) collective-permute-start(bf16[4,16,5120]{2,1,0:T(8,128)(2,1)S(1)} %slice.604), channel_id=1, source_target_pairs={{0,6},{1,49},{2,0},{3,51},{4,2},{5,53},{6,4},{7,55},{8,14},{9,57},... | collective-permute-start | bytes 1966088 | tf_op jit(solution)/shard_map/ppermute | solution.py:47
  118.1 13.4 %collective-permute-start.24 = (bf16[8,16,5120]{2,1,0:T(8,128)(2,1)S(1)}, bf16[8,16,5120]{2,1,0:T(8,128)(2,1)S(1)}, u32[]{:S(2)}, u32[]{:S(2)}) collective-permute-start(bf16[8,16,5120]{2,1,0:T(8,128)(2,1)S(1)} %collective-permute-done.19), channel_id=1, source_target_pairs={{0,1},{1,0},{2,3},{3,2},{4,5},{5,4},{6,7},{7,6},{8,9},{9,8},{10,11... | collective-permute-start | bytes 3932168 | tf_op jit(solution)/shard_map/ppermute | solution.py:47
  118.1 16.4 %collective-permute-start.27 = (bf16[8,16,5120]{2,1,0:T(8,128)(2,1)S(1)}, bf16[8,16,5120]{2,1,0:T(8,128)(2,1)S(1)}, u32[]{:S(2)}, u32[]{:S(2)}) collective-permute-start(bf16[8,16,5120]{2,1,0:T(8,128)(2,1)S(1)} %collective-permute-done.20), channel_id=1, source_target_pairs={{0,1},{1,0},{2,3},{3,2},{4,5},{5,4},{6,7},{7,6},{8,9},{9,8},{10,11... | collective-permute-start | bytes 3932168 | tf_op jit(solution)/shard_map/ppermute | solution.py:47
  125.5 7.1 %collective-permute-start.25 = (bf16[4,16,5120]{2,1,0:T(8,128)(2,1)S(1)}, bf16[4,16,5120]{2,1,0:T(8,128)(2,1)S(1)}, u32[]{:S(2)}, u32[]{:S(2)}) collective-permute-start(bf16[4,16,5120]{2,1,0:T(8,128)(2,1)S(1)} %collective-permute-done.21), channel_id=1, source_target_pairs={{0,1},{1,0},{2,3},{3,2},{4,5},{5,4},{6,7},{7,6},{8,9},{9,8},{10,11... | collective-permute-start | bytes 1966088 | tf_op jit(solution)/shard_map/ppermute | solution.py:47
  126.4 7.1 %collective-permute-start.26 = (bf16[4,16,5120]{2,1,0:T(8,128)(2,1)S(1)}, bf16[4,16,5120]{2,1,0:T(8,128)(2,1)S(1)}, u32[]{:S(2)}, u32[]{:S(2)}) collective-permute-start(bf16[4,16,5120]{2,1,0:T(8,128)(2,1)S(1)} %collective-permute-done.22), channel_id=1, source_target_pairs={{0,1},{1,0},{2,3},{3,2},{4,5},{5,4},{6,7},{7,6},{8,9},{9,8},{10,11... | collective-permute-start | bytes 1966088 | tf_op jit(solution)/shard_map/ppermute | solution.py:47
  143.9 10.0 %collective-permute-start.42 = (bf16[128,960]{0,1:T(8,128)(2,1)S(1)}, bf16[128,960]{0,1:T(8,128)(2,1)S(1)}, u32[]{:S(2)}, u32[]{:S(2)}) collective-permute-start(bf16[128,960]{0,1:T(8,128)(2,1)S(1)} %fusion.108), channel_id=1, source_target_pairs={{0,64},{1,65},{2,66},{3,67},{4,68},{5,69},{6,70},{7,71},{8,72},{9,... | collective-permute-start | bytes 737288 | tf_op jit(solution)/shard_map/ppermute | solution.py:150
  215.0 14.3 %collective-permute-start.43 = (bf16[128,960]{0,1:T(8,128)(2,1)}, bf16[128,960]{0,1:T(8,128)(2,1)}, u32[]{:S(2)}, u32[]{:S(2)}) collective-permute-start(bf16[128,960]{0,1:T(8,128)(2,1)} %fusion.109), channel_id=1, source_target_pairs={{0,64},{1,65},{2,66},{3,67},{4,68},{5,69},{6,70},{7,71},{8,72},{9,... | collective-permute-start | bytes 737288 | tf_op jit(solution)/shard_map/ppermute | solution.py:150
  267.4 10.1 %collective-permute-start.44 = (bf16[128,960]{0,1:T(8,128)(2,1)S(1)}, bf16[128,960]{0,1:T(8,128)(2,1)S(1)}, u32[]{:S(2)}, u32[]{:S(2)}) collective-permute-start(bf16[128,960]{0,1:T(8,128)(2,1)S(1)} %fusion.161), channel_id=1, source_target_pairs={{64,0},{65,1},{66,2},{67,3},{68,4},{69,5},{70,6},{71,7},{72,8},{73... | collective-permute-start | bytes 737288 | tf_op jit(solution)/shard_map/ppermute | solution.py:150
  305.3 9.6 %collective-permute-start.45 = (bf16[128,960]{0,1:T(8,128)(2,1)S(1)}, bf16[128,960]{0,1:T(8,128)(2,1)S(1)}, u32[]{:S(2)}, u32[]{:S(2)}) collective-permute-start(bf16[128,960]{0,1:T(8,128)(2,1)S(1)} %get-tuple-element.44), channel_id=1, source_target_pairs={{64,0},{65,1},{66,2},{67,3},{68,4},{69,5},{70,6},{71,7},{72,8},{73... | collective-permute-start | bytes 737288 | tf_op jit(solution)/shard_map/ppermute | solution.py:150
  362.3 51.4 %collective-permute-start.66 = (bf16[32,40,960]{2,1,0:T(8,128)(2,1)}, bf16[32,40,960]{2,1,0:T(8,128)(2,1)}, u32[]{:S(2)}, u32[]{:S(2)}) collective-permute-start(bf16[32,40,960]{2,1,0:T(8,128)(2,1)} %slice.695), channel_id=1, source_target_pairs={{0,1},{1,0},{2,3},{3,2},{4,5},{5,4},{6,7},{7,6},{8,9},{9,8},{10,11... | collective-permute-start | bytes 7372808 | tf_op jit(solution)/shard_map/ppermute | solution.py:47
  381.8 39.2 %collective-permute-start.46 = (bf16[32,16,2688]{2,1,0:T(8,128)(2,1)}, bf16[32,16,2688]{2,1,0:T(8,128)(2,1)}, u32[]{:S(2)}, u32[]{:S(2)}) collective-permute-start(bf16[32,16,2688]{2,1,0:T(8,128)(2,1)} %bitcast.555), channel_id=1, source_target_pairs={{0,1},{1,0},{2,3},{3,2},{4,5},{5,4},{6,7},{7,6},{8,9},{9,8},{10,11... | collective-permute-start | bytes 8257544 | tf_op jit(solution)/shard_map/ppermute | solution.py:47
  413.3 52.2 %collective-permute-start.56 = (bf16[32,16,5120]{2,1,0:T(8,128)(2,1)}, bf16[32,16,5120]{2,1,0:T(8,128)(2,1)}, u32[]{:S(2)}, u32[]{:S(2)}) collective-permute-start(bf16[32,16,5120]{2,1,0:T(8,128)(2,1)} %bitcast.155), channel_id=1, source_target_pairs={{0,1},{1,0},{2,3},{3,2},{4,5},{5,4},{6,7},{7,6},{8,9},{9,8},{10,11... | collective-permute-start | bytes 15728648 | tf_op jit(solution)/shard_map/ppermute | solution.py:47
  416.7 10.5 %collective-permute-start.67 = (bf16[4,40,960]{2,1,0:T(8,128)(2,1)S(1)}, bf16[4,40,960]{2,1,0:T(8,128)(2,1)S(1)}, u32[]{:S(2)}, u32[]{:S(2)}) collective-permute-start(bf16[4,40,960]{2,1,0:T(8,128)(2,1)S(1)} %get-tuple-element.75), channel_id=1, source_target_pairs={{0,2},{1,17},{2,4},{3,19},{4,6},{5,21},{6,0},{7,23},{8,10},{9,25},... | collective-permute-start | bytes 921608 | tf_op jit(solution)/shard_map/ppermute | solution.py:47
  419.1 8.0 %collective-permute-start.69 = (bf16[4,40,960]{2,1,0:T(8,128)(2,1)S(1)}, bf16[4,40,960]{2,1,0:T(8,128)(2,1)S(1)}, u32[]{:S(2)}, u32[]{:S(2)}) collective-permute-start(bf16[4,40,960]{2,1,0:T(8,128)(2,1)S(1)} %get-tuple-element.76), channel_id=1, source_target_pairs={{0,6},{1,49},{2,0},{3,51},{4,2},{5,53},{6,4},{7,55},{8,14},{9,57},... | collective-permute-start | bytes 921608 | tf_op jit(solution)/shard_map/ppermute | solution.py:47
  423.7 8.5 %collective-permute-start.47 = (bf16[4,16,2688]{2,1,0:T(8,128)(2,1)S(1)}, bf16[4,16,2688]{2,1,0:T(8,128)(2,1)S(1)}, u32[]{:S(2)}, u32[]{:S(2)}) collective-permute-start(bf16[4,16,2688]{2,1,0:T(8,128)(2,1)S(1)} %get-tuple-element.69), channel_id=1, source_target_pairs={{0,2},{1,17},{2,4},{3,19},{4,6},{5,21},{6,0},{7,23},{8,10},{9,25},... | collective-permute-start | bytes 1032200 | tf_op jit(solution)/shard_map/ppermute | solution.py:47
  423.9 8.3 %collective-permute-start.49 = (bf16[4,16,2688]{2,1,0:T(8,128)(2,1)S(1)}, bf16[4,16,2688]{2,1,0:T(8,128)(2,1)S(1)}, u32[]{:S(2)}, u32[]{:S(2)}) collective-permute-start(bf16[4,16,2688]{2,1,0:T(8,128)(2,1)S(1)} %get-tuple-element.70), channel_id=1, source_target_pairs={{0,6},{1,49},{2,0},{3,51},{4,2},{5,53},{6,4},{7,55},{8,14},{9,57},... | collective-permute-start | bytes 1032200 | tf_op jit(solution)/shard_map/ppermute | solution.py:47
  427.5 11.5 %collective-permute-start.70 = (bf16[8,40,960]{2,1,0:T(8,128)(2,1)S(1)}, bf16[8,40,960]{2,1,0:T(8,128)(2,1)S(1)}, u32[]{:S(2)}, u32[]{:S(2)}) collective-permute-start(bf16[8,40,960]{2,1,0:T(8,128)(2,1)S(1)} %pad_maximum_fusion.16), channel_id=1, source_target_pairs={{0,6},{1,49},{2,0},{3,51},{4,2},{5,53},{6,4},{7,55},{8,14},{9,57},... | collective-permute-start | bytes 1843208 | tf_op jit(solution)/shard_map/ppermute | solution.py:47
  429.8 11.9 %collective-permute-start.68 = (bf16[8,40,960]{2,1,0:T(8,128)(2,1)S(1)}, bf16[8,40,960]{2,1,0:T(8,128)(2,1)S(1)}, u32[]{:S(2)}, u32[]{:S(2)}) collective-permute-start(bf16[8,40,960]{2,1,0:T(8,128)(2,1)S(1)} %pad_maximum_fusion.15), channel_id=1, source_target_pairs={{0,2},{1,17},{2,4},{3,19},{4,6},{5,21},{6,0},{7,23},{8,10},{9,25},... | collective-permute-start | bytes 1843208 | tf_op jit(solution)/shard_map/ppermute | solution.py:47
  432.5 25.7 %collective-permute-start.50 = (bf16[8,16,2688]{2,1,0:T(8,128)(2,1)S(1)}, bf16[8,16,2688]{2,1,0:T(8,128)(2,1)S(1)}, u32[]{:S(2)}, u32[]{:S(2)}) collective-permute-start(bf16[8,16,2688]{2,1,0:T(8,128)(2,1)S(1)} %pad_maximum_fusion.14), channel_id=1, source_target_pairs={{0,6},{1,49},{2,0},{3,51},{4,2},{5,53},{6,4},{7,55},{8,14},{9,57},... | collective-permute-start | bytes 2064392 | tf_op jit(solution)/shard_map/ppermute | solution.py:47
  442.1 6.6 %collective-permute-start.71 = (bf16[1,40,960]{2,1,0:T(8,128)(2,1)S(1)}, bf16[1,40,960]{2,1,0:T(8,128)(2,1)S(1)}, u32[]{:S(2)}, u32[]{:S(2)}) collective-permute-start(bf16[1,40,960]{2,1,0:T(8,128)(2,1)S(1)} %get-tuple-element.97), channel_id=1, source_target_pairs={{0,16},{1,3},{2,18},{3,5},{4,20},{5,7},{6,22},{7,1},{8,24},{9,11},... | collective-permute-start | bytes 230408 | tf_op jit(solution)/shard_map/ppermute | solution.py:47
  442.2 6.5 %collective-permute-start.73 = (bf16[1,40,960]{2,1,0:T(8,128)(2,1)S(1)}, bf16[1,40,960]{2,1,0:T(8,128)(2,1)S(1)}, u32[]{:S(2)}, u32[]{:S(2)}) collective-permute-start(bf16[1,40,960]{2,1,0:T(8,128)(2,1)S(1)} %get-tuple-element.98), channel_id=1, source_target_pairs={{0,48},{1,7},{2,50},{3,1},{4,52},{5,3},{6,54},{7,5},{8,56},{9,15},... | collective-permute-start | bytes 230408 | tf_op jit(solution)/shard_map/ppermute | solution.py:47
  445.4 14.0 %collective-permute-start.48 = (bf16[8,16,2688]{2,1,0:T(8,128)(2,1)S(1)}, bf16[8,16,2688]{2,1,0:T(8,128)(2,1)S(1)}, u32[]{:S(2)}, u32[]{:S(2)}) collective-permute-start(bf16[8,16,2688]{2,1,0:T(8,128)(2,1)S(1)} %pad_maximum_fusion.13), channel_id=1, source_target_pairs={{0,2},{1,17},{2,4},{3,19},{4,6},{5,21},{6,0},{7,23},{8,10},{9,25},... | collective-permute-start | bytes 2064392 | tf_op jit(solution)/shard_map/ppermute | solution.py:47
  451.2 6.6 %collective-permute-start.72 = (bf16[2,40,960]{2,1,0:T(8,128)(2,1)S(1)}, bf16[2,40,960]{2,1,0:T(8,128)(2,1)S(1)}, u32[]{:S(2)}, u32[]{:S(2)}) collective-permute-start(bf16[2,40,960]{2,1,0:T(8,128)(2,1)S(1)} %pad_maximum_fusion.50), channel_id=1, source_target_pairs={{0,16},{1,3},{2,18},{3,5},{4,20},{5,7},{6,22},{7,1},{8,24},{9,11},... | collective-permute-start | bytes 460808 | tf_op jit(solution)/shard_map/ppermute | solution.py:47
  470.3 13.7 %collective-permute-start.57 = (bf16[4,16,5120]{2,1,0:T(8,128)(2,1)S(1)}, bf16[4,16,5120]{2,1,0:T(8,128)(2,1)S(1)}, u32[]{:S(2)}, u32[]{:S(2)}) collective-permute-start(bf16[4,16,5120]{2,1,0:T(8,128)(2,1)S(1)} %get-tuple-element.57), channel_id=1, source_target_pairs={{0,2},{1,17},{2,4},{3,19},{4,6},{5,21},{6,0},{7,23},{8,10},{9,25},... | collective-permute-start | bytes 1966088 | tf_op jit(solution)/shard_map/ppermute | solution.py:47
  470.4 13.6 %collective-permute-start.59 = (bf16[4,16,5120]{2,1,0:T(8,128)(2,1)S(1)}, bf16[4,16,5120]{2,1,0:T(8,128)(2,1)S(1)}, u32[]{:S(2)}, u32[]{:S(2)}) collective-permute-start(bf16[4,16,5120]{2,1,0:T(8,128)(2,1)S(1)} %get-tuple-element.58), channel_id=1, source_target_pairs={{0,6},{1,49},{2,0},{3,51},{4,2},{5,53},{6,4},{7,55},{8,14},{9,57},... | collective-permute-start | bytes 1966088 | tf_op jit(solution)/shard_map/ppermute | solution.py:47
  473.6 13.1 %collective-permute-start.54 = (bf16[2,16,2688]{2,1,0:T(8,128)(2,1)S(1)}, bf16[2,16,2688]{2,1,0:T(8,128)(2,1)S(1)}, u32[]{:S(2)}, u32[]{:S(2)}) collective-permute-start(bf16[2,16,2688]{2,1,0:T(8,128)(2,1)S(1)} %pad_maximum_fusion.44), channel_id=1, source_target_pairs={{0,48},{1,7},{2,50},{3,1},{4,52},{5,3},{6,54},{7,5},{8,56},{9,15},... | collective-permute-start | bytes 516104 | tf_op jit(solution)/shard_map/ppermute | solution.py:47
  476.9 9.8 %collective-permute-start.52 = (bf16[2,16,2688]{2,1,0:T(8,128)(2,1)S(1)}, bf16[2,16,2688]{2,1,0:T(8,128)(2,1)S(1)}, u32[]{:S(2)}, u32[]{:S(2)}) collective-permute-start(bf16[2,16,2688]{2,1,0:T(8,128)(2,1)S(1)} %pad_maximum_fusion.43), channel_id=1, source_target_pairs={{0,16},{1,3},{2,18},{3,5},{4,20},{5,7},{6,22},{7,1},{8,24},{9,11},... | collective-permute-start | bytes 516104 | tf_op jit(solution)/shard_map/ppermute | solution.py:47
  484.4 17.7 %collective-permute-start.60 = (bf16[8,16,5120]{2,1,0:T(8,128)(2,1)S(1)}, bf16[8,16,5120]{2,1,0:T(8,128)(2,1)S(1)}, u32[]{:S(2)}, u32[]{:S(2)}) collective-permute-start(bf16[8,16,5120]{2,1,0:T(8,128)(2,1)S(1)} %pad_maximum_fusion.7), channel_id=1, source_target_pairs={{0,6},{1,49},{2,0},{3,51},{4,2},{5,53},{6,4},{7,55},{8,14},{9,57},... | collective-permute-start | bytes 3932168 | tf_op jit(solution)/shard_map/ppermute | solution.py:47
  486.0 19.1 %collective-permute-start.58 = (bf16[8,16,5120]{2,1,0:T(8,128)(2,1)S(1)}, bf16[8,16,5120]{2,1,0:T(8,128)(2,1)S(1)}, u32[]{:S(2)}, u32[]{:S(2)}) collective-permute-start(bf16[8,16,5120]{2,1,0:T(8,128)(2,1)S(1)} %pad_maximum_fusion.6), channel_id=1, source_target_pairs={{0,2},{1,17},{2,4},{3,19},{4,6},{5,21},{6,0},{7,23},{8,10},{9,25},... | collective-permute-start | bytes 3932168 | tf_op jit(solution)/shard_map/ppermute | solution.py:47
  486.8 24.0 %collective-permute-start.55 = (bf16[16,2688]{1,0:T(8,128)(2,1)S(1)}, bf16[16,2688]{1,0:T(8,128)(2,1)S(1)}, u32[]{:S(2)}, u32[]{:S(2)}) collective-permute-start(bf16[16,2688]{1,0:T(8,128)(2,1)S(1)} %slice_bitcast_fusion.27), channel_id=1, source_target_pairs={{0,8},{1,9},{2,10},{3,11},{4,12},{5,13},{6,14},{7,15},{8,0},{9,1},... | collective-permute-start | bytes 258056 | tf_op jit(solution)/shard_map/ppermute | solution.py:47
  505.8 8.1 %collective-permute-start.61 = (bf16[1,16,5120]{2,1,0:T(8,128)(2,1)S(1)}, bf16[1,16,5120]{2,1,0:T(8,128)(2,1)S(1)}, u32[]{:S(2)}, u32[]{:S(2)}) collective-permute-start(bf16[1,16,5120]{2,1,0:T(8,128)(2,1)S(1)} %get-tuple-element.83), channel_id=1, source_target_pairs={{0,16},{1,3},{2,18},{3,5},{4,20},{5,7},{6,22},{7,1},{8,24},{9,11},... | collective-permute-start | bytes 491528 | tf_op jit(solution)/shard_map/ppermute | solution.py:47
  505.9 8.1 %collective-permute-start.63 = (bf16[1,16,5120]{2,1,0:T(8,128)(2,1)S(1)}, bf16[1,16,5120]{2,1,0:T(8,128)(2,1)S(1)}, u32[]{:S(2)}, u32[]{:S(2)}) collective-permute-start(bf16[1,16,5120]{2,1,0:T(8,128)(2,1)S(1)} %get-tuple-element.84), channel_id=1, source_target_pairs={{0,48},{1,7},{2,50},{3,1},{4,52},{5,3},{6,54},{7,5},{8,56},{9,15},... | collective-permute-start | bytes 491528 | tf_op jit(solution)/shard_map/ppermute | solution.py:47
  514.1 8.0 %collective-permute-start.64 = (bf16[2,16,5120]{2,1,0:T(8,128)(2,1)S(1)}, bf16[2,16,5120]{2,1,0:T(8,128)(2,1)S(1)}, u32[]{:S(2)}, u32[]{:S(2)}) collective-permute-start(bf16[2,16,5120]{2,1,0:T(8,128)(2,1)S(1)} %pad_maximum_fusion.27), channel_id=1, source_target_pairs={{0,48},{1,7},{2,50},{3,1},{4,52},{5,3},{6,54},{7,5},{8,56},{9,15},... | collective-permute-start | bytes 983048 | tf_op jit(solution)/shard_map/ppermute | solution.py:47
  517.5 8.4 %collective-permute-start.62 = (bf16[2,16,5120]{2,1,0:T(8,128)(2,1)S(1)}, bf16[2,16,5120]{2,1,0:T(8,128)(2,1)S(1)}, u32[]{:S(2)}, u32[]{:S(2)}) collective-permute-start(bf16[2,16,5120]{2,1,0:T(8,128)(2,1)S(1)} %pad_maximum_fusion.26), channel_id=1, source_target_pairs={{0,16},{1,3},{2,18},{3,5},{4,20},{5,7},{6,22},{7,1},{8,24},{9,11},... | collective-permute-start | bytes 983048 | tf_op jit(solution)/shard_map/ppermute | solution.py:47
  (184 other events, 1195.9 us)

commit v2 on v1

v2 whole, which is shorter than its diff:
```python
import jax
import jax.numpy as jnp
from jax import lax
from jax.experimental import pallas as pl
from jax.experimental.pallas import tpu as pltpu
from jax.sharding import PartitionSpec as P

D = 960
H = 15
KV = 5
HD = 64
FF = 2560
QKV = D + 2 * KV * HD
N_DP = 64
ROWS = D // N_DP
PAD = 16
FROWS = FF // N_DP
LANES = 128
QKV_PAD = 1664
OUT_PAD = 1024

EPSILON = 1e-05
ROPE_BASE = 100000.0
BF16 = jnp.bfloat16
F32 = jnp.float32


def place(y, x, z, core):
    return ((y % 4 * 2 + x % 2) * 4 + z % 4) * 2 + core % 2


def route(kind, step):
    pairs = []
    for source in range(N_DP):
        y, x, z, core = source // 16, source // 8 % 2, source // 2 % 4, source % 2
        if kind == "core":
            target = place(y, x, z, core + 1)
        elif kind == "x":
            target = place(y, x + 1, z, core)
        elif (kind == "wide") == (core == 0):
            target = place(y, x, z + step, core)
        else:
            target = place(y + step, x, z, core)
        pairs.append((source, target))
    return pairs


def send(block, kind, step=1):
    return lax.ppermute(block, "dp", route(kind, step))


def total(*terms):
    result = terms[0].astype(F32)
    for term in terms[1:]:
        result = result + term.astype(F32)
    return result


def near_scatter(blocks):
    blocks = yield from ring_scatter(blocks, "narrow")
    (got,) = yield (send(blocks[1], "x"),)
    return total(blocks[0], got)


def ring_scatter(blocks, kind):
    blocks = blocks.reshape((4, blocks.shape[0] // 4) + blocks.shape[1:])
    half = blocks.shape[1] // 2
    left, right = yield (send(blocks[3, :half], kind, 1), send(blocks[3, half:], kind, -1))
    onward = jnp.concatenate([total(blocks[1, :half], left).astype(BF16), blocks[1, half:]], 0)
    back = jnp.concatenate([blocks[2, :half], total(blocks[2, half:], right).astype(BF16)], 0)
    left, right = yield (send(onward, kind, 1), send(back, kind, -1))
    return total(blocks[0], left, right).astype(BF16)


def far_scatter(for_other, for_own):
    (got,) = yield (send(for_other, "core"),)
    blocks = total(for_own(), got).astype(BF16)
    return (yield from ring_scatter(blocks, "wide"))


def down_scatter(for_other, for_own):
    blocks = yield from far_scatter(for_other, for_own)
    return (yield from near_scatter(blocks))


class Flow:
    def __init__(self, stages):
        self.stages = stages
        self.result = None
        self.pending = next(stages)

    def advance(self, arrived):
        try:
            self.pending = self.stages.send(arrived)
        except StopIteration as end:
            self.pending = ()
            self.result = end.value


def step(flows, value):
    flows = [flow for flow in flows if flow.result is None]
    arrived, value = lax.optimization_barrier((tuple(flow.pending for flow in flows), value))
    for flow, got in zip(flows, arrived):
        flow.advance(got)
    return value


def ring_gather(block, kind):
    half = block.shape[0] // 2
    from_left = send(block, kind, 1)
    from_right = send(block, kind, -1)
    far_left = send(from_left[:half], kind, 1)
    far_right = send(from_right[half:], kind, -1)
    sides = jnp.concatenate([from_right, from_left], 0)
    return [block, sides, jnp.concatenate([far_left, far_right], 0)]


def gather_near(shard):
    block = jnp.stack([shard, send(shard, "x")], 0)
    return jnp.concatenate(ring_gather(block, "narrow"), 0)


def gather_far(block):
    pieces = ring_gather(block, "wide")
    others = [send(piece, "core") for piece in pieces]
    return (pieces[2], jnp.concatenate(pieces + others, 0))


def after(value, earlier):
    return lax.optimization_barrier((value, earlier))[0]


def block_order():
    index = lax.axis_index("dp")
    y, x, z, core = index // 16, index // 8 % 2, index // 2 % 4, index % 2
    position = jnp.arange(N_DP)
    core_step, wide, narrow, x_step = position // 32, position // 8 % 4, position // 2 % 4, position % 2
    wide, narrow = wide ^ (wide // 2), narrow ^ (narrow // 2)
    core_there = (core + core_step) % 2
    z_step = jnp.where(core_there == 0, wide, narrow)
    y_step = jnp.where(core_there == 0, narrow, wide)
    return (((y + y_step) % 4 * 2 + (x + x_step) % 2) * 4 + (z + z_step) % 4) * 2 + core_there


def placement(order):
    column = jnp.arange(N_DP * PAD)
    inner = column % PAD
    row = jnp.where(inner < ROWS, jnp.repeat(order, PAD) * ROWS + inner, -1)
    return (jnp.arange(D)[:, None] == row[None, :]).astype(BF16)


def reorder_kernel(scatter, order_ref, blocks_ref, out_ref):
    def one(step, carry):
        there = order_ref[step]
        if scatter:
            out_ref[there] = blocks_ref[step]
        else:
            out_ref[step] = blocks_ref[there]
        return carry

    lax.fori_loop(0, N_DP, one, 0)


def reorder(blocks, order, scatter):
    return pl.pallas_call(
        lambda *refs: reorder_kernel(scatter, *refs),
        out_shape=jax.ShapeDtypeStruct(blocks.shape, blocks.dtype),
        in_specs=[
            pl.BlockSpec(memory_space=pltpu.SMEM),
            pl.BlockSpec(memory_space=pltpu.VMEM),
        ],
        out_specs=pl.BlockSpec(memory_space=pltpu.VMEM),
        compiler_params=pltpu.CompilerParams(vmem_limit_bytes=32 * 1024 * 1024),
    )(order, blocks)


def across(left, right):
    return lax.dot_general(left, right, (((0,), (0,)), ((), ())), preferred_element_type=F32)


VMEM_BYTES = 48 * 1024 * 1024


def down_kernel(place_ref, left_ref, right_ref, out_ref):
    step = pl.program_id(0)
    rows = across(left_ref[...], right_ref[...]).astype(BF16)
    count = rows.shape[0] // FROWS
    for block in range(count):
        out_ref[place_ref[step * count + block]] = rows[block * FROWS : (block + 1) * FROWS]


def down_sums(left, right, places):
    tokens = left.shape[0]
    width = 640
    return pl.pallas_call(
        down_kernel,
        grid=(FF // width,),
        out_shape=jax.ShapeDtypeStruct((N_DP, FROWS, D), BF16),
        in_specs=[
            pl.BlockSpec(memory_space=pltpu.SMEM),
            pl.BlockSpec((tokens, width), lambda i: (0, i)),
            pl.BlockSpec((tokens, D), lambda i: (0, 0)),
        ],
        out_specs=pl.BlockSpec((N_DP, FROWS, D), lambda i: (0, 0, 0)),
        compiler_params=pltpu.CompilerParams(vmem_limit_bytes=VMEM_BYTES),
        cost_estimate=pl.CostEstimate(
            flops=2 * tokens * FF * D, bytes_accessed=2 * FF * D, transcendentals=0
        ),
    )(places, left, right)


def gate_up_kernel(left_ref, gate_ref, up_ref, out_ref):
    left = left_ref[...]
    out_ref[:, :FF] = across(left, gate_ref[...]).astype(BF16)
    out_ref[:, FF:] = across(left, up_ref[...]).astype(BF16)


def gate_up_sums(left, gate, up, first):
    tokens = left.shape[0]
    columns = 2 * FF
    width = 128
    count = N_DP * PAD // 2 // width
    return pl.pallas_call(
        gate_up_kernel,
        grid=(count,),
        out_shape=jax.ShapeDtypeStruct((N_DP * PAD // 2, columns), BF16),
        in_specs=[
            pl.BlockSpec((tokens, width), lambda i: (0, i + first * count)),
            pl.BlockSpec((tokens, FF), lambda i: (0, 0)),
            pl.BlockSpec((tokens, FF), lambda i: (0, 0)),
        ],
        out_specs=pl.BlockSpec((width, columns), lambda i: (i, 0)),
        compiler_params=pltpu.CompilerParams(vmem_limit_bytes=VMEM_BYTES),
        cost_estimate=pl.CostEstimate(
            flops=tokens * N_DP * PAD * columns, bytes_accessed=N_DP * PAD * columns, transcendentals=0
        ),
    )(left, gate, up)


def attn_kernel(left_ref, mixed_ref, proj_ref, attn_ref, gain_ref, out_ref):
    qkv = across(left_ref[...], proj_ref[...])
    edge = QKV_PAD - LANES
    out_ref[:, :edge] = qkv[:, :edge].astype(BF16)
    out_ref[:, edge:QKV_PAD] = (qkv[:, edge:] + gain_ref[...]).astype(BF16)
    out_ref[:, QKV_PAD:] = across(mixed_ref[...], attn_ref[...]).astype(BF16)


def attn_sums(left, mixed, proj, attn, gain, first):
    tokens = left.shape[0]
    width = 128
    count = N_DP * PAD // 2 // width
    columns = QKV_PAD + OUT_PAD
    return pl.pallas_call(
        attn_kernel,
        grid=(count,),
        out_shape=jax.ShapeDtypeStruct((N_DP * PAD // 2, columns), BF16),
        in_specs=[
            pl.BlockSpec((tokens, width), lambda i: (0, i + first * count)),
            pl.BlockSpec((tokens, width), lambda i: (0, i + first * count)),
            pl.BlockSpec((tokens, QKV_PAD), lambda i: (0, 0)),
            pl.BlockSpec((tokens, OUT_PAD), lambda i: (0, 0)),
            pl.BlockSpec((width, LANES), lambda i: (i + first * count, 0)),
        ],
        out_specs=pl.BlockSpec((width, columns), lambda i: (i, 0)),
        compiler_params=pltpu.CompilerParams(vmem_limit_bytes=VMEM_BYTES),
        cost_estimate=pl.CostEstimate(
            flops=tokens * N_DP * PAD * columns, bytes_accessed=N_DP * PAD * columns, transcendentals=0
        ),
    )(left, mixed, proj, attn, gain)


def dot(left, right):
    return jnp.dot(left, right, preferred_element_type=F32)


def dot_t(left, right):
    return lax.dot_general(left, right, (((1,), (1,)), ((), ())), preferred_element_type=F32)


def shifted(block, axis, distance):
    devices = range(lax.axis_size(axis))
    pairs = [(i - distance, i) for i in devices if i - distance in devices]
    return lax.ppermute(block, axis, pairs)


def rope_tables(length):
    position = jnp.arange(length, dtype=F32)[:, None]
    frequency = ROPE_BASE ** (-jnp.arange(0, HD, 2, dtype=F32) / HD)
    angle = position * frequency[None, :]
    cosine, sine = jnp.cos(angle), jnp.sin(angle)
    return (jnp.tile(cosine, (1, LANES // (HD // 2))), jnp.tile(jnp.concatenate([-sine, sine], 1), (1, LANES // HD)))


SCALE = HD**-0.5
TURNED = D + KV * HD
PARTS = 5
PART = FF // PARTS


def params():
    return pltpu.CompilerParams(vmem_limit_bytes=VMEM_BYTES)


def whole(*shape):
    return pl.BlockSpec(shape, lambda *_: (0,) * len(shape))


def scaled(value, gain):
    return value * lax.rsqrt(jnp.mean(value * value, axis=-1, keepdims=True) + EPSILON) * gain


def scaled_backward(value, gain, grad):
    inverse = lax.rsqrt(jnp.mean(value * value, axis=-1, keepdims=True) + EPSILON)
    normed = value * inverse
    inner = grad * gain
    gain_sum = jnp.sum(grad * normed, axis=0, keepdims=True)
    through = inverse * (inner - normed * jnp.mean(inner * normed, axis=-1, keepdims=True))
    return (through, gain_sum)


def turn_heads(value, cosine, sine):
    first = lax.broadcasted_iota(jnp.int32, cosine.shape, 1) % HD < HD // 2
    tiles = []
    for start in range(0, TURNED, LANES):
        tile = value[:, start : start + LANES]
        other = jnp.where(first, pltpu.roll(tile, LANES - HD // 2, 1), pltpu.roll(tile, HD // 2, 1))
        tiles.append(tile * cosine + other * sine)
    return tiles


def head_columns(value, index):
    return value[:, index * HD : index * HD + HD]


def group_rows(value, group):
    return jnp.concatenate(
        [head_columns(value, group * (H // KV) + j) for j in range(H // KV)], 0
    ).astype(BF16)


def probabilities(queries, keys, mask):
    scores = jnp.where(mask > 0, dot_t(queries, keys) * SCALE, -1000000000.0)
    terms = jnp.exp(scores - jnp.max(scores, axis=-1, keepdims=True))
    return terms / jnp.sum(terms, axis=-1, keepdims=True)


def attend_forward_kernel(
    flag_ref, own_ref, got_ref, mask_ref, spread_ref, mat_ref, gains_ref, cosine_ref, sine_ref,
    hidden_ref, heads_ref, mixed_ref, middle_ref, second_ref,
):
    first = flag_ref[0] == 1
    stream = jnp.where(first, own_ref[0].astype(F32), got_ref[...].astype(F32))
    spread = spread_ref[...]
    gains = gains_ref[...]
    hidden = dot(scaled(stream, gains[0:1]).astype(BF16), spread).astype(BF16)
    hidden_ref[...] = hidden
    projected = dot(hidden, mat_ref[:, :QKV_PAD])
    tiles = turn_heads(projected, cosine_ref[...], sine_ref[...])
    for index, tile in enumerate(tiles):
        heads_ref[:, index * LANES : index * LANES + LANES] = tile.astype(BF16)
    heads_ref[:, TURNED:] = projected[:, TURNED:].astype(BF16)
    turned = jnp.concatenate(tiles, 1)
    mask = jnp.concatenate([mask_ref[0]] * (H // KV), 0)
    length = stream.shape[0]
    outs = []
    for group in range(KV):
        queries = group_rows(turned, group)
        keys = head_columns(turned, H + group).astype(BF16)
        values = head_columns(projected, H + KV + group).astype(BF16)
        mixed = dot(probabilities(queries, keys, mask).astype(BF16), values)
        outs += [mixed[j * length : j * length + length] for j in range(H // KV)]
    mixed = dot(jnp.concatenate(outs, 1).astype(BF16), spread).astype(BF16)
    mixed_ref[...] = mixed
    middle = stream + dot(mixed, mat_ref[:, QKV_PAD:])[:, :D]
    middle_ref[...] = middle
    second_ref[...] = dot(scaled(middle, gains[1:2]).astype(BF16), spread).astype(BF16)


def attend_forward(flags, inputs, got, masks, spread, mat, gains, cosine, sine):
    length = got.shape[0]
    wide = N_DP * PAD
    return pl.pallas_call(
        attend_forward_kernel,
        grid_spec=pltpu.PrefetchScalarGridSpec(
            num_scalar_prefetch=1,
            grid=(1,),
            in_specs=[
                pl.BlockSpec((1, length, D), lambda i, flag: (flag[1], 0, 0)),
                whole(length, D),
                pl.BlockSpec((1, length, length), lambda i, flag: (flag[1], 0, 0)),
                whole(D, wide),
                whole(wide, QKV_PAD + OUT_PAD),
                whole(2, D),
                whole(length, LANES),
                whole(length, LANES),
            ],
            out_specs=[
                whole(length, wide),
                whole(length, QKV_PAD),
                whole(length, wide),
                whole(length, D),
                whole(length, wide),
            ],
        ),
        out_shape=[
            jax.ShapeDtypeStruct((length, wide), BF16),
            jax.ShapeDtypeStruct((length, QKV_PAD), BF16),
            jax.ShapeDtypeStruct((length, wide), BF16),
            jax.ShapeDtypeStruct((length, D), F32),
            jax.ShapeDtypeStruct((length, wide), BF16),
        ],
        compiler_params=params(),
        cost_estimate=pl.CostEstimate(
            flops=2 * length * wide * 5700, bytes_accessed=8000000, transcendentals=H * length * length
        ),
    )(flags, inputs, got, masks, spread, mat, gains, cosine, sine)


def mlp_forward_kernel(
    second_ref, middle_ref, gate_mat_ref, up_mat_ref, down_ref, gate_ref, up_ref, act_ref, out_ref, sum_ref
):
    part = pl.program_id(0)
    second = second_ref[...]
    gate = dot(second, gate_mat_ref[...])
    up = dot(second, up_mat_ref[...])
    gate_ref[...] = gate
    up_ref[...] = up
    act = (gate / (1.0 + jnp.exp(-gate)) * up).astype(BF16)
    act_ref[...] = act
    before = jnp.where(part == 0, middle_ref[...], sum_ref[...])
    after_part = before + dot(act, down_ref[...])
    sum_ref[...] = after_part
    out_ref[...] = after_part.astype(BF16)


def mlp_forward(second, middle, gate_up_mat, down_mat):
    length, wide = second.shape
    column = lambda i: (0, i)
    return pl.pallas_call(
        mlp_forward_kernel,
        grid=(PARTS,),
        in_specs=[
            whole(length, wide),
            whole(length, D),
            pl.BlockSpec((wide, PART), column),
            pl.BlockSpec((wide, PART), lambda i: (0, i + PARTS)),
            pl.BlockSpec((PART, D), lambda i: (i, 0)),
        ],
        out_specs=[
            pl.BlockSpec((length, PART), column),
            pl.BlockSpec((length, PART), column),
            pl.BlockSpec((length, PART), column),
            whole(length, D),
        ],
        out_shape=[
            jax.ShapeDtypeStruct((length, FF), F32),
            jax.ShapeDtypeStruct((length, FF), F32),
            jax.ShapeDtypeStruct((length, FF), BF16),
            jax.ShapeDtypeStruct((length, D), BF16),
        ],
        scratch_shapes=[pltpu.VMEM((length, D), F32)],
        compiler_params=params(),
        cost_estimate=pl.CostEstimate(
            flops=2 * length * wide * 7680, bytes_accessed=20000000, transcendentals=length * FF
        ),
    )(second, middle, gate_up_mat, gate_up_mat, down_mat)


def mlp_backward_kernel(
    flag_ref, grad_ref, middle_a_ref, middle_b_ref, gate_a_ref, gate_b_ref, up_a_ref, up_b_ref,
    gate_mat_ref, up_mat_ref, down_ref, spread_ref, gains_ref,
    grad_gate_ref, grad_up_ref, grad_middle_ref, gain_ref, sum_ref,
):
    part = pl.program_id(0)
    first = flag_ref[0] == 1
    gate = jnp.where(first, gate_a_ref[...], gate_b_ref[...])
    up = jnp.where(first, up_a_ref[...], up_b_ref[...])
    grad_act = dot_t(grad_ref[...], down_ref[...])
    sig = 1.0 / (1.0 + jnp.exp(-gate))
    grad_gate = (grad_act * up * sig * (1.0 + gate * (1.0 - sig))).astype(BF16)
    grad_up = (grad_act * gate * sig).astype(BF16)
    grad_gate_ref[...] = grad_gate
    grad_up_ref[...] = grad_up
    more = dot_t(grad_gate, gate_mat_ref[...]) + dot_t(grad_up, up_mat_ref[...])

    @pl.when(part == 0)
    def begin():
        sum_ref[...] = more

    @pl.when(part > 0)
    def go_on():
        sum_ref[...] += more

    @pl.when(part == PARTS - 1)
    def end():
        grad_two = dot_t(sum_ref[...].astype(BF16), spread_ref[...])
        middle = jnp.where(first, middle_a_ref[...], middle_b_ref[...])
        through, gain = scaled_backward(middle, gains_ref[1:2], grad_two)
        grad_middle_ref[...] = grad_ref[...].astype(F32) + through
        gain_ref[...] = gain


def mlp_backward(flags, grad, middles, gates, ups, gate_up_mat, down_mat, spread, gains):
    length = grad.shape[0]
    wide = N_DP * PAD
    column = lambda i, flag: (0, i)
    chosen = pl.BlockSpec((length, PART), lambda i, flag: (0, i * flag[0]))
    other = pl.BlockSpec((length, PART), lambda i, flag: (0, i * (1 - flag[0])))
    return pl.pallas_call(
        mlp_backward_kernel,
        grid_spec=pltpu.PrefetchScalarGridSpec(
            num_scalar_prefetch=1,
            grid=(PARTS,),
            in_specs=[
                whole(length, D),
                whole(length, D),
                whole(length, D),
                chosen,
                other,
                chosen,
                other,
                pl.BlockSpec((wide, PART), column),
                pl.BlockSpec((wide, PART), lambda i, flag: (0, i + PARTS)),
                pl.BlockSpec((PART, D), lambda i, flag: (i, 0)),
                whole(D, wide),
                whole(2, D),
            ],
            out_specs=[
                pl.BlockSpec((length, PART), column),
                pl.BlockSpec((length, PART), column),
                whole(length, D),
                whole(1, D),
            ],
            scratch_shapes=[pltpu.VMEM((length, wide), F32)],
        ),
        out_shape=[
            jax.ShapeDtypeStruct((length, FF), BF16),
            jax.ShapeDtypeStruct((length, FF), BF16),
            jax.ShapeDtypeStruct((length, D), F32),
            jax.ShapeDtypeStruct((1, D), F32),
        ],
        compiler_params=params(),
        cost_estimate=pl.CostEstimate(
            flops=2 * length * wide * 7680, bytes_accessed=22000000, transcendentals=length * FF
        ),
    )(flags, grad, *middles, *gates, *ups, gate_up_mat, gate_up_mat, down_mat, spread, gains)


def attend_backward_kernel(
    flag_ref, grad_ref, own_ref, got_ref, heads_a_ref, heads_b_ref, mask_ref, spread_ref, mat_ref,
    gains_ref, cosine_ref, sine_ref, grad_proj_ref, grad_attn_ref, grad_in_ref, gain_ref,
):
    first = flag_ref[0] == 1
    spread = spread_ref[...]
    grad_middle = grad_ref[...]
    grad_attn = grad_middle.astype(BF16)
    length = grad_middle.shape[0]
    grad_attn_ref[:, :D] = grad_attn
    grad_attn_ref[:, D:] = jnp.zeros((length, OUT_PAD - D), BF16)
    grad_mixed = dot_t(grad_attn, mat_ref[:, QKV_PAD : QKV_PAD + D]).astype(BF16)
    grad_mixed = dot_t(grad_mixed, spread)
    heads = jnp.where(first, heads_a_ref[...].astype(F32), heads_b_ref[...].astype(F32))
    mask = jnp.concatenate([mask_ref[0]] * (H // KV), 0)
    grad_queries, grad_keys, grad_values = [], [], []
    for group in range(KV):
        queries = group_rows(heads, group)
        keys = head_columns(heads, H + group).astype(BF16)
        values = head_columns(heads, H + KV + group).astype(BF16)
        mixed = group_rows(grad_mixed, group)
        probs = probabilities(queries, keys, mask)
        grad_probs = dot_t(mixed, values)
        grad_scores = probs * (grad_probs - jnp.sum(grad_probs * probs, axis=-1, keepdims=True))
        grad_scores = grad_scores.astype(BF16)
        queries_part = dot(grad_scores, keys) * SCALE
        grad_queries += [queries_part[j * length : j * length + length] for j in range(H // KV)]
        grad_keys.append(across(grad_scores, queries) * SCALE)
        grad_values.append(across(probs.astype(BF16), mixed))
    turned = jnp.concatenate(grad_queries + grad_keys, 1).astype(BF16).astype(F32)
    tiles = turn_heads(turned, cosine_ref[...], -sine_ref[...])
    blank = jnp.zeros((length, QKV_PAD - QKV), F32)
    grad_proj = jnp.concatenate(tiles + grad_values + [blank], 1).astype(BF16)
    grad_proj_ref[...] = grad_proj
    grad_one = dot_t(grad_proj, mat_ref[:, :QKV_PAD]).astype(BF16)
    grad_one = dot_t(grad_one, spread)
    stream = jnp.where(first, own_ref[0].astype(F32), got_ref[...].astype(F32))
    through, gain = scaled_backward(stream, gains_ref[0:1], grad_one)
    grad_in_ref[...] = (grad_middle + through).astype(BF16)
    gain_ref[...] = gain


def attend_backward(flags, grad, inputs, got, heads, masks, spread, mat, gains, cosine, sine):
    length = grad.shape[0]
    wide = N_DP * PAD
    return pl.pallas_call(
        attend_backward_kernel,
        grid_spec=pltpu.PrefetchScalarGridSpec(
            num_scalar_prefetch=1,
            grid=(1,),
            in_specs=[
                whole(length, D),
                pl.BlockSpec((1, length, D), lambda i, flag: (flag[1], 0, 0)),
                whole(length, D),
                whole(length, QKV_PAD),
                whole(length, QKV_PAD),
                pl.BlockSpec((1, length, length), lambda i, flag: (flag[1], 0, 0)),
                whole(D, wide),
                whole(wide, QKV_PAD + OUT_PAD),
                whole(2, D),
                whole(length, LANES),
                whole(length, LANES),
            ],
            out_specs=[
                whole(length, QKV_PAD),
                whole(length, OUT_PAD),
                whole(length, D),
                whole(1, D),
            ],
        ),
        out_shape=[
            jax.ShapeDtypeStruct((length, QKV_PAD), BF16),
            jax.ShapeDtypeStruct((length, OUT_PAD), BF16),
            jax.ShapeDtypeStruct((length, D), BF16),
            jax.ShapeDtypeStruct((1, D), F32),
        ],
        compiler_params=params(),
        cost_estimate=pl.CostEstimate(
            flops=2 * length * wide * 6700, bytes_accessed=9000000, transcendentals=H * length * length
        ),
    )(flags, grad, inputs, got, *heads, masks, spread, mat, gains, cosine, sine)


def as_blocks(rows):
    return rows.reshape(N_DP // 2, -1, rows.shape[-1])


def per_device(
    inputs, segment_ids, qkv_weight, out_weight, gate_up_weight, down_weight, norm_gains, cotangent
):
    batches = inputs.shape[0]
    is_first = lax.axis_index("section") == 0
    order = block_order()
    spread = placement(order)
    attn_shard = jnp.concatenate(
        [
            qkv_weight[0],
            norm_gains[0],
            jnp.zeros((ROWS, QKV_PAD - QKV - 2), BF16),
            out_weight[0],
            jnp.zeros((ROWS, OUT_PAD - D), BF16),
        ],
        1,
    )
    widths = (QKV_PAD + OUT_PAD, 2 * FF)
    down_shard = jnp.pad(down_weight[0], ((0, 0), (0, OUT_PAD - D))).reshape(PAD, -1)
    rows = jnp.concatenate(
        [
            jnp.pad(attn_shard, ((0, 1), (0, 0))),
            jnp.pad(gate_up_weight[0], ((0, 1), (0, 0))),
            down_shard,
        ],
        1,
    )
    near = gather_near(rows)
    near_attn = near[:, :, : widths[0]]
    near_gate_up = near[:, :, widths[0] : widths[0] + widths[1]]
    near_down = near[:, :, widths[0] + widths[1] :].reshape(8, FROWS, OUT_PAD)[:, :, :D]
    signal, attn_mat = gather_far(near_attn)
    signal, gate_up_mat = gather_far(after(near_gate_up, signal))
    signal, down_mat = gather_far(after(near_down, signal))
    attn_mat = attn_mat.reshape(N_DP * PAD, -1)
    gate_up_mat = gate_up_mat.reshape(N_DP * PAD, -1)
    down_mat = reorder(down_mat, order, True).reshape(FF, D)
    gains_full = lax.dot_general(
        attn_mat[:, QKV : QKV + 2], spread, (((0,), (1,)), ((), ())), preferred_element_type=F32
    )
    length = inputs.shape[1]
    cosine, sine = rope_tables(length)
    positions = jnp.arange(length)
    masks = (
        (segment_ids[:, :, None] == segment_ids[:, None, :])
        & (positions[:, None] >= positions[None, :])[None]
    ).astype(F32)
    first = is_first.astype(jnp.int32)

    def flags(for_first, for_second):
        return jnp.stack([first, jnp.where(is_first, for_first, for_second)])

    received = jnp.zeros(inputs.shape[1:], BF16)
    saved = []
    produced = []
    arrivals = []
    for turn in range(batches + 1):
        arrivals.append(received)
        hidden, heads, mixed, middle, second = attend_forward(
            flags(min(turn, batches - 1), max(turn - 1, 0)),
            inputs, received, masks, spread, attn_mat, gains_full, cosine, sine,
        )
        gate, up, act, layer_out = mlp_forward(second, middle, gate_up_mat, down_mat)
        saved.append((hidden, heads, mixed, middle, second, gate, up, act))
        produced.append(layer_out)
        if turn < batches:
            received = shifted(layer_out, "section", 1)
    section_outputs = jnp.stack(
        [
            jnp.where(is_first, produced[position], produced[position + 1])
            for position in range(batches)
        ]
    )[None]
    received = jnp.zeros(inputs.shape[1:], BF16)
    places = jnp.sum(
        jnp.where(order[:, None] == jnp.arange(N_DP)[None, :], jnp.arange(N_DP)[:, None], 0), 0
    ).astype(jnp.int32)

    def lefts(member):
        return jnp.concatenate(
            [jnp.where(is_first, saved[b][member], saved[b + 1][member]) for b in range(batches)], 0
        )

    def rights(turns):
        return jnp.concatenate(
            [jnp.where(is_first, turns[b + 1], turns[b]) for b in range(batches)], 0
        )

    returned = []
    downs = []
    gates = []
    ups = []
    projs = []
    attns = []
    gain_sum = 0
    flows = {}
    gate_up_own = []
    attn_own = []
    for turn in range(batches + 1):
        last = turn == batches
        if turn < batches:
            own_grad = cotangent[turn]
        else:
            own_grad = jnp.zeros(inputs.shape[1:], BF16)
        grad_out = jnp.where(is_first, received, own_grad)
        downs.append(grad_out)
        if last:
            blocks = down_sums(lefts(7), rights(downs), places)
            grad_out = after(grad_out, blocks)
            flows["down"] = Flow(
                down_scatter(blocks[N_DP // 2 :], lambda: blocks[: N_DP // 2])
            )
        kept_first, kept_second = saved[max(turn - 1, 0)], saved[min(turn + 1, batches)]
        chosen = flags(max(turn - 1, 0), min(turn, batches - 1))

        def both(member):
            return (kept_first[member], kept_second[member])

        grad_gate, grad_up, grad_middle, gain_two = mlp_backward(
            chosen, grad_out, both(3), both(5), both(6), gate_up_mat, down_mat, spread, gains_full
        )
        gates.append(grad_gate)
        ups.append(grad_up)
        if last:
            terms = (lefts(4), rights(gates), rights(ups))
            other = gate_up_sums(*terms, 1)
            other = step([flows["down"]], other)
            flows["gate_up"] = Flow(
                far_scatter(as_blocks(other), lambda: as_blocks(gate_up_own[0]))
            )
            gate_up_own.append(gate_up_sums(*after(terms, other), 0))
            grad_middle = after(grad_middle, gate_up_own[0])
        grad_proj, grad_attn, grad_in, gain_one = attend_backward(
            chosen, grad_middle, inputs, arrivals[min(turn + 1, batches)], both(1), masks, spread,
            attn_mat, gains_full, cosine, sine,
        )
        if last:
            grad_proj = step([flows["down"], flows["gate_up"]], grad_proj)
        projs.append(grad_proj)
        attns.append(grad_attn)
        gain_sum = gain_sum + jnp.concatenate([gain_one, gain_two], 0)
        returned.append(grad_in)
        if turn < batches:
            received = shifted(grad_in, "section", -1)
    section_input_grads = jnp.stack(
        [
            jnp.where(is_first, returned[position + 1], returned[position])
            for position in range(batches)
        ]
    )[None]
    gain_high = gain_sum.astype(BF16)
    gain_low = (gain_sum - gain_high.astype(F32)).astype(BF16)
    gain_rows = lax.dot_general(
        spread, jnp.stack([gain_high, gain_low]), (((0,), (2,)), ((), ())), preferred_element_type=F32
    )
    first_lane = QKV - (QKV_PAD - LANES)
    gain_rows = jnp.pad(
        gain_rows[:, 0] + gain_rows[:, 1], ((0, 0), (first_lane, LANES - first_lane - 2))
    )
    terms = (lefts(0), lefts(2), rights(projs), rights(attns), gain_rows)
    other = attn_sums(*terms, 1)
    flows["attn"] = Flow(far_scatter(as_blocks(other), lambda: as_blocks(attn_own[0])))
    attn_own.append(attn_sums(*after(terms, other), 0))
    down_flow, gate_up_flow, attn_flow = flows["down"], flows["gate_up"], flows["attn"]
    waiting = attn_own[0]
    while attn_flow.result is None or gate_up_flow.result is None:
        waiting = step([down_flow, gate_up_flow, attn_flow], waiting)
    near_flow = Flow(near_scatter(jnp.concatenate([attn_flow.result, gate_up_flow.result], -1)))
    while near_flow.result is None or down_flow.result is None:
        waiting = step([down_flow, near_flow], waiting)
    down_grad = down_flow.result
    attn_grad = near_flow.result[:, : QKV_PAD + OUT_PAD]
    gate_up_grad = near_flow.result[:, QKV_PAD + OUT_PAD :]
    return (
        section_outputs,
        section_input_grads,
        attn_grad[None, :ROWS, :QKV],
        attn_grad[None, :ROWS, QKV_PAD : QKV_PAD + D],
        gate_up_grad[None, :ROWS],
        down_grad[None],
        attn_grad[None, :ROWS, QKV : QKV + 2],
    )


def solution(mesh):
    in_specs = (
        P(None, "dp", None),
        P(None, "dp"),
        P("section", "dp", None),
        P("section", "dp", None),
        P("section", "dp", None),
        P("section", "dp", None),
        P("section", "dp", None),
        P(None, "dp", None),
    )
    out_specs = (
        P("section", None, "dp", None),
        P("section", None, "dp", None),
        P("section", "dp", None),
        P("section", "dp", None),
        P("section", "dp", None),
        P("section", "dp", None),
        P("section", "dp", None),
    )
    return jax.shard_map(
        per_device, mesh=mesh, in_specs=in_specs, out_specs=out_specs, check_vma=False
    )
```

time: 543 us -> 421 us (0.78); the launches traced: 533 us -> 417 us
  matrix products: 157 us -> 2.62 us
  Pallas kernels: 2.4 us -> 129 us
  local copies, waits for them, and re-layouts: 96.9 us -> 62.5 us
  waiting for transfers between devices: 121 us -> 94.7 us
  other arithmetic: 54.7 us -> 36.2 us
  starting transfers between devices: 96.2 us -> 90.4 us
    dot_general x61 -> x0, matrix products: 156 us -> none  [the longest x12 65.8 us: dot_t(): lax.dot_general(left, right, (((1,), (1,)), ((), ())), preferred_element_...]
    pallas_call x0 -> x17, Pallas kernels: none -> 127 us  [the longest x3 38.4 us: mlp_backward(): pl.pallas_call(mlp_backward_kernel, grid_spec=pltpu.PrefetchScalarGridSpe...]
    concatenate x9 -> x6, local copies, waits for them, and re-layouts: 29.7 us -> 5.12 us  [the longest x3 2.62 us: gather_far(): return (pieces[2], jnp.concatenate(pieces + others, 0))]
    ppermute x72 -> x51, waiting for transfers between devices: 103 us -> 83.8 us  [send(): return lax.ppermute(block, 'dp', route(kind, step))]
    ppermute x72 -> x51, starting transfers between devices: 81.8 us -> 64.1 us  [send(): return lax.ppermute(block, 'dp', route(kind, step))]
    slice x21 -> x8, local copies, waits for them, and re-layouts: 21.4 us -> 7.6 us  [the longest x1 2.52 us: per_device(): near_attn = near[:, :, :widths[0]]]
    ppermute x4, starting transfers between devices: 14.4 us -> 26.4 us  [shifted(): return lax.ppermute(block, axis, pairs)]
    convert_element_type x2 -> x0, local copies, waits for them, and re-layouts: 11.4 us -> none  [the longest x1 7.83 us: contract(): return lax.dot_general(left_rows, right_rows, (((0,), (0,)), ((), ())), p...]
  transfers between devices with their start and end apart: 76 -> 55, of which waited for: 30 -> 21; matrix products, arithmetic and copies ran while one was open for 22% -> 17% of each run, Pallas kernels for 0% -> 19%
where the time goes in v2:
time: 421 us; the launch traced here: 417 us
  Pallas kernels  129 us (31%)
  waiting for transfers between devices  94.7 us (22%)
  starting transfers between devices  90.4 us (21%)
  local copies, waits for them, and re-layouts  62.5 us (15%)
  other arithmetic  36.2 us (9%)
    ppermute x51, waiting for transfers between devices, send(): return lax.ppermute(block, 'dp', route(kind, step))  83.8 us
    ppermute x51, starting transfers between devices, send(): return lax.ppermute(block, 'dp', route(kind, step))  64.1 us
    pallas_call x3, Pallas kernels, mlp_backward(): pl.pallas_call(mlp_backward_kernel, grid_spec=pltpu.PrefetchScalarGridSpe...  38.4 us
    unnamed x161, local copies, waits for them, and re-layouts  36.7 us
    pallas_call x3, Pallas kernels, attend_backward(): pl.pallas_call(attend_backward_kernel, grid_spec=pltpu.PrefetchScalarGrid...  27.8 us
    ppermute x4, starting transfers between devices, shifted(): return lax.ppermute(block, axis, pairs)  26.4 us
    pallas_call x3, Pallas kernels, mlp_forward(): pl.pallas_call(mlp_forward_kernel, grid=(PARTS,), in_specs=[whole(length,...  25.3 us
    pallas_call x3, Pallas kernels, attend_forward(): pl.pallas_call(attend_forward_kernel, grid_spec=pltpu.PrefetchScalarGridS...  19.5 us
  transfers between devices with their start and end apart: 55, of which 21 were waited for; matrix products, arithmetic and copies ran while one was open for 17% of the time, Pallas kernels for 19%

profile of v2, /device:TPU:0, one launch (start us, length us, event | category | flops | bytes accessed | tf_op | source)
XLA Modules:
  0.0 417.5 jit_solution(14404274313679295015)
XLA Ops:
  9.5 5.0 %collective-permute-done = bf16[16,10368]{1,0:T(8,128)(2,1)S(1)} collective-permute-done((bf16[16,10368]{1,0:T(8,128)(2,1)S(1)}, bf16[16,10368]{1,0:T(8,128)(2,1)S(1)}, u32[]{:S(2)}, u32[]{:S(2)}) %collective-permute-start) | collective-permute-done | bytes 331808 | tf_op jit(solution)/shard_map/ppermute | solution.py:49
  14.5 1.9 collective-permute-start.2
  18.7 7.8 %collective-permute-done.2 = bf16[2,16,10368]{2,1,0:T(8,128)(2,1)S(1)} collective-permute-done((bf16[2,16,10368]{2,1,0:T(8,128)(2,1)S(1)}, bf16[2,16,10368]{2,1,0:T(8,128)(2,1)S(1)}, u32[]{:S(2)}, u32[]{:S(2)}) %collective-permute-start.2) | collective-permute-done | bytes 663584 | tf_op jit(solution)/shard_map/ppermute | solution.py:49
  27.2 2.7 collective-permute-start.4
  31.7 3.2 collective-permute-done.3
  36.4 2.5 fusion.59
  39.0 2.1 collective-permute-start.6
  41.1 2.1 collective-permute-start.5
  47.1 2.4 reshape.481
  49.5 3.0 collective-permute-done.6
  54.6 3.3 collective-permute-start.8
  59.4 2.1 constant_dynamic-update-slice_fusion.14
  61.5 2.0 constant_dynamic-update-slice_fusion.13
  65.6 3.2 collective-permute-start.12
  68.8 2.0 constant_dynamic-update-slice_fusion.10
  73.2 11.2 %collective-permute-done.13 = bf16[8,16,5120]{2,1,0:T(8,128)(2,1)S(1)} collective-permute-done((bf16[8,16,5120]{2,1,0:T(8,128)(2,1)S(1)}, bf16[8,16,5120]{2,1,0:T(8,128)(2,1)S(1)}, u32[]{:S(2)}, u32[]{:S(2)}) %collective-permute-start.13) | collective-permute-done | bytes 1310752 | tf_op jit(solution)/shard_map/ppermute | solution.py:49
  84.6 3.3 collective-permute-start.15
  90.6 5.8 %collective-permute-done.14 = bf16[4,16,5120]{2,1,0:T(8,128)(2,1)S(1)} collective-permute-done((bf16[4,16,5120]{2,1,0:T(8,128)(2,1)S(1)}, bf16[4,16,5120]{2,1,0:T(8,128)(2,1)S(1)}, u32[]{:S(2)}, u32[]{:S(2)}) %collective-permute-start.14) | collective-permute-done | bytes 655392 | tf_op jit(solution)/shard_map/ppermute | solution.py:49
  98.3 3.5 collective-permute-start.19
  104.6 6.5 %shard_map.135 = (bf16[128,1024]{1,0:T(8,128)(2,1)S(1)}, bf16[128,1664]{1,0:T(8,128)(2,1)S(1)}, bf16[128,1024]{1,0:T(8,128)(2,1)S(1)}, f32[128,960]{1,0:T(8,128)S(1)}, bf16[128,1024]{1,0:T(8,128)(2,1)S(1)}) custom-call(s32[2]{0:T(128)S(1)} %pad_add_fusion.flag_ref, bf16[2,128,960]{2,1,0:T(8,128)(2,1)S(1)} %copy.56.own_ref, ...), custom_call_target="tpu_custom_call" | custom-call | flops 1494220800 | bytes 8000000 | tf_op jit(solution)/shard_map/pallas_call | solution.py:382
  111.4 3.3 collective-permute-start.22
  116.3 3.3 collective-permute-done.21
  120.5 3.0 collective-permute-done.25
  128.3 8.7 %shard_map.137 = (f32[128,2560]{1,0:T(8,128)S(1)}, f32[128,2560]{1,0:T(8,128)S(1)}, bf16[128,2560]{1,0:T(8,128)(2,1)S(1)}, bf16[128,960]{1,0:T(8,128)(2,1)}) custom-call(bf16[128,1024]{1,0:T(8,128)(2,1)S(1)} %get-tuple-element.96.second_ref, f32[128,960]{1,0:T(8,128)S(1)} %get-tuple-element.97.middle_ref.middle_a_ref, ...), custom_call_target="tpu_custom_call" | custom-call | flops 2013265920 | bytes 20000000 | tf_op jit(solution)/shard_map/pallas_call | solution.py:439
  140.1 5.6 %collective-permute-start.26 = (bf16[128,960]{1,0:T(8,128)(2,1)}, bf16[128,960]{1,0:T(8,128)(2,1)}, u32[]{:S(2)}, u32[]{:S(2)}) collective-permute-start(bf16[128,960]{1,0:T(8,128)(2,1)} %get-tuple-element.100), channel_id=1, source_target_pairs={{0,64},{1,65},{2,66},{3,67},{4,68},{5,69},{6,70},{7,71},{8,72},{9,... | collective-permute-start | bytes 737288 | tf_op jit(solution)/shard_map/ppermute | solution.py:283
  151.8 6.6 %shard_map.138 = (bf16[128,1024]{1,0:T(8,128)(2,1)S(1)}, bf16[128,1664]{1,0:T(8,128)(2,1)S(1)}, bf16[128,1024]{1,0:T(8,128)(2,1)S(1)}, f32[128,960]{1,0:T(8,128)S(1)}, bf16[128,1024]{1,0:T(8,128)(2,1)S(1)}) custom-call(s32[2]{0:T(128)S(1)} %copy-done.50, bf16[2,128,960]{2,1,0:T(8,128)(2,1)S(1)} %copy.56.own_ref, ...), custom_call_target="tpu_custom_call" | custom-call | flops 1494220800 | bytes 8000000 | tf_op jit(solution)/shard_map/pallas_call | solution.py:382
  158.4 8.5 %shard_map.139 = (f32[128,2560]{1,0:T(8,128)S(1)}, f32[128,2560]{1,0:T(8,128)S(1)}, bf16[128,2560]{1,0:T(8,128)(2,1)S(1)}, bf16[128,960]{1,0:T(8,128)(2,1)S(1)}) custom-call(bf16[128,1024]{1,0:T(8,128)(2,1)S(1)} %get-tuple-element.101.second_ref, f32[128,960]{1,0:T(8,128)S(1)} %get-tuple-element.102.middle_ref.middle_b_ref.middle_a_ref, ...), custom_call_target="tpu_custom_call" | custom-call | flops 2013265920 | bytes 20000000 | tf_op jit(solution)/shard_map/pallas_call | solution.py:439
  168.0 18.1 %collective-permute-start.27 = (bf16[128,960]{1,0:T(8,128)(2,1)S(1)}, bf16[128,960]{1,0:T(8,128)(2,1)S(1)}, u32[]{:S(2)}, u32[]{:S(2)}) collective-permute-start(bf16[128,960]{1,0:T(8,128)(2,1)S(1)} %get-tuple-element.103), channel_id=1, source_target_pairs={{0,64},{1,65},{2,66},{3,67},{4,68},{5,69},{6,70},{7,71},{8,72},{9,... | collective-permute-start | bytes 737288 | tf_op jit(solution)/shard_map/ppermute | solution.py:283
  186.2 13.0 %shard_map.142 = (bf16[128,2560]{1,0:T(8,128)(2,1)S(1)}, bf16[128,2560]{1,0:T(8,128)(2,1)S(1)}, f32[128,960]{1,0:T(8,128)S(1)}, f32[1,960]{1,0:T(1,128)S(1)}) custom-call(s32[2]{0:T(128)S(1)} %pad_add_fusion.flag_ref, bf16[128,960]{1,0:T(8,128)(2,1)S(1)} %select_bitcast_fusion.2.grad_ref, f32[128,960]{1,0:T(8,128)S(1)} %get-tuple-element.97.middle_ref.middle_a_ref, ...), custom_call_target="tpu_custom_call" | custom-call | flops 2013265920 | bytes 22000000 | tf_op jit(solution)/shard_map/pallas_call | solution.py:509
  199.3 9.4 %shard_map.143 = (bf16[128,1664]{1,0:T(8,128)(2,1)S(1)}, bf16[128,1024]{1,0:T(8,128)(2,1)S(1)}, bf16[128,960]{1,0:T(8,128)(2,1)S(1)}, f32[1,960]{1,0:T(1,128)S(1)}) custom-call(s32[2]{0:T(128)S(1)} %pad_add_fusion.flag_ref, f32[128,960]{1,0:T(8,128)S(1)} %get-tuple-element.111.grad_ref, bf16[2,128,960]{2,1,0:T(8,128)(2,1)S(1)} %copy.56.own_ref, ...), custom_call_target="tpu_custom_call" | custom-call | flops 1756364800 | bytes 9000000 | tf_op jit(solution)/shard_map/pallas_call | solution.py:594
  210.7 6.5 %shard_map.140 = (bf16[128,1024]{1,0:T(8,128)(2,1)S(1)}, bf16[128,1664]{1,0:T(8,128)(2,1)S(1)}, bf16[128,1024]{1,0:T(8,128)(2,1)S(1)}, f32[128,960]{1,0:T(8,128)S(1)}, bf16[128,1024]{1,0:T(8,128)(2,1)S(1)}) custom-call(s32[2]{0:T(128)S(1)} %pad_add_fusion.2.flag_ref, bf16[2,128,960]{2,1,0:T(8,128)(2,1)S(1)} %copy.56.own_ref, ...), custom_call_target="tpu_custom_call" | custom-call | flops 1494220800 | bytes 8000000 | tf_op jit(solution)/shard_map/pallas_call | solution.py:382
  218.6 8.1 %shard_map.141 = (f32[128,2560]{1,0:T(8,128)S(1)}, f32[128,2560]{1,0:T(8,128)S(1)}, bf16[128,2560]{1,0:T(8,128)(2,1)S(1)}, bf16[128,960]{1,0:T(8,128)(2,1)S(1)}) custom-call(bf16[128,1024]{1,0:T(8,128)(2,1)S(1)} %get-tuple-element.104.second_ref, f32[128,960]{1,0:T(8,128)S(1)} %get-tuple-element.105.middle_ref.middle_b_ref, ...), custom_call_target="tpu_custom_call" | custom-call | flops 2013265920 | bytes 20000000 | tf_op jit(solution)/shard_map/pallas_call | solution.py:439
  228.4 13.1 %shard_map.144 = (bf16[128,2560]{1,0:T(8,128)(2,1)S(1)}, bf16[128,2560]{1,0:T(8,128)(2,1)S(1)}, f32[128,960]{1,0:T(8,128)S(1)}, f32[1,960]{1,0:T(1,128)S(1)}) custom-call(s32[2]{0:T(128)S(1)} %copy-done.48, bf16[128,960]{1,0:T(8,128)(2,1)S(1)} %get-tuple-element.209.grad_ref, f32[128,960]{1,0:T(8,128)S(1)} %get-tuple-element.97.middle_ref.middle_a_ref, ...), custom_call_target="tpu_custom_call" | custom-call | flops 2013265920 | bytes 22000000 | tf_op jit(solution)/shard_map/pallas_call | solution.py:509
  243.2 9.2 %shard_map.145 = (bf16[128,1664]{1,0:T(8,128)(2,1)S(1)}, bf16[128,1024]{1,0:T(8,128)(2,1)S(1)}, bf16[128,960]{1,0:T(8,128)(2,1)S(1)}, f32[1,960]{1,0:T(1,128)S(1)}) custom-call(s32[2]{0:T(128)S(1)} %copy-done.48, f32[128,960]{1,0:T(8,128)S(1)} %get-tuple-element.117.grad_ref, bf16[2,128,960]{2,1,0:T(8,128)(2,1)S(1)} %copy.56.own_ref, ...), custom_call_target="tpu_custom_call" | custom-call | flops 1756364800 | bytes 9000000 | tf_op jit(solution)/shard_map/pallas_call | solution.py:594
  254.1 9.1 %collective-permute-done.29 = bf16[128,960]{1,0:T(8,128)(2,1)S(1)} collective-permute-done((bf16[128,960]{1,0:T(8,128)(2,1)S(1)}, bf16[128,960]{1,0:T(8,128)(2,1)S(1)}, u32[]{:S(2)}, u32[]{:S(2)}) %collective-permute-start.29) | collective-permute-done | bytes 245792 | tf_op jit(solution)/shard_map/ppermute | solution.py:283
  263.3 5.1 %shard_map.146 = bf16[64,40,960]{2,1,0:T(8,128)(2,1)} custom-call(s32[64]{0:T(128)S(1)} %copy-done.49, bf16[256,2560]{1,0:T(8,128)(2,1)S(1)} %pad_maximum_fusion.4.left_ref, bf16[256,960]{1,0:T(8,128)(2,1)S(1)} %pad_maximum_fusion.16.right_ref), custom_call_target="tpu_custom_call" | custom-call | flops 1258291200 | bytes 4915200 | tf_op jit(solution)/shard_map/pallas_call | solution.py:195
  268.4 2.0 slice.272
  271.1 12.3 %shard_map.147 = (bf16[128,2560]{1,0:T(8,128)(2,1)S(1)}, bf16[128,2560]{1,0:T(8,128)(2,1)S(1)}, f32[128,960]{1,0:T(8,128)S(1)}, f32[1,960]{1,0:T(1,128)S(1)}) custom-call(s32[2]{0:T(128)S(1)} %pad_add_fusion.2.flag_ref, bf16[128,960]{1,0:T(8,128)(2,1)S(1)} %get-tuple-element.123.grad_ref, ...), custom_call_target="tpu_custom_call" | custom-call | flops 2013265920 | bytes 22000000 | tf_op jit(solution)/shard_map/pallas_call | solution.py:509
  283.9 4.0 shard_map.148
  288.6 3.8 add_convert_fusion
  294.6 3.8 shard_map.149
  298.4 9.2 %shard_map.150 = (bf16[128,1664]{1,0:T(8,128)(2,1)S(1)}, bf16[128,1024]{1,0:T(8,128)(2,1)S(1)}, bf16[128,960]{1,0:T(8,128)(2,1)S(1)}, f32[1,960]{1,0:T(1,128)S(1)}) custom-call(s32[2]{0:T(128)S(1)} %pad_add_fusion.2.flag_ref, f32[128,960]{1,0:T(8,128)S(1)} %get-tuple-element.135.grad_ref, bf16[2,128,960]{2,1,0:T(8,128)(2,1)S(1)} %copy.56.own_ref, ...), custom_call_target="tpu_custom_call" | custom-call | flops 1756364800 | bytes 9000000 | tf_op jit(solution)/shard_map/pallas_call | solution.py:594
  312.7 8.5 %fusion = bf16[32,16,5120]{2,1,0:T(8,128)(2,1)} fusion(bf16[32,16,5120]{2,1,0:T(8,128)(2,1)} %bitcast.184, bf16[32,16,5120]{2,1,0:T(8,128)(2,1)} %collective-permute-done.33), kind=kLoop, calls=%fused_computation.1 | loop fusion | flops 10485760 | bytes 15728640 | tf_op jit(solution)/shard_map/convert_element_type | solution.py:77
  321.1 1.9 slice_bitcast_fusion.1
  323.0 2.9 collective-permute-start.37
  326.9 3.2 collective-permute-start.35
  331.9 9.3 %collective-permute-done.35 = bf16[8,40,960]{2,1,0:T(8,128)(2,1)S(1)} collective-permute-done((bf16[8,40,960]{2,1,0:T(8,128)(2,1)}, bf16[8,40,960]{2,1,0:T(8,128)(2,1)S(1)}, u32[]{:S(2)}, u32[]{:S(2)}) %collective-permute-start.35) | collective-permute-done | bytes 614432 | tf_op jit(solution)/shard_map/ppermute | solution.py:49
  341.2 2.0 fusion.10
  344.9 2.3 collective-permute-start.42
  347.9 2.1 collective-permute-start.44
  351.5 2.7 collective-permute-start.40
  354.2 2.9 collective-permute-done.40
  358.1 6.0 %collective-permute-done.39 = bf16[1,40,960]{2,1,0:T(8,128)(2,1)S(1)} collective-permute-done((bf16[1,40,960]{2,1,0:T(8,128)(2,1)S(1)}, bf16[1,40,960]{2,1,0:T(8,128)(2,1)S(1)}, u32[]{:S(2)}, u32[]{:S(2)}) %collective-permute-start.39) | collective-permute-done | bytes 76832 | tf_op jit(solution)/shard_map/ppermute | solution.py:49
  364.1 3.0 collective-permute-done.44
  367.7 3.0 collective-permute-start.46
  370.9 2.1 collective-permute-start.47
  374.6 1.9 add_convert_fusion.1
  376.5 6.8 %collective-permute-done.47 = bf16[8,16,2688]{2,1,0:T(8,128)(2,1)S(1)} collective-permute-done((bf16[8,16,2688]{2,1,0:T(8,128)(2,1)S(1)}, bf16[8,16,2688]{2,1,0:T(8,128)(2,1)S(1)}, u32[]{:S(2)}, u32[]{:S(2)}) %collective-permute-start.47) | collective-permute-done | bytes 688160 | tf_op jit(solution)/shard_map/ppermute | solution.py:49
  387.6 3.8 collective-permute-done.49
  391.4 2.2 collective-permute-done.50
  395.5 3.2 collective-permute-start.53
  400.6 2.0 copy.79
  402.6 2.4 collective-permute-done.52
  409.4 3.8 collective-permute-done.54
  (345 shorter events, 95.6 us)
Async XLA Ops:
  5.1 9.4 %collective-permute-start = (bf16[16,10368]{1,0:T(8,128)(2,1)S(1)}, bf16[16,10368]{1,0:T(8,128)(2,1)S(1)}, u32[]{:S(2)}, u32[]{:S(2)}) collective-permute-start(bf16[16,10368]{1,0:T(8,128)(2,1)S(1)} %get-tuple-element.211), channel_id=1, source_target_pairs={{0,8},{1,9},{2,10},{3,11},{4,12},{5,13},{6,14},{7,15},{8,0},{9,1},... | collective-permute-start | bytes 995336 | tf_op jit(solution)/shard_map/ppermute | solution.py:49
  14.5 12.0 %collective-permute-start.2 = (bf16[2,16,10368]{2,1,0:T(8,128)(2,1)S(1)}, bf16[2,16,10368]{2,1,0:T(8,128)(2,1)S(1)}, u32[]{:S(2)}, u32[]{:S(2)}) collective-permute-start(bf16[2,16,10368]{2,1,0:T(8,128)(2,1)S(1)} %pad_maximum_fusion.12), channel_id=1, source_target_pairs={{0,16},{1,3},{2,18},{3,5},{4,20},{5,7},{6,22},{7,1},{8,24},{9,11},... | collective-permute-start | bytes 1990664 | tf_op jit(solution)/shard_map/ppermute | solution.py:49
  16.4 10.8 %collective-permute-start.1 = (bf16[2,16,10368]{2,1,0:T(8,128)(2,1)S(1)}, bf16[2,16,10368]{2,1,0:T(8,128)(2,1)S(1)}, u32[]{:S(2)}, u32[]{:S(2)}) collective-permute-start(bf16[2,16,10368]{2,1,0:T(8,128)(2,1)S(1)} %pad_maximum_fusion.12), channel_id=1, source_target_pairs={{0,48},{1,7},{2,50},{3,1},{4,52},{5,3},{6,54},{7,5},{8,56},{9,15},... | collective-permute-start | bytes 1990664 | tf_op jit(solution)/shard_map/ppermute | solution.py:49
  26.5 8.4 %collective-permute-start.3 = (bf16[1,16,10368]{2,1,0:T(8,128)(2,1)S(1)}, bf16[1,16,10368]{2,1,0:T(8,128)(2,1)S(1)}, u32[]{:S(2)}, u32[]{:S(2)}) collective-permute-start(bf16[1,16,10368]{2,1,0:T(8,128)(2,1)S(1)} %slice.259), channel_id=1, source_target_pairs={{0,16},{1,3},{2,18},{3,5},{4,20},{5,7},{6,22},{7,1},{8,24},{9,11},... | collective-permute-start | bytes 995336 | tf_op jit(solution)/shard_map/ppermute | solution.py:49
  27.2 8.5 %collective-permute-start.4 = (bf16[1,16,10368]{2,1,0:T(8,128)(2,1)S(1)}, bf16[1,16,10368]{2,1,0:T(8,128)(2,1)S(1)}, u32[]{:S(2)}, u32[]{:S(2)}) collective-permute-start(bf16[1,16,10368]{2,1,0:T(8,128)(2,1)S(1)} %slice.260), channel_id=1, source_target_pairs={{0,48},{1,7},{2,50},{3,1},{4,52},{5,3},{6,54},{7,5},{8,56},{9,15},... | collective-permute-start | bytes 995336 | tf_op jit(solution)/shard_map/ppermute | solution.py:49
  39.0 13.5 %collective-permute-start.6 = (bf16[8,16,2688]{2,1,0:T(8,128)(2,1)}, bf16[8,16,2688]{2,1,0:T(8,128)(2,1)}, u32[]{:S(2)}, u32[]{:S(2)}) collective-permute-start(bf16[8,16,2688]{2,1,0:T(8,128)(2,1)} %get-tuple-element.226), channel_id=1, source_target_pairs={{0,2},{1,17},{2,4},{3,19},{4,6},{5,21},{6,0},{7,23},{8,10},{9,25},... | collective-permute-start | bytes 2064392 | tf_op jit(solution)/shard_map/ppermute | solution.py:49
  41.1 12.4 %collective-permute-start.5 = (bf16[8,16,2688]{2,1,0:T(8,128)(2,1)}, bf16[8,16,2688]{2,1,0:T(8,128)(2,1)}, u32[]{:S(2)}, u32[]{:S(2)}) collective-permute-start(bf16[8,16,2688]{2,1,0:T(8,128)(2,1)} %get-tuple-element.226), channel_id=1, source_target_pairs={{0,6},{1,49},{2,0},{3,51},{4,2},{5,53},{6,4},{7,55},{8,14},{9,57},... | collective-permute-start | bytes 2064392 | tf_op jit(solution)/shard_map/ppermute | solution.py:49
  43.2 59.5 %copy-start.64 = (s32[1024]{0:T(1024)}, s32[1024]{0:T(1024)S(1)}, u32[]{:S(2)}) copy-start(s32[1024]{0:T(1024)S(1)} %add_select_fusion.1) | copy-start | bytes 12292
  44.9 106.3 %copy-start.1 = (bf16[960,1024]{1,0:T(8,128)(2,1)}, bf16[960,1024]{1,0:T(8,128)(2,1)S(1)}, u32[]{:S(2)}) copy-start(bf16[960,1024]{1,0:T(8,128)(2,1)S(1)} %fusion.4.spread_ref) | copy-start | bytes 5898244
  47.1 18.5 %collective-permute-start.9 = (bf16[8,16,2688]{2,1,0:T(8,128)(2,1)}, bf16[8,16,2688]{2,1,0:T(8,128)(2,1)}, u32[]{:S(2)}, u32[]{:S(2)}) collective-permute-start(bf16[8,16,2688]{2,1,0:T(8,128)(2,1)} %get-tuple-element.226), channel_id=1, source_target_pairs={{0,1},{1,0},{2,3},{3,2},{4,5},{5,4},{6,7},{7,6},{8,9},{9,8},{10,11... | collective-permute-start | bytes 2064392 | tf_op jit(solution)/shard_map/ppermute | solution.py:49
  53.5 10.1 %collective-permute-start.7 = (bf16[4,16,2688]{2,1,0:T(8,128)(2,1)S(1)}, bf16[4,16,2688]{2,1,0:T(8,128)(2,1)S(1)}, u32[]{:S(2)}, u32[]{:S(2)}) collective-permute-start(bf16[4,16,2688]{2,1,0:T(8,128)(2,1)S(1)} %slice.262), channel_id=1, source_target_pairs={{0,2},{1,17},{2,4},{3,19},{4,6},{5,21},{6,0},{7,23},{8,10},{9,25},... | collective-permute-start | bytes 1032200 | tf_op jit(solution)/shard_map/ppermute | solution.py:49
  54.6 9.7 %collective-permute-start.8 = (bf16[4,16,2688]{2,1,0:T(8,128)(2,1)S(1)}, bf16[4,16,2688]{2,1,0:T(8,128)(2,1)S(1)}, u32[]{:S(2)}, u32[]{:S(2)}) collective-permute-start(bf16[4,16,2688]{2,1,0:T(8,128)(2,1)S(1)} %slice.263), channel_id=1, source_target_pairs={{0,6},{1,49},{2,0},{3,51},{4,2},{5,53},{6,4},{7,55},{8,14},{9,57},... | collective-permute-start | bytes 1032200 | tf_op jit(solution)/shard_map/ppermute | solution.py:49
  59.3 12.7 %collective-permute-start.10 = (bf16[16,16,2688]{2,1,0:T(8,128)(2,1)S(1)}, bf16[16,16,2688]{2,1,0:T(8,128)(2,1)S(1)}, u32[]{:S(2)}, u32[]{:S(2)}) collective-permute-start(bf16[16,16,2688]{2,1,0:T(8,128)(2,1)S(1)} %pad_maximum_fusion.2), channel_id=1, source_target_pairs={{0,1},{1,0},{2,3},{3,2},{4,5},{5,4},{6,7},{7,6},{8,9},{9,8},{10,11... | collective-permute-start | bytes 4128776 | tf_op jit(solution)/shard_map/ppermute | solution.py:49
  65.1 36.7 %collective-permute-start.11 = (bf16[8,16,2688]{2,1,0:T(8,128)(2,1)S(1)}, bf16[8,16,2688]{2,1,0:T(8,128)(2,1)S(1)}, u32[]{:S(2)}, u32[]{:S(2)}) collective-permute-start(bf16[8,16,2688]{2,1,0:T(8,128)(2,1)S(1)} %get-tuple-element.260), channel_id=1, source_target_pairs={{0,1},{1,0},{2,3},{3,2},{4,5},{5,4},{6,7},{7,6},{8,9},{9,8},{10,11... | collective-permute-start | bytes 2064392 | tf_op jit(solution)/shard_map/ppermute | solution.py:49
  65.5 49.3 %collective-permute-start.16 = (bf16[8,16,5120]{2,1,0:T(8,128)(2,1)S(1)}, bf16[8,16,5120]{2,1,0:T(8,128)(2,1)S(1)}, u32[]{:S(2)}, u32[]{:S(2)}) collective-permute-start(bf16[8,16,5120]{2,1,0:T(8,128)(2,1)S(1)} %copy-done.52), channel_id=1, source_target_pairs={{0,1},{1,0},{2,3},{3,2},{4,5},{5,4},{6,7},{7,6},{8,9},{9,8},{10,11... | collective-permute-start | bytes 3932168 | tf_op jit(solution)/shard_map/ppermute | solution.py:49
  65.6 18.8 %collective-permute-start.13 = (bf16[8,16,5120]{2,1,0:T(8,128)(2,1)S(1)}, bf16[8,16,5120]{2,1,0:T(8,128)(2,1)S(1)}, u32[]{:S(2)}, u32[]{:S(2)}) collective-permute-start(bf16[8,16,5120]{2,1,0:T(8,128)(2,1)S(1)} %copy-done.52), channel_id=1, source_target_pairs={{0,2},{1,17},{2,4},{3,19},{4,6},{5,21},{6,0},{7,23},{8,10},{9,25},... | collective-permute-start | bytes 3932168 | tf_op jit(solution)/shard_map/ppermute | solution.py:49
  65.6 18.9 %collective-permute-start.12 = (bf16[8,16,5120]{2,1,0:T(8,128)(2,1)S(1)}, bf16[8,16,5120]{2,1,0:T(8,128)(2,1)S(1)}, u32[]{:S(2)}, u32[]{:S(2)}) collective-permute-start(bf16[8,16,5120]{2,1,0:T(8,128)(2,1)S(1)} %copy-done.52), channel_id=1, source_target_pairs={{0,6},{1,49},{2,0},{3,51},{4,2},{5,53},{6,4},{7,55},{8,14},{9,57},... | collective-permute-start | bytes 3932168 | tf_op jit(solution)/shard_map/ppermute | solution.py:49
  84.5 11.9 %collective-permute-start.14 = (bf16[4,16,5120]{2,1,0:T(8,128)(2,1)S(1)}, bf16[4,16,5120]{2,1,0:T(8,128)(2,1)S(1)}, u32[]{:S(2)}, u32[]{:S(2)}) collective-permute-start(bf16[4,16,5120]{2,1,0:T(8,128)(2,1)S(1)} %slice.266), channel_id=1, source_target_pairs={{0,2},{1,17},{2,4},{3,19},{4,6},{5,21},{6,0},{7,23},{8,10},{9,25},... | collective-permute-start | bytes 1966088 | tf_op jit(solution)/shard_map/ppermute | solution.py:49
  84.6 12.7 %collective-permute-start.15 = (bf16[4,16,5120]{2,1,0:T(8,128)(2,1)S(1)}, bf16[4,16,5120]{2,1,0:T(8,128)(2,1)S(1)}, u32[]{:S(2)}, u32[]{:S(2)}) collective-permute-start(bf16[4,16,5120]{2,1,0:T(8,128)(2,1)S(1)} %slice.267), channel_id=1, source_target_pairs={{0,6},{1,49},{2,0},{3,51},{4,2},{5,53},{6,4},{7,55},{8,14},{9,57},... | collective-permute-start | bytes 1966088 | tf_op jit(solution)/shard_map/ppermute | solution.py:49
  88.1 36.7 %collective-permute-start.17 = (bf16[16,16,5120]{2,1,0:T(8,128)(2,1)S(1)}, bf16[16,16,5120]{2,1,0:T(8,128)(2,1)S(1)}, u32[]{:S(2)}, u32[]{:S(2)}) collective-permute-start(bf16[16,16,5120]{2,1,0:T(8,128)(2,1)S(1)} %pad_maximum_fusion), channel_id=1, source_target_pairs={{0,1},{1,0},{2,3},{3,2},{4,5},{5,4},{6,7},{7,6},{8,9},{9,8},{10,11... | collective-permute-start | bytes 7864328 | tf_op jit(solution)/shard_map/ppermute | solution.py:49
  98.3 12.9 %collective-permute-start.20 = (bf16[8,40,960]{2,1,0:T(8,128)(2,1)S(1)}, bf16[8,40,960]{2,1,0:T(8,128)(2,1)S(1)}, u32[]{:S(2)}, u32[]{:S(2)}) collective-permute-start(bf16[8,40,960]{2,1,0:T(8,128)(2,1)S(1)} %bitcast.194), channel_id=1, source_target_pairs={{0,2},{1,17},{2,4},{3,19},{4,6},{5,21},{6,0},{7,23},{8,10},{9,25},... | collective-permute-start | bytes 1843208 | tf_op jit(solution)/shard_map/ppermute | solution.py:49
  98.3 13.0 %collective-permute-start.19 = (bf16[8,40,960]{2,1,0:T(8,128)(2,1)S(1)}, bf16[8,40,960]{2,1,0:T(8,128)(2,1)S(1)}, u32[]{:S(2)}, u32[]{:S(2)}) collective-permute-start(bf16[8,40,960]{2,1,0:T(8,128)(2,1)S(1)} %bitcast.195), channel_id=1, source_target_pairs={{0,6},{1,49},{2,0},{3,51},{4,2},{5,53},{6,4},{7,55},{8,14},{9,57},... | collective-permute-start | bytes 1843208 | tf_op jit(solution)/shard_map/ppermute | solution.py:49
  111.1 9.3 %collective-permute-start.23 = (bf16[8,40,960]{2,1,0:T(8,128)(2,1)S(1)}, bf16[8,40,960]{2,1,0:T(8,128)(2,1)S(1)}, u32[]{:S(2)}, u32[]{:S(2)}) collective-permute-start(bf16[8,40,960]{2,1,0:T(8,128)(2,1)S(1)} %bitcast.196), channel_id=1, source_target_pairs={{0,1},{1,0},{2,3},{3,2},{4,5},{5,4},{6,7},{7,6},{8,9},{9,8},{10,11... | collective-permute-start | bytes 1843208 | tf_op jit(solution)/shard_map/ppermute | solution.py:49
  111.2 8.4 %collective-permute-start.21 = (bf16[4,40,960]{2,1,0:T(8,128)(2,1)S(1)}, bf16[4,40,960]{2,1,0:T(8,128)(2,1)S(1)}, u32[]{:S(2)}, u32[]{:S(2)}) collective-permute-start(bf16[4,40,960]{2,1,0:T(8,128)(2,1)S(1)} %slice.270), channel_id=1, source_target_pairs={{0,2},{1,17},{2,4},{3,19},{4,6},{5,21},{6,0},{7,23},{8,10},{9,25},... | collective-permute-start | bytes 921608 | tf_op jit(solution)/shard_map/ppermute | solution.py:49
  111.4 8.2 %collective-permute-start.22 = (bf16[4,40,960]{2,1,0:T(8,128)(2,1)S(1)}, bf16[4,40,960]{2,1,0:T(8,128)(2,1)S(1)}, u32[]{:S(2)}, u32[]{:S(2)}) collective-permute-start(bf16[4,40,960]{2,1,0:T(8,128)(2,1)S(1)} %slice.271), channel_id=1, source_target_pairs={{0,6},{1,49},{2,0},{3,51},{4,2},{5,53},{6,4},{7,55},{8,14},{9,57},... | collective-permute-start | bytes 921608 | tf_op jit(solution)/shard_map/ppermute | solution.py:49
  114.8 5.6 %collective-permute-start.24 = (bf16[16,40,960]{2,1,0:T(8,128)(2,1)S(1)}, bf16[16,40,960]{2,1,0:T(8,128)(2,1)S(1)}, u32[]{:S(2)}, u32[]{:S(2)}) collective-permute-start(bf16[16,40,960]{2,1,0:T(8,128)(2,1)S(1)} %pad_maximum_fusion.3), channel_id=1, source_target_pairs={{0,1},{1,0},{2,3},{3,2},{4,5},{5,4},{6,7},{7,6},{8,9},{9,8},{10,11... | collective-permute-start | bytes 3686408 | tf_op jit(solution)/shard_map/ppermute | solution.py:49
  119.6 7.1 %collective-permute-start.18 = (bf16[8,16,5120]{2,1,0:T(8,128)(2,1)S(1)}, bf16[8,16,5120]{2,1,0:T(8,128)(2,1)S(1)}, u32[]{:S(2)}, u32[]{:S(2)}) collective-permute-start(bf16[8,16,5120]{2,1,0:T(8,128)(2,1)S(1)} %copy-done.63), channel_id=1, source_target_pairs={{0,1},{1,0},{2,3},{3,2},{4,5},{5,4},{6,7},{7,6},{8,9},{9,8},{10,11... | collective-permute-start | bytes 3932168 | tf_op jit(solution)/shard_map/ppermute | solution.py:49
  119.7 3.9 collective-permute-start.25
  140.1 11.1 %collective-permute-start.26 = (bf16[128,960]{1,0:T(8,128)(2,1)}, bf16[128,960]{1,0:T(8,128)(2,1)}, u32[]{:S(2)}, u32[]{:S(2)}) collective-permute-start(bf16[128,960]{1,0:T(8,128)(2,1)} %get-tuple-element.100), channel_id=1, source_target_pairs={{0,64},{1,65},{2,66},{3,67},{4,68},{5,69},{6,70},{7,71},{8,72},{9,... | collective-permute-start | bytes 737288 | tf_op jit(solution)/shard_map/ppermute | solution.py:283
  158.4 40.9 %copy-start.10 = (bf16[128,1664]{1,0:T(8,128)(2,1)}, bf16[128,1664]{1,0:T(8,128)(2,1)S(1)}, u32[]{:S(2)}) copy-start(bf16[128,1664]{1,0:T(8,128)(2,1)S(1)} %get-tuple-element.113.heads_b_ref.heads_a_ref) | copy-start | bytes 1277956
  158.4 27.8 %copy-start.8 = (f32[128,2560]{1,0:T(8,128)S(1)}, f32[128,2560]{1,0:T(8,128)}, u32[]{:S(2)}) copy-start(f32[128,2560]{1,0:T(8,128)} %copy-done.7) | copy-start | bytes 3932164
  168.0 42.6 %collective-permute-start.27 = (bf16[128,960]{1,0:T(8,128)(2,1)S(1)}, bf16[128,960]{1,0:T(8,128)(2,1)S(1)}, u32[]{:S(2)}, u32[]{:S(2)}) collective-permute-start(bf16[128,960]{1,0:T(8,128)(2,1)S(1)} %get-tuple-element.103), channel_id=1, source_target_pairs={{0,64},{1,65},{2,66},{3,67},{4,68},{5,69},{6,70},{7,71},{8,72},{9,... | collective-permute-start | bytes 737288 | tf_op jit(solution)/shard_map/ppermute | solution.py:283
  186.2 13.1 %copy-start.2 = (bf16[960,1024]{1,0:T(8,128)(2,1)S(1)}, bf16[960,1024]{1,0:T(8,128)(2,1)}, u32[]{:S(2)}) copy-start(bf16[960,1024]{1,0:T(8,128)(2,1)} %copy-done.1) | copy-start | bytes 5898244
  186.2 13.1 %copy-start.13 = (bf16[128,1664]{1,0:T(8,128)(2,1)S(1)}, bf16[128,1664]{1,0:T(8,128)(2,1)}, u32[]{:S(2)}) copy-start(bf16[128,1664]{1,0:T(8,128)(2,1)} %copy-done.12) | copy-start | bytes 1277956
  209.4 18.0 %collective-permute-start.28 = (bf16[128,960]{1,0:T(8,128)(2,1)S(1)}, bf16[128,960]{1,0:T(8,128)(2,1)S(1)}, u32[]{:S(2)}, u32[]{:S(2)}) collective-permute-start(bf16[128,960]{1,0:T(8,128)(2,1)S(1)} %get-tuple-element.114), channel_id=1, source_target_pairs={{64,0},{65,1},{66,2},{67,3},{68,4},{69,5},{70,6},{71,7},{72,8},{73... | collective-permute-start | bytes 737288 | tf_op jit(solution)/shard_map/ppermute | solution.py:283
  228.4 14.8 %copy-start.3 = (bf16[960,1024]{1,0:T(8,128)(2,1)S(1)}, bf16[960,1024]{1,0:T(8,128)(2,1)}, u32[]{:S(2)}) copy-start(bf16[960,1024]{1,0:T(8,128)(2,1)} %copy-done.1) | copy-start | bytes 5898244
  252.5 10.7 %collective-permute-start.29 = (bf16[128,960]{1,0:T(8,128)(2,1)S(1)}, bf16[128,960]{1,0:T(8,128)(2,1)S(1)}, u32[]{:S(2)}, u32[]{:S(2)}) collective-permute-start(bf16[128,960]{1,0:T(8,128)(2,1)S(1)} %get-tuple-element.119), channel_id=1, source_target_pairs={{64,0},{65,1},{66,2},{67,3},{68,4},{69,5},{70,6},{71,7},{72,8},{73... | collective-permute-start | bytes 737288 | tf_op jit(solution)/shard_map/ppermute | solution.py:283
  270.5 17.4 %collective-permute-start.30 = (bf16[32,40,960]{2,1,0:T(8,128)(2,1)S(1)}, bf16[32,40,960]{2,1,0:T(8,128)(2,1)}, u32[]{:S(2)}, u32[]{:S(2)}) collective-permute-start(bf16[32,40,960]{2,1,0:T(8,128)(2,1)S(1)} %slice.272), channel_id=1, source_target_pairs={{0,1},{1,0},{2,3},{3,2},{4,5},{5,4},{6,7},{7,6},{8,9},{9,8},{10,11... | collective-permute-start | bytes 7372808 | tf_op jit(solution)/shard_map/ppermute | solution.py:49
  287.9 21.0 %collective-permute-start.33 = (bf16[32,16,5120]{2,1,0:T(8,128)(2,1)}, bf16[32,16,5120]{2,1,0:T(8,128)(2,1)}, u32[]{:S(2)}, u32[]{:S(2)}) collective-permute-start(bf16[32,16,5120]{2,1,0:T(8,128)(2,1)} %bitcast.191), channel_id=1, source_target_pairs={{0,1},{1,0},{2,3},{3,2},{4,5},{5,4},{6,7},{7,6},{8,9},{9,8},{10,11... | collective-permute-start | bytes 15728648 | tf_op jit(solution)/shard_map/ppermute | solution.py:49
  292.4 16.6 %copy-start.51 = (bf16[32,40,960]{2,1,0:T(8,128)(2,1)}, bf16[32,40,960]{2,1,0:T(8,128)(2,1)S(1)}, u32[]{:S(2)}) copy-start(bf16[32,40,960]{2,1,0:T(8,128)(2,1)S(1)} %add_convert_fusion) | copy-start | bytes 7372804
  292.5 16.4 %collective-permute-start.32 = (bf16[4,40,960]{2,1,0:T(8,128)(2,1)S(1)}, bf16[4,40,960]{2,1,0:T(8,128)(2,1)S(1)}, u32[]{:S(2)}, u32[]{:S(2)}) collective-permute-start(bf16[4,40,960]{2,1,0:T(8,128)(2,1)S(1)} %get-tuple-element.230), channel_id=1, source_target_pairs={{0,6},{1,49},{2,0},{3,51},{4,2},{5,53},{6,4},{7,55},{8,14},{9,57},... | collective-permute-start | bytes 921608 | tf_op jit(solution)/shard_map/ppermute | solution.py:49
  294.2 14.7 %collective-permute-start.31 = (bf16[4,40,960]{2,1,0:T(8,128)(2,1)S(1)}, bf16[4,40,960]{2,1,0:T(8,128)(2,1)S(1)}, u32[]{:S(2)}, u32[]{:S(2)}) collective-permute-start(bf16[4,40,960]{2,1,0:T(8,128)(2,1)S(1)} %get-tuple-element.231), channel_id=1, source_target_pairs={{0,2},{1,17},{2,4},{3,19},{4,6},{5,21},{6,0},{7,23},{8,10},{9,25},... | collective-permute-start | bytes 921608 | tf_op jit(solution)/shard_map/ppermute | solution.py:49
  310.2 21.7 %collective-permute-start.34 = (bf16[8,40,960]{2,1,0:T(8,128)(2,1)}, bf16[8,40,960]{2,1,0:T(8,128)(2,1)S(1)}, u32[]{:S(2)}, u32[]{:S(2)}) collective-permute-start(bf16[8,40,960]{2,1,0:T(8,128)(2,1)} %pad_maximum_fusion.14), channel_id=1, source_target_pairs={{0,2},{1,17},{2,4},{3,19},{4,6},{5,21},{6,0},{7,23},{8,10},{9,25},... | collective-permute-start | bytes 1843208 | tf_op jit(solution)/shard_map/ppermute | solution.py:49
  312.3 29.0 %collective-permute-start.38 = (bf16[32,16,2688]{2,1,0:T(8,128)(2,1)S(1)}, bf16[32,16,2688]{2,1,0:T(8,128)(2,1)S(1)}, u32[]{:S(2)}, u32[]{:S(2)}) collective-permute-start(bf16[32,16,2688]{2,1,0:T(8,128)(2,1)S(1)} %bitcast.175), channel_id=1, source_target_pairs={{0,1},{1,0},{2,3},{3,2},{4,5},{5,4},{6,7},{7,6},{8,9},{9,8},{10,11... | collective-permute-start | bytes 8257544 | tf_op jit(solution)/shard_map/ppermute | solution.py:49
  323.0 18.2 %collective-permute-start.37 = (bf16[4,16,5120]{2,1,0:T(8,128)(2,1)S(1)}, bf16[4,16,5120]{2,1,0:T(8,128)(2,1)}, u32[]{:S(2)}, u32[]{:S(2)}) collective-permute-start(bf16[4,16,5120]{2,1,0:T(8,128)(2,1)S(1)} %get-tuple-element.216), channel_id=1, source_target_pairs={{0,6},{1,49},{2,0},{3,51},{4,2},{5,53},{6,4},{7,55},{8,14},{9,57},... | collective-permute-start | bytes 1966088 | tf_op jit(solution)/shard_map/ppermute | solution.py:49
  326.0 15.2 %collective-permute-start.36 = (bf16[4,16,5120]{2,1,0:T(8,128)(2,1)S(1)}, bf16[4,16,5120]{2,1,0:T(8,128)(2,1)}, u32[]{:S(2)}, u32[]{:S(2)}) collective-permute-start(bf16[4,16,5120]{2,1,0:T(8,128)(2,1)S(1)} %get-tuple-element.217), channel_id=1, source_target_pairs={{0,2},{1,17},{2,4},{3,19},{4,6},{5,21},{6,0},{7,23},{8,10},{9,25},... | collective-permute-start | bytes 1966088 | tf_op jit(solution)/shard_map/ppermute | solution.py:49
  326.9 14.3 %collective-permute-start.35 = (bf16[8,40,960]{2,1,0:T(8,128)(2,1)}, bf16[8,40,960]{2,1,0:T(8,128)(2,1)S(1)}, u32[]{:S(2)}, u32[]{:S(2)}) collective-permute-start(bf16[8,40,960]{2,1,0:T(8,128)(2,1)} %pad_maximum_fusion.15), channel_id=1, source_target_pairs={{0,6},{1,49},{2,0},{3,51},{4,2},{5,53},{6,4},{7,55},{8,14},{9,57},... | collective-permute-start | bytes 1843208 | tf_op jit(solution)/shard_map/ppermute | solution.py:49
  343.3 23.8 %collective-permute-start.41 = (bf16[8,16,5120]{2,1,0:T(8,128)(2,1)S(1)}, bf16[8,16,5120]{2,1,0:T(8,128)(2,1)S(1)}, u32[]{:S(2)}, u32[]{:S(2)}) collective-permute-start(bf16[8,16,5120]{2,1,0:T(8,128)(2,1)S(1)} %pad_maximum_fusion.7), channel_id=1, source_target_pairs={{0,2},{1,17},{2,4},{3,19},{4,6},{5,21},{6,0},{7,23},{8,10},{9,25},... | collective-permute-start | bytes 3932168 | tf_op jit(solution)/shard_map/ppermute | solution.py:49
  344.9 22.3 %collective-permute-start.42 = (bf16[8,16,5120]{2,1,0:T(8,128)(2,1)S(1)}, bf16[8,16,5120]{2,1,0:T(8,128)(2,1)S(1)}, u32[]{:S(2)}, u32[]{:S(2)}) collective-permute-start(bf16[8,16,5120]{2,1,0:T(8,128)(2,1)S(1)} %pad_maximum_fusion.8), channel_id=1, source_target_pairs={{0,6},{1,49},{2,0},{3,51},{4,2},{5,53},{6,4},{7,55},{8,14},{9,57},... | collective-permute-start | bytes 3932168 | tf_op jit(solution)/shard_map/ppermute | solution.py:49
  347.9 19.2 %collective-permute-start.44 = (bf16[4,16,2688]{2,1,0:T(8,128)(2,1)S(1)}, bf16[4,16,2688]{2,1,0:T(8,128)(2,1)S(1)}, u32[]{:S(2)}, u32[]{:S(2)}) collective-permute-start(bf16[4,16,2688]{2,1,0:T(8,128)(2,1)S(1)} %get-tuple-element.222), channel_id=1, source_target_pairs={{0,6},{1,49},{2,0},{3,51},{4,2},{5,53},{6,4},{7,55},{8,14},{9,57},... | collective-permute-start | bytes 1032200 | tf_op jit(solution)/shard_map/ppermute | solution.py:49
  350.0 17.1 %collective-permute-start.43 = (bf16[4,16,2688]{2,1,0:T(8,128)(2,1)S(1)}, bf16[4,16,2688]{2,1,0:T(8,128)(2,1)S(1)}, u32[]{:S(2)}, u32[]{:S(2)}) collective-permute-start(bf16[4,16,2688]{2,1,0:T(8,128)(2,1)S(1)} %get-tuple-element.223), channel_id=1, source_target_pairs={{0,2},{1,17},{2,4},{3,19},{4,6},{5,21},{6,0},{7,23},{8,10},{9,25},... | collective-permute-start | bytes 1032200 | tf_op jit(solution)/shard_map/ppermute | solution.py:49
  351.5 5.6 %collective-permute-start.40 = (bf16[1,40,960]{2,1,0:T(8,128)(2,1)S(1)}, bf16[1,40,960]{2,1,0:T(8,128)(2,1)S(1)}, u32[]{:S(2)}, u32[]{:S(2)}) collective-permute-start(bf16[1,40,960]{2,1,0:T(8,128)(2,1)S(1)} %get-tuple-element.242), channel_id=1, source_target_pairs={{0,48},{1,7},{2,50},{3,1},{4,52},{5,3},{6,54},{7,5},{8,56},{9,15},... | collective-permute-start | bytes 230408 | tf_op jit(solution)/shard_map/ppermute | solution.py:49
  357.1 7.1 %collective-permute-start.39 = (bf16[1,40,960]{2,1,0:T(8,128)(2,1)S(1)}, bf16[1,40,960]{2,1,0:T(8,128)(2,1)S(1)}, u32[]{:S(2)}, u32[]{:S(2)}) collective-permute-start(bf16[1,40,960]{2,1,0:T(8,128)(2,1)S(1)} %get-tuple-element.243), channel_id=1, source_target_pairs={{0,16},{1,3},{2,18},{3,5},{4,20},{5,7},{6,22},{7,1},{8,24},{9,11},... | collective-permute-start | bytes 230408 | tf_op jit(solution)/shard_map/ppermute | solution.py:49
  367.2 9.2 %collective-permute-start.45 = (bf16[2,40,960]{2,1,0:T(8,128)(2,1)S(1)}, bf16[2,40,960]{2,1,0:T(8,128)(2,1)S(1)}, u32[]{:S(2)}, u32[]{:S(2)}) collective-permute-start(bf16[2,40,960]{2,1,0:T(8,128)(2,1)S(1)} %pad_maximum_fusion.23), channel_id=1, source_target_pairs={{0,16},{1,3},{2,18},{3,5},{4,20},{5,7},{6,22},{7,1},{8,24},{9,11},... | collective-permute-start | bytes 460808 | tf_op jit(solution)/shard_map/ppermute | solution.py:49
  367.7 8.8 %collective-permute-start.46 = (bf16[2,40,960]{2,1,0:T(8,128)(2,1)S(1)}, bf16[2,40,960]{2,1,0:T(8,128)(2,1)S(1)}, u32[]{:S(2)}, u32[]{:S(2)}) collective-permute-start(bf16[2,40,960]{2,1,0:T(8,128)(2,1)S(1)} %pad_maximum_fusion.24), channel_id=1, source_target_pairs={{0,48},{1,7},{2,50},{3,1},{4,52},{5,3},{6,54},{7,5},{8,56},{9,15},... | collective-permute-start | bytes 460808 | tf_op jit(solution)/shard_map/ppermute | solution.py:49
  370.9 12.4 %collective-permute-start.47 = (bf16[8,16,2688]{2,1,0:T(8,128)(2,1)S(1)}, bf16[8,16,2688]{2,1,0:T(8,128)(2,1)S(1)}, u32[]{:S(2)}, u32[]{:S(2)}) collective-permute-start(bf16[8,16,2688]{2,1,0:T(8,128)(2,1)S(1)} %pad_maximum_fusion.10), channel_id=1, source_target_pairs={{0,2},{1,17},{2,4},{3,19},{4,6},{5,21},{6,0},{7,23},{8,10},{9,25},... | collective-permute-start | bytes 2064392 | tf_op jit(solution)/shard_map/ppermute | solution.py:49
  373.0 11.0 %collective-permute-start.48 = (bf16[8,16,2688]{2,1,0:T(8,128)(2,1)S(1)}, bf16[8,16,2688]{2,1,0:T(8,128)(2,1)S(1)}, u32[]{:S(2)}, u32[]{:S(2)}) collective-permute-start(bf16[8,16,2688]{2,1,0:T(8,128)(2,1)S(1)} %pad_maximum_fusion.11), channel_id=1, source_target_pairs={{0,6},{1,49},{2,0},{3,51},{4,2},{5,53},{6,4},{7,55},{8,14},{9,57},... | collective-permute-start | bytes 2064392 | tf_op jit(solution)/shard_map/ppermute | solution.py:49
  384.5 14.2 %copy-start.31 = (bf16[128,960]{1,0:T(8,128)(2,1)S(1)}, bf16[128,960]{1,0:T(8,128)(2,1)}, u32[]{:S(2)}) copy-start(bf16[128,960]{1,0:T(8,128)(2,1)} %copy-done.30) | copy-start | bytes 737284
  384.5 6.9 %collective-permute-start.51 = (bf16[1,16,7808]{2,1,0:T(8,128)(2,1)S(1)}, bf16[1,16,7808]{2,1,0:T(8,128)(2,1)S(1)}, u32[]{:S(2)}, u32[]{:S(2)}) collective-permute-start(bf16[1,16,7808]{2,1,0:T(8,128)(2,1)S(1)} %get-tuple-element.236), channel_id=1, source_target_pairs={{0,48},{1,7},{2,50},{3,1},{4,52},{5,3},{6,54},{7,5},{8,56},{9,15},... | collective-permute-start | bytes 749576 | tf_op jit(solution)/shard_map/ppermute | solution.py:49
  386.0 7.6 %collective-permute-start.50 = (bf16[1,16,7808]{2,1,0:T(8,128)(2,1)S(1)}, bf16[1,16,7808]{2,1,0:T(8,128)(2,1)S(1)}, u32[]{:S(2)}, u32[]{:S(2)}) collective-permute-start(bf16[1,16,7808]{2,1,0:T(8,128)(2,1)S(1)} %get-tuple-element.237), channel_id=1, source_target_pairs={{0,16},{1,3},{2,18},{3,5},{4,20},{5,7},{6,22},{7,1},{8,24},{9,11},... | collective-permute-start | bytes 749576 | tf_op jit(solution)/shard_map/ppermute | solution.py:49
  386.9 4.5 %collective-permute-start.49 = (bf16[40,960]{1,0:T(8,128)(2,1)S(1)}, bf16[40,960]{1,0:T(8,128)(2,1)S(1)}, u32[]{:S(2)}, u32[]{:S(2)}) collective-permute-start(bf16[40,960]{1,0:T(8,128)(2,1)S(1)} %slice_bitcast_fusion.27), channel_id=1, source_target_pairs={{0,8},{1,9},{2,10},{3,11},{4,12},{5,13},{6,14},{7,15},{8,0},{9,1},... | collective-permute-start | bytes 230408 | tf_op jit(solution)/shard_map/ppermute | solution.py:49
  394.6 10.4 %collective-permute-start.52 = (bf16[2,16,7808]{2,1,0:T(8,128)(2,1)}, bf16[2,16,7808]{2,1,0:T(8,128)(2,1)}, u32[]{:S(2)}, u32[]{:S(2)}) collective-permute-start(bf16[2,16,7808]{2,1,0:T(8,128)(2,1)} %pad_maximum_fusion.21), channel_id=1, source_target_pairs={{0,16},{1,3},{2,18},{3,5},{4,20},{5,7},{6,22},{7,1},{8,24},{9,11},... | collective-permute-start | bytes 1499144 | tf_op jit(solution)/shard_map/ppermute | solution.py:49
  395.5 10.0 %collective-permute-start.53 = (bf16[2,16,7808]{2,1,0:T(8,128)(2,1)}, bf16[2,16,7808]{2,1,0:T(8,128)(2,1)}, u32[]{:S(2)}, u32[]{:S(2)}) collective-permute-start(bf16[2,16,7808]{2,1,0:T(8,128)(2,1)} %pad_maximum_fusion.22), channel_id=1, source_target_pairs={{0,48},{1,7},{2,50},{3,1},{4,52},{5,3},{6,54},{7,5},{8,56},{9,15},... | collective-permute-start | bytes 1499144 | tf_op jit(solution)/shard_map/ppermute | solution.py:49
  406.9 6.3 %collective-permute-start.54 = (bf16[16,7808]{1,0:T(8,128)(2,1)S(1)}, bf16[16,7808]{1,0:T(8,128)(2,1)S(1)}, u32[]{:S(2)}, u32[]{:S(2)}) collective-permute-start(bf16[16,7808]{1,0:T(8,128)(2,1)S(1)} %slice_bitcast_fusion.18), channel_id=1, source_target_pairs={{0,8},{1,9},{2,10},{3,11},{4,12},{5,13},{6,14},{7,15},{8,0},{9,1},... | collective-permute-start | bytes 749576 | tf_op jit(solution)/shard_map/ppermute | solution.py:49
  (58 other events, 314.4 us)

commit v3 on v2

--- a/solution.py
+++ b/solution.py
@@ -57,28 +57,35 @@
 
 
 def near_scatter(blocks):
-    blocks = yield from ring_scatter(blocks, "narrow")
-    (got,) = yield (send(blocks[1], "x"),)
+    blocks = yield from ring_scatter((blocks,), "narrow")
+    (got,) = yield ((blocks[1], "x"),)
     return total(blocks[0], got)
 
 
-def ring_scatter(blocks, kind):
-    blocks = blocks.reshape((4, blocks.shape[0] // 4) + blocks.shape[1:])
-    half = blocks.shape[1] // 2
-    left, right = yield (send(blocks[3, :half], kind, 1), send(blocks[3, half:], kind, -1))
-    onward = jnp.concatenate([total(blocks[1, :half], left).astype(BF16), blocks[1, half:]], 0)
-    back = jnp.concatenate([blocks[2, :half], total(blocks[2, half:], right).astype(BF16)], 0)
-    left, right = yield (send(onward, kind, 1), send(back, kind, -1))
-    return total(blocks[0], left, right).astype(BF16)
+def ring_scatter(terms, kind):
+    terms = [term.reshape((4, term.shape[0] // 4) + term.shape[1:]) for term in terms]
+    half = terms[0].shape[1] // 2
+
+    def own(step, part):
+        return [term[step, part] for term in terms]
+
+    near, far = slice(0, half), slice(half, None)
+    left, right = yield (
+        (total(*own(3, near)).astype(BF16), kind, 1),
+        (total(*own(3, far)).astype(BF16), kind, -1),
+    )
+    onward = jnp.concatenate([total(*own(1, near), left), total(*own(1, far))], 0).astype(BF16)
+    back = jnp.concatenate([total(*own(2, near)), total(*own(2, far), right)], 0).astype(BF16)
+    left, right = yield ((onward, kind, 1), (back, kind, -1))
+    return total(*[term[0] for term in terms], left, right).astype(BF16)
 
 
 def far_scatter(for_other, for_own):
-    (got,) = yield (send(for_other, "core"),)
-    blocks = total(for_own(), got).astype(BF16)
-    return (yield from ring_scatter(blocks, "wide"))
-
-
-def down_scatter(for_other, for_own):
+    (got,) = yield ((for_other, "core"),)
+    return (yield from ring_scatter((for_own(), got), "wide"))
+
+
+def full_scatter(for_other, for_own):
     blocks = yield from far_scatter(for_other, for_own)
     return (yield from near_scatter(blocks))
 
@@ -87,13 +94,19 @@
     def __init__(self, stages):
         self.stages = stages
         self.result = None
-        self.pending = next(stages)
+        self.wanted = next(stages)
+        self.launch(tuple(request[0] for request in self.wanted))
+
+    def launch(self, blocks):
+        self.pending = tuple(
+            send(block, *request[1:]) for block, request in zip(blocks, self.wanted)
+        )
 
     def advance(self, arrived):
         try:
-            self.pending = self.stages.send(arrived)
+            self.wanted = self.stages.send(arrived)
         except StopIteration as end:
-            self.pending = ()
+            self.wanted = ()
             self.result = end.value
 
 
@@ -102,6 +115,10 @@
     arrived, value = lax.optimization_barrier((tuple(flow.pending for flow in flows), value))
     for flow, got in zip(flows, arrived):
         flow.advance(got)
+    blocks = tuple(tuple(request[0] for request in flow.wanted) for flow in flows)
+    blocks, value = lax.optimization_barrier((blocks, value))
+    for flow, ready in zip(flows, blocks):
+        flow.launch(ready)
     return value
 
 
@@ -121,9 +138,17 @@
 
 
 def gather_far(block):
-    pieces = ring_gather(block, "wide")
-    others = [send(piece, "core") for piece in pieces]
-    return (pieces[2], jnp.concatenate(pieces + others, 0))
+    half = block.shape[0] // 2
+    left, right, others = yield ((block, "wide", 1), (block, "wide", -1), (block, "core"))
+    sides = jnp.concatenate([right, left], 0)
+    left, right, sides_there = yield (
+        (left[:half], "wide", 1),
+        (right[half:], "wide", -1),
+        (sides, "core"),
+    )
+    far = jnp.concatenate([left, right], 0)
+    (far_there,) = yield ((far, "core"),)
+    return jnp.concatenate([block, sides, far, others, sides_there, far_there], 0)
 
 
 def after(value, earlier):
@@ -170,7 +195,7 @@
             pl.BlockSpec(memory_space=pltpu.VMEM),
         ],
         out_specs=pl.BlockSpec(memory_space=pltpu.VMEM),
-        compiler_params=pltpu.CompilerParams(vmem_limit_bytes=32 * 1024 * 1024),
+        compiler_params=pltpu.CompilerParams(vmem_limit_bytes=24 * 1024 * 1024),
     )(order, blocks)
 
 
@@ -178,15 +203,24 @@
     return lax.dot_general(left, right, (((0,), (0,)), ((), ())), preferred_element_type=F32)
 
 
-VMEM_BYTES = 48 * 1024 * 1024
-
-
-def down_kernel(place_ref, left_ref, right_ref, out_ref):
+VMEM_BYTES = 16 * 1024 * 1024
+
+
+def down_kernel(place_ref, left_ref, right_ref, own_ref, other_ref):
     step = pl.program_id(0)
     rows = across(left_ref[...], right_ref[...]).astype(BF16)
     count = rows.shape[0] // FROWS
     for block in range(count):
-        out_ref[place_ref[step * count + block]] = rows[block * FROWS : (block + 1) * FROWS]
+        place_here = place_ref[step * count + block]
+        part = rows[block * FROWS : (block + 1) * FROWS]
+
+        @pl.when(place_here < N_DP // 2)
+        def keep():
+            own_ref[place_here] = part
+
+        @pl.when(place_here >= N_DP // 2)
+        def give():
+            other_ref[place_here - N_DP // 2] = part
 
 
 def down_sums(left, right, places):
@@ -195,13 +229,13 @@
     return pl.pallas_call(
         down_kernel,
         grid=(FF // width,),
-        out_shape=jax.ShapeDtypeStruct((N_DP, FROWS, D), BF16),
+        out_shape=[jax.ShapeDtypeStruct((N_DP // 2, FROWS, D), BF16)] * 2,
         in_specs=[
             pl.BlockSpec(memory_space=pltpu.SMEM),
             pl.BlockSpec((tokens, width), lambda i: (0, i)),
             pl.BlockSpec((tokens, D), lambda i: (0, 0)),
         ],
-        out_specs=pl.BlockSpec((N_DP, FROWS, D), lambda i: (0, 0, 0)),
+        out_specs=[pl.BlockSpec((N_DP // 2, FROWS, D), lambda i: (0, 0, 0))] * 2,
         compiler_params=pltpu.CompilerParams(vmem_limit_bytes=VMEM_BYTES),
         cost_estimate=pl.CostEstimate(
             flops=2 * tokens * FF * D, bytes_accessed=2 * FF * D, transcendentals=0
@@ -302,7 +336,7 @@
 
 
 def whole(*shape):
-    return pl.BlockSpec(shape, lambda *_: (0,) * len(shape))
+    return pl.BlockSpec(shape, lambda *_: (0,) * len(shape), pipeline_mode=pl.Buffered(1))
 
 
 def scaled(value, gain):
@@ -544,6 +578,104 @@
             flops=2 * length * wide * 7680, bytes_accessed=22000000, transcendentals=length * FF
         ),
     )(flags, grad, *middles, *gates, *ups, gate_up_mat, gate_up_mat, down_mat, spread, gains)
+
+
+def gate_grads_kernel(
+    flag_ref, grad_ref, gate_a_ref, gate_b_ref, up_a_ref, up_b_ref, down_ref, grad_gate_ref, grad_up_ref
+):
+    first = flag_ref[0] == 1
+    gate = jnp.where(first, gate_a_ref[...], gate_b_ref[...])
+    up = jnp.where(first, up_a_ref[...], up_b_ref[...])
+    grad_act = dot_t(grad_ref[...], down_ref[...])
+    sig = 1.0 / (1.0 + jnp.exp(-gate))
+    grad_gate_ref[...] = (grad_act * up * sig * (1.0 + gate * (1.0 - sig))).astype(BF16)
+    grad_up_ref[...] = (grad_act * gate * sig).astype(BF16)
+
+
+def gate_grads(flags, grad, gates, ups, down_mat):
+    length = grad.shape[0]
+    column = lambda i, flag: (0, i)
+    chosen = pl.BlockSpec((length, PART), lambda i, flag: (0, i * flag[0]))
+    other = pl.BlockSpec((length, PART), lambda i, flag: (0, i * (1 - flag[0])))
+    return pl.pallas_call(
+        gate_grads_kernel,
+        grid_spec=pltpu.PrefetchScalarGridSpec(
+            num_scalar_prefetch=1,
+            grid=(PARTS,),
+            in_specs=[
+                whole(length, D),
+                chosen,
+                other,
+                chosen,
+                other,
+                pl.BlockSpec((PART, D), lambda i, flag: (i, 0)),
+            ],
+            out_specs=[pl.BlockSpec((length, PART), column)] * 2,
+        ),
+        out_shape=[jax.ShapeDtypeStruct((length, FF), BF16)] * 2,
+        compiler_params=params(),
+        cost_estimate=pl.CostEstimate(
+            flops=2 * length * D * FF, bytes_accessed=9000000, transcendentals=length * FF
+        ),
+    )(flags, grad, *gates, *ups, down_mat)
+
+
+def middle_grad_kernel(
+    flag_ref, grad_ref, middle_a_ref, middle_b_ref, grad_gate_ref, grad_up_ref,
+    gate_mat_ref, up_mat_ref, spread_ref, gains_ref, grad_middle_ref, gain_ref, sum_ref,
+):
+    part = pl.program_id(0)
+    more = dot_t(grad_gate_ref[...], gate_mat_ref[...]) + dot_t(grad_up_ref[...], up_mat_ref[...])
+
+    @pl.when(part == 0)
+    def begin():
+        sum_ref[...] = more
+
+    @pl.when(part > 0)
+    def go_on():
+        sum_ref[...] += more
+
+    @pl.when(part == PARTS - 1)
+    def end():
+        grad_two = dot_t(sum_ref[...].astype(BF16), spread_ref[...])
+        middle = jnp.where(flag_ref[0] == 1, middle_a_ref[...], middle_b_ref[...])
+        through, gain = scaled_backward(middle, gains_ref[1:2], grad_two)
+        grad_middle_ref[...] = grad_ref[...].astype(F32) + through
+        gain_ref[...] = gain
+
+
+def middle_grad(flags, grad, middles, grad_gate, grad_up, gate_up_mat, spread, gains):
+    length = grad.shape[0]
+    wide = N_DP * PAD
+    column = lambda i, flag: (0, i)
+    return pl.pallas_call(
+        middle_grad_kernel,
+        grid_spec=pltpu.PrefetchScalarGridSpec(
+            num_scalar_prefetch=1,
+            grid=(PARTS,),
+            in_specs=[
+                whole(length, D),
+                whole(length, D),
+                whole(length, D),
+                pl.BlockSpec((length, PART), column),
+                pl.BlockSpec((length, PART), column),
+                pl.BlockSpec((wide, PART), column),
+                pl.BlockSpec((wide, PART), lambda i, flag: (0, i + PARTS)),
+                whole(D, wide),
+                whole(2, D),
+            ],
+            out_specs=[whole(length, D), whole(1, D)],
+            scratch_shapes=[pltpu.VMEM((length, wide), F32)],
+        ),
+        out_shape=[
+            jax.ShapeDtypeStruct((length, D), F32),
+            jax.ShapeDtypeStruct((1, D), F32),
+        ],
+        compiler_params=params(),
+        cost_estimate=pl.CostEstimate(
+            flops=2 * length * wide * 5120, bytes_accessed=14000000, transcendentals=0
+        ),
+    )(flags, grad, *middles, grad_gate, grad_up, gate_up_mat, gate_up_mat, spread, gains)
 
 
 def attend_backward_kernel(
@@ -664,9 +796,15 @@
     near_attn = near[:, :, : widths[0]]
     near_gate_up = near[:, :, widths[0] : widths[0] + widths[1]]
     near_down = near[:, :, widths[0] + widths[1] :].reshape(8, FROWS, OUT_PAD)[:, :, :D]
-    signal, attn_mat = gather_far(near_attn)
-    signal, gate_up_mat = gather_far(after(near_gate_up, signal))
-    signal, down_mat = gather_far(after(near_down, signal))
+    gate_up_flow = Flow(gather_far(near_gate_up))
+    attn_flow = Flow(gather_far(after(near_attn, near_gate_up)))
+    spread = step([attn_flow], spread)
+    spread, near_down = step([gate_up_flow], (spread, near_down))
+    down_flow = Flow(gather_far(near_down))
+    for group in ([attn_flow], [gate_up_flow], [attn_flow], [down_flow], [gate_up_flow], [down_flow]):
+        spread = step(group, spread)
+    spread = step([down_flow], spread)
+    attn_mat, gate_up_mat, down_mat = attn_flow.result, gate_up_flow.result, down_flow.result
     attn_mat = attn_mat.reshape(N_DP * PAD, -1)
     gate_up_mat = gate_up_mat.reshape(N_DP * PAD, -1)
     down_mat = reorder(down_mat, order, True).reshape(FF, D)
@@ -742,35 +880,40 @@
         if last:
             blocks = down_sums(lefts(7), rights(downs), places)
             grad_out = after(grad_out, blocks)
-            flows["down"] = Flow(
-                down_scatter(blocks[N_DP // 2 :], lambda: blocks[: N_DP // 2])
-            )
+            down_own, down_other = blocks
+            flows["down"] = Flow(full_scatter(down_other, lambda: down_own))
         kept_first, kept_second = saved[max(turn - 1, 0)], saved[min(turn + 1, batches)]
         chosen = flags(max(turn - 1, 0), min(turn, batches - 1))
 
         def both(member):
             return (kept_first[member], kept_second[member])
 
-        grad_gate, grad_up, grad_middle, gain_two = mlp_backward(
-            chosen, grad_out, both(3), both(5), both(6), gate_up_mat, down_mat, spread, gains_full
-        )
-        gates.append(grad_gate)
-        ups.append(grad_up)
-        if last:
+        if not last:
+            grad_gate, grad_up, grad_middle, gain_two = mlp_backward(
+                chosen, grad_out, both(3), both(5), both(6), gate_up_mat, down_mat, spread, gains_full
+            )
+            gates.append(grad_gate)
+            ups.append(grad_up)
+        else:
+            grad_gate, grad_up = gate_grads(chosen, grad_out, both(5), both(6), down_mat)
+            gates.append(grad_gate)
+            ups.append(grad_up)
             terms = (lefts(4), rights(gates), rights(ups))
             other = gate_up_sums(*terms, 1)
             other = step([flows["down"]], other)
             flows["gate_up"] = Flow(
-                far_scatter(as_blocks(other), lambda: as_blocks(gate_up_own[0]))
+                full_scatter(as_blocks(other), lambda: as_blocks(gate_up_own[0]))
             )
             gate_up_own.append(gate_up_sums(*after(terms, other), 0))
-            grad_middle = after(grad_middle, gate_up_own[0])
+            grad_gate, grad_up = after((grad_gate, grad_up), gate_up_own[0])
+            grad_middle, gain_two = middle_grad(
+                chosen, grad_out, both(3), grad_gate, grad_up, gate_up_mat, spread, gains_full
+            )
+            grad_middle = step([flows["down"], flows["gate_up"]], grad_middle)
         grad_proj, grad_attn, grad_in, gain_one = attend_backward(
             chosen, grad_middle, inputs, arrivals[min(turn + 1, batches)], both(1), masks, spread,
             attn_mat, gains_full, cosine, sine,
         )
-        if last:
-            grad_proj = step([flows["down"], flows["gate_up"]], grad_proj)
         projs.append(grad_proj)
         attns.append(grad_attn)
         gain_sum = gain_sum + jnp.concatenate([gain_one, gain_two], 0)
@@ -794,18 +937,28 @@
     )
     terms = (lefts(0), lefts(2), rights(projs), rights(attns), gain_rows)
     other = attn_sums(*terms, 1)
-    flows["attn"] = Flow(far_scatter(as_blocks(other), lambda: as_blocks(attn_own[0])))
+    flows["attn"] = Flow(full_scatter(as_blocks(other), lambda: as_blocks(attn_own[0])))
     attn_own.append(attn_sums(*after(terms, other), 0))
     down_flow, gate_up_flow, attn_flow = flows["down"], flows["gate_up"], flows["attn"]
-    waiting = attn_own[0]
-    while attn_flow.result is None or gate_up_flow.result is None:
-        waiting = step([down_flow, gate_up_flow, attn_flow], waiting)
-    near_flow = Flow(near_scatter(jnp.concatenate([attn_flow.result, gate_up_flow.result], -1)))
-    while near_flow.result is None or down_flow.result is None:
-        waiting = step([down_flow, near_flow], waiting)
-    down_grad = down_flow.result
-    attn_grad = near_flow.result[:, : QKV_PAD + OUT_PAD]
-    gate_up_grad = near_flow.result[:, QKV_PAD + OUT_PAD :]
+    waiting = after(section_outputs, attn_own[0])
+    for group in (
+        [gate_up_flow],
+        [attn_flow],
+        [down_flow],
+        [down_flow],
+        [attn_flow],
+        [gate_up_flow],
+        [down_flow],
+        [attn_flow],
+        [gate_up_flow, down_flow],
+        [attn_flow],
+        [gate_up_flow],
+        [attn_flow],
+        [gate_up_flow, attn_flow],
+    ):
+        waiting = step(group, waiting)
+    section_outputs = waiting
+    down_grad, gate_up_grad, attn_grad = down_flow.result, gate_up_flow.result, attn_flow.result
     return (
         section_outputs,
         section_input_grads,

time: 421 us -> 375 us (0.89)
  Pallas kernels: 129 us -> 91.7 us
  local copies, waits for them, and re-layouts: 62.5 us -> 53.4 us
  starting transfers between devices: 90.4 us -> 96.6 us
  waiting for transfers between devices: 94.7 us -> 89.8 us
    pallas_call x3 -> x2, Pallas kernels: 38.4 us -> 18.3 us  [mlp_backward(): pl.pallas_call(mlp_backward_kernel, grid_spec=pltpu.PrefetchScalarGridSpe...]
    convert_element_type x13 -> x6, other arithmetic: 20.5 us -> 7.27 us  [ring_scatter(): return total(*[term[0] for term in terms], left, right).astype(BF16)]
    pallas_call x3, Pallas kernels: 25.3 us -> 14.2 us  [mlp_forward(): pl.pallas_call(mlp_forward_kernel, grid=(PARTS,), in_specs=[whole(length,...]
    pallas_call x1 -> x3, Pallas kernels: 5.15 us -> 15.9 us  [the longest x1 6.6 us: middle_grad(): pl.pallas_call(middle_grad_kernel, grid_spec=pltpu.PrefetchScalarGridSpec...]
    pallas_call x3, Pallas kernels: 27.8 us -> 21 us  [attend_backward(): pl.pallas_call(attend_backward_kernel, grid_spec=pltpu.PrefetchScalarGrid...]
    pallas_call x3, Pallas kernels: 19.5 us -> 13 us  [attend_forward(): pl.pallas_call(attend_forward_kernel, grid_spec=pltpu.PrefetchScalarGridS...]
    ppermute x51 -> x56, waiting for transfers between devices: 83.8 us -> 78 us  [send(): return lax.ppermute(block, 'dp', route(kind, step))]
    ppermute x51 -> x56, starting transfers between devices: 64.1 us -> 69.9 us  [send(): return lax.ppermute(block, 'dp', route(kind, step))]
  transfers between devices with their start and end apart: 55 -> 60, of which waited for: 21 -> 22; matrix products, arithmetic and copies ran while one was open for 17% -> 13% of each run, Pallas kernels for 19% -> 12%
where the time goes in v3:
time: 375 us; the launch traced here: 371 us
  starting transfers between devices  96.6 us (26%)
  Pallas kernels  91.7 us (24%)
  waiting for transfers between devices  89.8 us (24%)
  local copies, waits for them, and re-layouts  53.4 us (14%)
  other arithmetic  35.3 us (9%)
    ppermute x56, waiting for transfers between devices, send(): return lax.ppermute(block, 'dp', route(kind, step))  78 us
    ppermute x56, starting transfers between devices, send(): return lax.ppermute(block, 'dp', route(kind, step))  69.9 us
    unnamed x225, local copies, waits for them, and re-layouts  34.6 us
    ppermute x4, starting transfers between devices, shifted(): return lax.ppermute(block, axis, pairs)  26.7 us
    pallas_call x3, Pallas kernels, attend_backward(): pl.pallas_call(attend_backward_kernel, grid_spec=pltpu.PrefetchScalarGrid...  21 us
    pallas_call x2, Pallas kernels, mlp_backward(): pl.pallas_call(mlp_backward_kernel, grid_spec=pltpu.PrefetchScalarGridSpe...  18.3 us
    pallas_call x3, Pallas kernels, mlp_forward(): pl.pallas_call(mlp_forward_kernel, grid=(PARTS,), in_specs=[whole(length,...  14.2 us
    pallas_call x3, Pallas kernels, attend_forward(): pl.pallas_call(attend_forward_kernel, grid_spec=pltpu.PrefetchScalarGridS...  13 us
  transfers between devices with their start and end apart: 60, of which 22 were waited for; matrix products, arithmetic and copies ran while one was open for 13% of the time, Pallas kernels for 12%

profile of v3, /device:TPU:0, one launch (start us, length us, event | category | flops | bytes accessed | tf_op | source)
XLA Modules:
  0.0 371.4 jit_solution(3631761602094014372)
XLA Ops:
  9.9 4.8 %collective-permute-done = bf16[16,10368]{1,0:T(8,128)(2,1)} collective-permute-done((bf16[16,10368]{1,0:T(8,128)(2,1)}, bf16[16,10368]{1,0:T(8,128)(2,1)}, u32[]{:S(2)}, u32[]{:S(2)}) %collective-permute-start) | collective-permute-done | bytes 331808 | tf_op jit(solution)/shard_map/ppermute | solution.py:49
  15.8 1.9 collective-permute-start.2
  20.3 7.6 %collective-permute-done.2 = bf16[2,16,10368]{2,1,0:T(8,128)(2,1)S(1)} collective-permute-done((bf16[2,16,10368]{2,1,0:T(8,128)(2,1)S(1)}, bf16[2,16,10368]{2,1,0:T(8,128)(2,1)S(1)}, u32[]{:S(2)}, u32[]{:S(2)}) %collective-permute-start.2) | collective-permute-done | bytes 663584 | tf_op jit(solution)/shard_map/ppermute | solution.py:49
  28.5 2.7 collective-permute-start.4
  31.4 4.9 %collective-permute-done.3 = bf16[1,16,10368]{2,1,0:T(8,128)(2,1)S(1)} collective-permute-done((bf16[1,16,10368]{2,1,0:T(8,128)(2,1)S(1)}, bf16[1,16,10368]{2,1,0:T(8,128)(2,1)S(1)}, u32[]{:S(2)}, u32[]{:S(2)}) %collective-permute-start.3) | collective-permute-done | bytes 331808 | tf_op jit(solution)/shard_map/ppermute | solution.py:49
  37.2 1.8 constant_dynamic-update-slice_fusion.21
  40.5 4.3 %collective-permute-start.9 = (bf16[8,16,2688]{2,1,0:T(8,128)(2,1)}, bf16[8,16,2688]{2,1,0:T(8,128)(2,1)S(1)}, u32[]{:S(2)}, u32[]{:S(2)}) collective-permute-start(bf16[8,16,2688]{2,1,0:T(8,128)(2,1)} %slice.372), channel_id=1, source_target_pairs={{0,6},{1,49},{2,0},{3,51},{4,2},{5,53},{6,4},{7,55},{8,14},{9,57},... | collective-permute-start | bytes 2064392 | tf_op jit(solution)/shard_map/ppermute | solution.py:49
  45.6 2.0 slice.373
  47.6 3.5 collective-permute-start.6
  51.1 2.4 reshape.659
  54.7 2.5 collective-permute-done.8
  59.6 3.2 collective-permute-start.15
  64.3 3.3 collective-permute-done.6
  67.6 5.0 %collective-permute-done.5 = bf16[8,16,5120]{2,1,0:T(8,128)(2,1)S(1)} collective-permute-done((bf16[8,16,5120]{2,1,0:T(8,128)(2,1)}, bf16[8,16,5120]{2,1,0:T(8,128)(2,1)S(1)}, u32[]{:S(2)}, u32[]{:S(2)}) %collective-permute-start.5) | collective-permute-done | bytes 1310752 | tf_op jit(solution)/shard_map/ppermute | solution.py:49
  77.6 2.0 collective-permute-start.12
  79.7 3.1 collective-permute-start.19
  84.1 7.2 %collective-permute-done.18 = bf16[4,16,5120]{2,1,0:T(8,128)(2,1)S(1)} collective-permute-done((bf16[4,16,5120]{2,1,0:T(8,128)(2,1)S(1)}, bf16[4,16,5120]{2,1,0:T(8,128)(2,1)S(1)}, u32[]{:S(2)}, u32[]{:S(2)}) %collective-permute-start.18) | collective-permute-done | bytes 655392 | tf_op jit(solution)/shard_map/ppermute | solution.py:49
  91.3 3.9 %collective-permute-done.19 = bf16[4,16,5120]{2,1,0:T(8,128)(2,1)S(1)} collective-permute-done((bf16[4,16,5120]{2,1,0:T(8,128)(2,1)S(1)}, bf16[4,16,5120]{2,1,0:T(8,128)(2,1)S(1)}, u32[]{:S(2)}, u32[]{:S(2)}) %collective-permute-start.19) | collective-permute-done | bytes 655392 | tf_op jit(solution)/shard_map/ppermute | solution.py:49
  95.8 1.8 collective-permute-done.17
  97.6 5.5 %collective-permute-done.11 = bf16[8,40,960]{2,1,0:T(8,128)(2,1)S(1)} collective-permute-done((bf16[8,40,960]{2,1,0:T(8,128)(2,1)S(1)}, bf16[8,40,960]{2,1,0:T(8,128)(2,1)S(1)}, u32[]{:S(2)}, u32[]{:S(2)}) %collective-permute-start.11) | collective-permute-done | bytes 614432 | tf_op jit(solution)/shard_map/ppermute | solution.py:49
  103.5 3.2 collective-permute-start.22
  109.1 2.6 collective-permute-done.24
  116.2 3.9 %shard_map.135 = (bf16[128,1024]{1,0:T(8,128)(2,1)S(1)}, bf16[128,1664]{1,0:T(8,128)(2,1)S(1)}, bf16[128,1024]{1,0:T(8,128)(2,1)S(1)}, f32[128,960]{1,0:T(8,128)S(1)}, bf16[128,1024]{1,0:T(8,128)(2,1)S(1)}) custom-call(s32[2]{0:T(128)S(1)} %pad_add_fusion.flag_ref, bf16[2,128,960]{2,1,0:T(8,128)(2,1)S(1)} %copy.56.own_ref, ...), custom_call_target="tpu_custom_call" | custom-call | flops 1494220800 | bytes 8000000 | tf_op jit(solution)/shard_map/pallas_call | solution.py:416
  120.2 5.2 %shard_map.137 = (f32[128,2560]{1,0:T(8,128)S(1)}, f32[128,2560]{1,0:T(8,128)S(1)}, bf16[128,2560]{1,0:T(8,128)(2,1)S(1)}, bf16[128,960]{1,0:T(8,128)(2,1)}) custom-call(bf16[128,1024]{1,0:T(8,128)(2,1)S(1)} %get-tuple-element.254.second_ref, f32[128,960]{1,0:T(8,128)S(1)} %get-tuple-element.255.middle_ref.middle_a_ref, bf16[1024,5120]{1,0:T(8,128)(2,1)S(1)} %bitcast.188, ...), custom_call_target="tpu_custom_call" | custom-call | flops 2013265920 | bytes 20000000 | tf_op jit(solution)/shard_map/pallas_call | solution.py:473
  128.5 5.6 %collective-permute-start.26 = (bf16[128,960]{1,0:T(8,128)(2,1)}, bf16[128,960]{1,0:T(8,128)(2,1)}, u32[]{:S(2)}, u32[]{:S(2)}) collective-permute-start(bf16[128,960]{1,0:T(8,128)(2,1)} %get-tuple-element.262), channel_id=1, source_target_pairs={{0,64},{1,65},{2,66},{3,67},{4,68},{5,69},{6,70},{7,71},{8,72},{9,... | collective-permute-start | bytes 737288 | tf_op jit(solution)/shard_map/ppermute | solution.py:317
  135.1 1.9 copy.82
  137.0 2.6 collective-permute-done.26.got_ref
  139.6 2.6 copy-done.6
  145.4 5.1 %shard_map.138 = (bf16[128,1024]{1,0:T(8,128)(2,1)S(1)}, bf16[128,1664]{1,0:T(8,128)(2,1)S(1)}, bf16[128,1024]{1,0:T(8,128)(2,1)S(1)}, f32[128,960]{1,0:T(8,128)S(1)}, bf16[128,1024]{1,0:T(8,128)(2,1)S(1)}) custom-call(s32[2]{0:T(128)S(1)} %copy-done.75, bf16[2,128,960]{2,1,0:T(8,128)(2,1)S(1)} %copy.56.own_ref, ...), custom_call_target="tpu_custom_call" | custom-call | flops 1494220800 | bytes 8000000 | tf_op jit(solution)/shard_map/pallas_call | solution.py:416
  152.7 4.1 %copy-done.2 = bf16[64,16,5120]{2,1,0:T(8,128)(2,1)S(1)} copy-done((bf16[64,16,5120]{2,1,0:T(8,128)(2,1)S(1)}, bf16[64,16,5120]{2,1,0:T(8,128)(2,1)}, u32[]{:S(2)}) %copy-start.2) | copy-done | bytes 10485784
  156.8 2.5 copy-done.4
  159.3 4.5 %shard_map.139 = (f32[128,2560]{1,0:T(8,128)S(1)}, f32[128,2560]{1,0:T(8,128)S(1)}, bf16[128,2560]{1,0:T(8,128)(2,1)S(1)}, bf16[128,960]{1,0:T(8,128)(2,1)S(1)}) custom-call(bf16[128,1024]{1,0:T(8,128)(2,1)S(1)} %get-tuple-element.263.second_ref, f32[128,960]{1,0:T(8,128)S(1)} %get-tuple-element.264.middle_ref.middle_b_ref.middle_a_ref, ...), custom_call_target="tpu_custom_call" | custom-call | flops 2013265920 | bytes 20000000 | tf_op jit(solution)/shard_map/pallas_call | solution.py:473
  163.9 18.5 %collective-permute-start.27 = (bf16[128,960]{1,0:T(8,128)(2,1)S(1)}, bf16[128,960]{1,0:T(8,128)(2,1)S(1)}, u32[]{:S(2)}, u32[]{:S(2)}) collective-permute-start(bf16[128,960]{1,0:T(8,128)(2,1)S(1)} %get-tuple-element.265), channel_id=1, source_target_pairs={{0,64},{1,65},{2,66},{3,67},{4,68},{5,69},{6,70},{7,71},{8,72},{9,... | collective-permute-start | bytes 737288 | tf_op jit(solution)/shard_map/ppermute | solution.py:317
  182.6 9.2 %shard_map.141 = (bf16[128,2560]{1,0:T(8,128)(2,1)S(1)}, bf16[128,2560]{1,0:T(8,128)(2,1)S(1)}, f32[128,960]{1,0:T(8,128)S(1)}, f32[1,960]{1,0:T(1,128)S(1)}) custom-call(s32[2]{0:T(128)S(1)} %pad_add_fusion.flag_ref, bf16[128,960]{1,0:T(8,128)(2,1)S(1)} %select_bitcast_fusion.4.grad_ref, f32[128,960]{1,0:T(8,128)S(1)} %copy-done.20, ...), custom_call_target="tpu_custom_call" | custom-call | flops 2013265920 | bytes 22000000 | tf_op jit(solution)/shard_map/pallas_call | solution.py:543
  191.9 7.7 %shard_map.142 = (bf16[128,1664]{1,0:T(8,128)(2,1)S(1)}, bf16[128,1024]{1,0:T(8,128)(2,1)S(1)}, bf16[128,960]{1,0:T(8,128)(2,1)S(1)}, f32[1,960]{1,0:T(1,128)S(1)}) custom-call(s32[2]{0:T(128)S(1)} %pad_add_fusion.flag_ref, f32[128,960]{1,0:T(8,128)S(1)} %get-tuple-element.271.grad_ref, bf16[2,128,960]{2,1,0:T(8,128)(2,1)S(1)} %copy.56.own_ref, ...), custom_call_target="tpu_custom_call" | custom-call | flops 1756364800 | bytes 9000000 | tf_op jit(solution)/shard_map/pallas_call | solution.py:726
  200.9 3.9 %shard_map.140 = (bf16[128,1024]{1,0:T(8,128)(2,1)S(1)}, bf16[128,1664]{1,0:T(8,128)(2,1)S(1)}, bf16[128,1024]{1,0:T(8,128)(2,1)S(1)}, f32[128,960]{1,0:T(8,128)S(1)}, bf16[128,1024]{1,0:T(8,128)(2,1)S(1)}) custom-call(s32[2]{0:T(128)S(1)} %pad_add_fusion.2.flag_ref, bf16[2,128,960]{2,1,0:T(8,128)(2,1)S(1)} %copy.56.own_ref, ...), custom_call_target="tpu_custom_call" | custom-call | flops 1494220800 | bytes 8000000 | tf_op jit(solution)/shard_map/pallas_call | solution.py:416
  204.9 4.5 %shard_map.143 = (f32[128,2560]{1,0:T(8,128)S(1)}, f32[128,2560]{1,0:T(8,128)S(1)}, bf16[128,2560]{1,0:T(8,128)(2,1)S(1)}, bf16[128,960]{1,0:T(8,128)(2,1)S(1)}) custom-call(bf16[128,1024]{1,0:T(8,128)(2,1)S(1)} %get-tuple-element.266.second_ref, f32[128,960]{1,0:T(8,128)S(1)} %get-tuple-element.275.middle_ref.middle_b_ref, ...), custom_call_target="tpu_custom_call" | custom-call | flops 2013265920 | bytes 20000000 | tf_op jit(solution)/shard_map/pallas_call | solution.py:473
  210.3 9.1 %shard_map.144 = (bf16[128,2560]{1,0:T(8,128)(2,1)S(1)}, bf16[128,2560]{1,0:T(8,128)(2,1)S(1)}, f32[128,960]{1,0:T(8,128)S(1)}, f32[1,960]{1,0:T(1,128)S(1)}) custom-call(s32[2]{0:T(128)S(1)} %copy-done.74, bf16[128,960]{1,0:T(8,128)(2,1)S(1)} %get-tuple-element.435.grad_ref, f32[128,960]{1,0:T(8,128)S(1)} %copy-done.20, ...), custom_call_target="tpu_custom_call" | custom-call | flops 2013265920 | bytes 22000000 | tf_op jit(solution)/shard_map/pallas_call | solution.py:543
  219.6 6.7 %shard_map.145 = (bf16[128,1664]{1,0:T(8,128)(2,1)S(1)}, bf16[128,1024]{1,0:T(8,128)(2,1)S(1)}, bf16[128,960]{1,0:T(8,128)(2,1)S(1)}, f32[1,960]{1,0:T(1,128)S(1)}) custom-call(s32[2]{0:T(128)S(1)} %copy-done.74, f32[128,960]{1,0:T(8,128)S(1)} %get-tuple-element.280.grad_ref, bf16[2,128,960]{2,1,0:T(8,128)(2,1)S(1)} %copy.56.own_ref, ...), custom_call_target="tpu_custom_call" | custom-call | flops 1756364800 | bytes 9000000 | tf_op jit(solution)/shard_map/pallas_call | solution.py:726
  227.9 8.3 %collective-permute-done.29 = bf16[128,960]{1,0:T(8,128)(2,1)S(1)} collective-permute-done((bf16[128,960]{1,0:T(8,128)(2,1)S(1)}, bf16[128,960]{1,0:T(8,128)(2,1)S(1)}, u32[]{:S(2)}, u32[]{:S(2)}) %collective-permute-start.29) | collective-permute-done | bytes 245792 | tf_op jit(solution)/shard_map/ppermute | solution.py:317
  236.3 5.6 %shard_map.146 = (bf16[32,40,960]{2,1,0:T(8,128)(2,1)S(1)}, bf16[32,40,960]{2,1,0:T(8,128)(2,1)}) custom-call(s32[64]{0:T(128)S(1)} %copy-done.76, bf16[256,2560]{1,0:T(8,128)(2,1)S(1)} %pad_maximum_fusion.4.left_ref, bf16[256,960]{1,0:T(8,128)(2,1)S(1)} %pad_maximum_fusion.18.right_ref), custom_call_target="tpu_custom_call" | custom-call | flops 1258291200 | bytes 4915200 | tf_op jit(solution)/shard_map/pallas_call | solution.py:229
  242.5 3.7 %shard_map.147 = (bf16[128,2560]{1,0:T(8,128)(2,1)S(1)}, bf16[128,2560]{1,0:T(8,128)(2,1)S(1)}) custom-call(s32[2]{0:T(128)S(1)} %pad_add_fusion.2.flag_ref, bf16[128,960]{1,0:T(8,128)(2,1)S(1)} %get-tuple-element.288.grad_ref, f32[128,2560]{1,0:T(8,128)S(1)} %copy-done.11, f32[128,2560]{1,0:T(8,128)S(1)} %get-tuple-element.276.gate_b_ref, ...), custom_call_target="tpu_custom_call" | custom-call | flops 629145600 | bytes 9000000 | tf_op jit(solution)/shard_map/pallas_call | solution.py:600
  246.8 2.3 shard_map.148
  249.1 1.9 fusion.32
  253.1 3.3 collective-permute-start.32
  256.4 2.3 shard_map.149
  258.7 6.6 %shard_map.150 = (f32[128,960]{1,0:T(8,128)S(1)}, f32[1,960]{1,0:T(1,128)S(1)}) custom-call(s32[2]{0:T(128)S(1)} %pad_add_fusion.2.flag_ref, bf16[128,960]{1,0:T(8,128)(2,1)S(1)} %get-tuple-element.288.grad_ref, f32[128,960]{1,0:T(8,128)S(1)} %get-tuple-element.264.middle_ref.middle_b_ref.middle_a_ref, ...), custom_call_target="tpu_custom_call" | custom-call | flops 1342177280 | bytes 14000000 | tf_op jit(solution)/shard_map/pallas_call | solution.py:651
  267.0 2.6 fusion.19
  269.6 6.7 %shard_map.151 = (bf16[128,1664]{1,0:T(8,128)(2,1)S(1)}, bf16[128,1024]{1,0:T(8,128)(2,1)S(1)}, bf16[128,960]{1,0:T(8,128)(2,1)S(1)}, f32[1,960]{1,0:T(1,128)S(1)}) custom-call(s32[2]{0:T(128)S(1)} %pad_add_fusion.2.flag_ref, f32[128,960]{1,0:T(8,128)S(1)} %get-tuple-element.319.grad_ref, bf16[2,128,960]{2,1,0:T(8,128)(2,1)S(1)} %copy.56.own_ref, ...), custom_call_target="tpu_custom_call" | custom-call | flops 1756364800 | bytes 9000000 | tf_op jit(solution)/shard_map/pallas_call | solution.py:726
  277.5 3.2 collective-permute-start.35
  285.1 3.2 collective-permute-start.42
  291.1 1.8 fusion.9
  296.9 2.4 add_convert_fusion
  301.0 3.2 collective-permute-start.44
  305.9 2.6 collective-permute-start.37
  308.5 3.2 collective-permute-start.40
  312.9 16.8 %collective-permute-done.39 = bf16[4,16,2688]{2,1,0:T(8,128)(2,1)S(1)} collective-permute-done((bf16[4,16,2688]{2,1,0:T(8,128)(2,1)}, bf16[4,16,2688]{2,1,0:T(8,128)(2,1)S(1)}, u32[]{:S(2)}, u32[]{:S(2)}) %collective-permute-start.39) | collective-permute-done | bytes 344096 | tf_op jit(solution)/shard_map/ppermute | solution.py:49
  331.4 3.2 collective-permute-start.51
  334.6 2.2 fusion.3
  338.5 2.0 collective-permute-start.45
  341.8 3.5 collective-permute-done.50
  346.8 2.3 collective-permute-start.54
  351.4 2.4 collective-permute-start.53
  354.0 3.2 collective-permute-start.58
  (424 shorter events, 92.9 us)
Async XLA Ops:
  5.0 9.7 %collective-permute-start = (bf16[16,10368]{1,0:T(8,128)(2,1)}, bf16[16,10368]{1,0:T(8,128)(2,1)}, u32[]{:S(2)}, u32[]{:S(2)}) collective-permute-start(bf16[16,10368]{1,0:T(8,128)(2,1)} %get-tuple-element.439), channel_id=1, source_target_pairs={{0,8},{1,9},{2,10},{3,11},{4,12},{5,13},{6,14},{7,15},{8,0},{9,1},... | collective-permute-start | bytes 995336 | tf_op jit(solution)/shard_map/ppermute | solution.py:49
  7.7 108.4 %copy-start.21 = (f32[128,128]{1,0:T(8,128)}, f32[128,128]{1,0:T(8,128)S(1)}, u32[]{:S(2)}) copy-start(f32[128,128]{1,0:T(8,128)S(1)} %copy.58.sine_ref) | copy-start | bytes 196612
  7.9 108.3 %copy-start.24 = (f32[128,128]{1,0:T(8,128)}, f32[128,128]{1,0:T(8,128)S(1)}, u32[]{:S(2)}) copy-start(f32[128,128]{1,0:T(8,128)S(1)} %copy.57.cosine_ref) | copy-start | bytes 196612
  9.9 106.3 %copy-start.7 = (f32[2,128,128]{2,1,0:T(8,128)}, f32[2,128,128]{2,1,0:T(8,128)S(1)}, u32[]{:S(2)}) copy-start(f32[2,128,128]{2,1,0:T(8,128)S(1)} %and_convert_fusion.mask_ref) | copy-start | bytes 393220
  15.8 12.0 %collective-permute-start.2 = (bf16[2,16,10368]{2,1,0:T(8,128)(2,1)S(1)}, bf16[2,16,10368]{2,1,0:T(8,128)(2,1)S(1)}, u32[]{:S(2)}, u32[]{:S(2)}) collective-permute-start(bf16[2,16,10368]{2,1,0:T(8,128)(2,1)S(1)} %pad_maximum_fusion.13), channel_id=1, source_target_pairs={{0,16},{1,3},{2,18},{3,5},{4,20},{5,7},{6,22},{7,1},{8,24},{9,11},... | collective-permute-start | bytes 1990664 | tf_op jit(solution)/shard_map/ppermute | solution.py:49
  17.7 10.8 %collective-permute-start.1 = (bf16[2,16,10368]{2,1,0:T(8,128)(2,1)S(1)}, bf16[2,16,10368]{2,1,0:T(8,128)(2,1)S(1)}, u32[]{:S(2)}, u32[]{:S(2)}) collective-permute-start(bf16[2,16,10368]{2,1,0:T(8,128)(2,1)S(1)} %pad_maximum_fusion.13), channel_id=1, source_target_pairs={{0,48},{1,7},{2,50},{3,1},{4,52},{5,3},{6,54},{7,5},{8,56},{9,15},... | collective-permute-start | bytes 1990664 | tf_op jit(solution)/shard_map/ppermute | solution.py:49
  27.9 8.4 %collective-permute-start.3 = (bf16[1,16,10368]{2,1,0:T(8,128)(2,1)S(1)}, bf16[1,16,10368]{2,1,0:T(8,128)(2,1)S(1)}, u32[]{:S(2)}, u32[]{:S(2)}) collective-permute-start(bf16[1,16,10368]{2,1,0:T(8,128)(2,1)S(1)} %slice.369), channel_id=1, source_target_pairs={{0,16},{1,3},{2,18},{3,5},{4,20},{5,7},{6,22},{7,1},{8,24},{9,11},... | collective-permute-start | bytes 995336 | tf_op jit(solution)/shard_map/ppermute | solution.py:49
  28.5 7.7 %collective-permute-start.4 = (bf16[1,16,10368]{2,1,0:T(8,128)(2,1)S(1)}, bf16[1,16,10368]{2,1,0:T(8,128)(2,1)S(1)}, u32[]{:S(2)}, u32[]{:S(2)}) collective-permute-start(bf16[1,16,10368]{2,1,0:T(8,128)(2,1)S(1)} %slice.370), channel_id=1, source_target_pairs={{0,48},{1,7},{2,50},{3,1},{4,52},{5,3},{6,54},{7,5},{8,56},{9,15},... | collective-permute-start | bytes 995336 | tf_op jit(solution)/shard_map/ppermute | solution.py:49
  39.1 14.4 %collective-permute-start.10 = (bf16[8,16,2688]{2,1,0:T(8,128)(2,1)}, bf16[8,16,2688]{2,1,0:T(8,128)(2,1)}, u32[]{:S(2)}, u32[]{:S(2)}) collective-permute-start(bf16[8,16,2688]{2,1,0:T(8,128)(2,1)} %slice.372), channel_id=1, source_target_pairs={{0,1},{1,0},{2,3},{3,2},{4,5},{5,4},{6,7},{7,6},{8,9},{9,8},{10,11... | collective-permute-start | bytes 2064392 | tf_op jit(solution)/shard_map/ppermute | solution.py:49
  40.5 14.2 %collective-permute-start.9 = (bf16[8,16,2688]{2,1,0:T(8,128)(2,1)}, bf16[8,16,2688]{2,1,0:T(8,128)(2,1)S(1)}, u32[]{:S(2)}, u32[]{:S(2)}) collective-permute-start(bf16[8,16,2688]{2,1,0:T(8,128)(2,1)} %slice.372), channel_id=1, source_target_pairs={{0,6},{1,49},{2,0},{3,51},{4,2},{5,53},{6,4},{7,55},{8,14},{9,57},... | collective-permute-start | bytes 2064392 | tf_op jit(solution)/shard_map/ppermute | solution.py:49
  44.7 12.5 %collective-permute-start.8 = (bf16[8,16,2688]{2,1,0:T(8,128)(2,1)}, bf16[8,16,2688]{2,1,0:T(8,128)(2,1)}, u32[]{:S(2)}, u32[]{:S(2)}) collective-permute-start(bf16[8,16,2688]{2,1,0:T(8,128)(2,1)} %slice.372), channel_id=1, source_target_pairs={{0,2},{1,17},{2,4},{3,19},{4,6},{5,21},{6,0},{7,23},{8,10},{9,25},... | collective-permute-start | bytes 2064392 | tf_op jit(solution)/shard_map/ppermute | solution.py:49
  47.6 16.6 %collective-permute-start.7 = (bf16[8,16,5120]{2,1,0:T(8,128)(2,1)}, bf16[8,16,5120]{2,1,0:T(8,128)(2,1)}, u32[]{:S(2)}, u32[]{:S(2)}) collective-permute-start(bf16[8,16,5120]{2,1,0:T(8,128)(2,1)} %get-tuple-element.459), channel_id=1, source_target_pairs={{0,1},{1,0},{2,3},{3,2},{4,5},{5,4},{6,7},{7,6},{8,9},{9,8},{10,11... | collective-permute-start | bytes 3932168 | tf_op jit(solution)/shard_map/ppermute | solution.py:49
  47.6 19.9 %collective-permute-start.6 = (bf16[8,16,5120]{2,1,0:T(8,128)(2,1)}, bf16[8,16,5120]{2,1,0:T(8,128)(2,1)}, u32[]{:S(2)}, u32[]{:S(2)}) collective-permute-start(bf16[8,16,5120]{2,1,0:T(8,128)(2,1)} %get-tuple-element.459), channel_id=1, source_target_pairs={{0,6},{1,49},{2,0},{3,51},{4,2},{5,53},{6,4},{7,55},{8,14},{9,57},... | collective-permute-start | bytes 3932168 | tf_op jit(solution)/shard_map/ppermute | solution.py:49
  53.5 19.0 %collective-permute-start.5 = (bf16[8,16,5120]{2,1,0:T(8,128)(2,1)}, bf16[8,16,5120]{2,1,0:T(8,128)(2,1)S(1)}, u32[]{:S(2)}, u32[]{:S(2)}) collective-permute-start(bf16[8,16,5120]{2,1,0:T(8,128)(2,1)} %get-tuple-element.459), channel_id=1, source_target_pairs={{0,2},{1,17},{2,4},{3,19},{4,6},{5,21},{6,0},{7,23},{8,10},{9,25},... | collective-permute-start | bytes 3932168 | tf_op jit(solution)/shard_map/ppermute | solution.py:49
  59.5 18.1 %collective-permute-start.14 = (bf16[4,16,2688]{2,1,0:T(8,128)(2,1)S(1)}, bf16[4,16,2688]{2,1,0:T(8,128)(2,1)S(1)}, u32[]{:S(2)}, u32[]{:S(2)}) collective-permute-start(bf16[4,16,2688]{2,1,0:T(8,128)(2,1)S(1)} %slice.283), channel_id=1, source_target_pairs={{0,2},{1,17},{2,4},{3,19},{4,6},{5,21},{6,0},{7,23},{8,10},{9,25},... | collective-permute-start | bytes 1032200 | tf_op jit(solution)/shard_map/ppermute | solution.py:49
  59.6 20.0 %collective-permute-start.15 = (bf16[4,16,2688]{2,1,0:T(8,128)(2,1)S(1)}, bf16[4,16,2688]{2,1,0:T(8,128)(2,1)S(1)}, u32[]{:S(2)}, u32[]{:S(2)}) collective-permute-start(bf16[4,16,2688]{2,1,0:T(8,128)(2,1)S(1)} %slice.284), channel_id=1, source_target_pairs={{0,6},{1,49},{2,0},{3,51},{4,2},{5,53},{6,4},{7,55},{8,14},{9,57},... | collective-permute-start | bytes 1032200 | tf_op jit(solution)/shard_map/ppermute | solution.py:49
  64.2 15.5 %collective-permute-start.16 = (bf16[16,16,2688]{2,1,0:T(8,128)(2,1)S(1)}, bf16[16,16,2688]{2,1,0:T(8,128)(2,1)S(1)}, u32[]{:S(2)}, u32[]{:S(2)}) collective-permute-start(bf16[16,16,2688]{2,1,0:T(8,128)(2,1)S(1)} %pad_maximum_fusion.1), channel_id=1, source_target_pairs={{0,1},{1,0},{2,3},{3,2},{4,5},{5,4},{6,7},{7,6},{8,9},{9,8},{10,11... | collective-permute-start | bytes 4128776 | tf_op jit(solution)/shard_map/ppermute | solution.py:49
  75.3 20.4 %collective-permute-start.20 = (bf16[16,16,5120]{2,1,0:T(8,128)(2,1)S(1)}, bf16[16,16,5120]{2,1,0:T(8,128)(2,1)S(1)}, u32[]{:S(2)}, u32[]{:S(2)}) collective-permute-start(bf16[16,16,5120]{2,1,0:T(8,128)(2,1)S(1)} %pad_maximum_fusion), channel_id=1, source_target_pairs={{0,1},{1,0},{2,3},{3,2},{4,5},{5,4},{6,7},{7,6},{8,9},{9,8},{10,11... | collective-permute-start | bytes 7864328 | tf_op jit(solution)/shard_map/ppermute | solution.py:49
  77.0 20.7 %collective-permute-start.13 = (bf16[8,40,960]{2,1,0:T(8,128)(2,1)S(1)}, bf16[8,40,960]{2,1,0:T(8,128)(2,1)S(1)}, u32[]{:S(2)}, u32[]{:S(2)}) collective-permute-start(bf16[8,40,960]{2,1,0:T(8,128)(2,1)S(1)} %bitcast.241), channel_id=1, source_target_pairs={{0,1},{1,0},{2,3},{3,2},{4,5},{5,4},{6,7},{7,6},{8,9},{9,8},{10,11... | collective-permute-start | bytes 1843208 | tf_op jit(solution)/shard_map/ppermute | solution.py:49
  77.6 20.1 %collective-permute-start.12 = (bf16[8,40,960]{2,1,0:T(8,128)(2,1)S(1)}, bf16[8,40,960]{2,1,0:T(8,128)(2,1)S(1)}, u32[]{:S(2)}, u32[]{:S(2)}) collective-permute-start(bf16[8,40,960]{2,1,0:T(8,128)(2,1)S(1)} %bitcast.243), channel_id=1, source_target_pairs={{0,6},{1,49},{2,0},{3,51},{4,2},{5,53},{6,4},{7,55},{8,14},{9,57},... | collective-permute-start | bytes 1843208 | tf_op jit(solution)/shard_map/ppermute | solution.py:49
  79.5 11.8 %collective-permute-start.18 = (bf16[4,16,5120]{2,1,0:T(8,128)(2,1)S(1)}, bf16[4,16,5120]{2,1,0:T(8,128)(2,1)S(1)}, u32[]{:S(2)}, u32[]{:S(2)}) collective-permute-start(bf16[4,16,5120]{2,1,0:T(8,128)(2,1)S(1)} %slice.287), channel_id=1, source_target_pairs={{0,2},{1,17},{2,4},{3,19},{4,6},{5,21},{6,0},{7,23},{8,10},{9,25},... | collective-permute-start | bytes 1966088 | tf_op jit(solution)/shard_map/ppermute | solution.py:49
  79.7 15.6 %collective-permute-start.19 = (bf16[4,16,5120]{2,1,0:T(8,128)(2,1)S(1)}, bf16[4,16,5120]{2,1,0:T(8,128)(2,1)S(1)}, u32[]{:S(2)}, u32[]{:S(2)}) collective-permute-start(bf16[4,16,5120]{2,1,0:T(8,128)(2,1)S(1)} %slice.288), channel_id=1, source_target_pairs={{0,6},{1,49},{2,0},{3,51},{4,2},{5,53},{6,4},{7,55},{8,14},{9,57},... | collective-permute-start | bytes 1966088 | tf_op jit(solution)/shard_map/ppermute | solution.py:49
  91.3 11.8 %collective-permute-start.11 = (bf16[8,40,960]{2,1,0:T(8,128)(2,1)S(1)}, bf16[8,40,960]{2,1,0:T(8,128)(2,1)S(1)}, u32[]{:S(2)}, u32[]{:S(2)}) collective-permute-start(bf16[8,40,960]{2,1,0:T(8,128)(2,1)S(1)} %bitcast.244), channel_id=1, source_target_pairs={{0,2},{1,17},{2,4},{3,19},{4,6},{5,21},{6,0},{7,23},{8,10},{9,25},... | collective-permute-start | bytes 1843208 | tf_op jit(solution)/shard_map/ppermute | solution.py:49
  95.3 2.4 collective-permute-start.17
  103.4 8.4 %collective-permute-start.21 = (bf16[4,40,960]{2,1,0:T(8,128)(2,1)S(1)}, bf16[4,40,960]{2,1,0:T(8,128)(2,1)S(1)}, u32[]{:S(2)}, u32[]{:S(2)}) collective-permute-start(bf16[4,40,960]{2,1,0:T(8,128)(2,1)S(1)} %slice.289), channel_id=1, source_target_pairs={{0,2},{1,17},{2,4},{3,19},{4,6},{5,21},{6,0},{7,23},{8,10},{9,25},... | collective-permute-start | bytes 921608 | tf_op jit(solution)/shard_map/ppermute | solution.py:49
  103.5 8.3 %collective-permute-start.22 = (bf16[4,40,960]{2,1,0:T(8,128)(2,1)S(1)}, bf16[4,40,960]{2,1,0:T(8,128)(2,1)S(1)}, u32[]{:S(2)}, u32[]{:S(2)}) collective-permute-start(bf16[4,40,960]{2,1,0:T(8,128)(2,1)S(1)} %slice.290), channel_id=1, source_target_pairs={{0,6},{1,49},{2,0},{3,51},{4,2},{5,53},{6,4},{7,55},{8,14},{9,57},... | collective-permute-start | bytes 921608 | tf_op jit(solution)/shard_map/ppermute | solution.py:49
  106.7 5.1 %collective-permute-start.23 = (bf16[16,40,960]{2,1,0:T(8,128)(2,1)S(1)}, bf16[16,40,960]{2,1,0:T(8,128)(2,1)S(1)}, u32[]{:S(2)}, u32[]{:S(2)}) collective-permute-start(bf16[16,40,960]{2,1,0:T(8,128)(2,1)S(1)} %pad_maximum_fusion.3), channel_id=1, source_target_pairs={{0,1},{1,0},{2,3},{3,2},{4,5},{5,4},{6,7},{7,6},{8,9},{9,8},{10,11... | collective-permute-start | bytes 3686408 | tf_op jit(solution)/shard_map/ppermute | solution.py:49
  106.8 4.9 %collective-permute-start.24 = (bf16[8,16,5120]{2,1,0:T(8,128)(2,1)S(1)}, bf16[8,16,5120]{2,1,0:T(8,128)(2,1)S(1)}, u32[]{:S(2)}, u32[]{:S(2)}) collective-permute-start(bf16[8,16,5120]{2,1,0:T(8,128)(2,1)S(1)} %pad_maximum_fusion.2), channel_id=1, source_target_pairs={{0,1},{1,0},{2,3},{3,2},{4,5},{5,4},{6,7},{7,6},{8,9},{9,8},{10,11... | collective-permute-start | bytes 3932168 | tf_op jit(solution)/shard_map/ppermute | solution.py:49
  111.9 2.2 collective-permute-start.25
  128.5 11.1 %collective-permute-start.26 = (bf16[128,960]{1,0:T(8,128)(2,1)}, bf16[128,960]{1,0:T(8,128)(2,1)}, u32[]{:S(2)}, u32[]{:S(2)}) collective-permute-start(bf16[128,960]{1,0:T(8,128)(2,1)} %get-tuple-element.262), channel_id=1, source_target_pairs={{0,64},{1,65},{2,66},{3,67},{4,68},{5,69},{6,70},{7,71},{8,72},{9,... | collective-permute-start | bytes 737288 | tf_op jit(solution)/shard_map/ppermute | solution.py:317
  135.1 47.3 %slice-start.3 = ((s8[5242880]{0:T(1024)(128)(4,1)}), s8[1048576]{0:T(1024)(128)(4,1)S(1)}, s32[]{:S(2)}) async-start(s8[5242880]{0:T(1024)(128)(4,1)} %bitcast.204), calls=%async_computation.3 | async-start | bytes 2097152
  163.9 37.1 %collective-permute-start.27 = (bf16[128,960]{1,0:T(8,128)(2,1)S(1)}, bf16[128,960]{1,0:T(8,128)(2,1)S(1)}, u32[]{:S(2)}, u32[]{:S(2)}) collective-permute-start(bf16[128,960]{1,0:T(8,128)(2,1)S(1)} %get-tuple-element.265), channel_id=1, source_target_pairs={{0,64},{1,65},{2,66},{3,67},{4,68},{5,69},{6,70},{7,71},{8,72},{9,... | collective-permute-start | bytes 737288 | tf_op jit(solution)/shard_map/ppermute | solution.py:317
  199.6 10.6 %collective-permute-start.28 = (bf16[128,960]{1,0:T(8,128)(2,1)S(1)}, bf16[128,960]{1,0:T(8,128)(2,1)S(1)}, u32[]{:S(2)}, u32[]{:S(2)}) collective-permute-start(bf16[128,960]{1,0:T(8,128)(2,1)S(1)} %get-tuple-element.274), channel_id=1, source_target_pairs={{64,0},{65,1},{66,2},{67,3},{68,4},{69,5},{70,6},{71,7},{72,8},{73... | collective-permute-start | bytes 737288 | tf_op jit(solution)/shard_map/ppermute | solution.py:317
  226.3 9.9 %collective-permute-start.29 = (bf16[128,960]{1,0:T(8,128)(2,1)S(1)}, bf16[128,960]{1,0:T(8,128)(2,1)S(1)}, u32[]{:S(2)}, u32[]{:S(2)}) collective-permute-start(bf16[128,960]{1,0:T(8,128)(2,1)S(1)} %get-tuple-element.282), channel_id=1, source_target_pairs={{64,0},{65,1},{66,2},{67,3},{68,4},{69,5},{70,6},{71,7},{72,8},{73... | collective-permute-start | bytes 737288 | tf_op jit(solution)/shard_map/ppermute | solution.py:317
  241.9 7.2 %collective-permute-start.30 = (bf16[32,40,960]{2,1,0:T(8,128)(2,1)}, bf16[32,40,960]{2,1,0:T(8,128)(2,1)}, u32[]{:S(2)}, u32[]{:S(2)}) collective-permute-start(bf16[32,40,960]{2,1,0:T(8,128)(2,1)} %get-tuple-element.287), channel_id=1, source_target_pairs={{0,1},{1,0},{2,3},{3,2},{4,5},{5,4},{6,7},{7,6},{8,9},{9,8},{10,11... | collective-permute-start | bytes 7372808 | tf_op jit(solution)/shard_map/ppermute | solution.py:49
  251.1 14.3 %collective-permute-start.33 = (bf16[32,16,5120]{2,1,0:T(8,128)(2,1)S(1)}, bf16[32,16,5120]{2,1,0:T(8,128)(2,1)}, u32[]{:S(2)}, u32[]{:S(2)}) collective-permute-start(bf16[32,16,5120]{2,1,0:T(8,128)(2,1)S(1)} %bitcast.223), channel_id=1, source_target_pairs={{0,1},{1,0},{2,3},{3,2},{4,5},{5,4},{6,7},{7,6},{8,9},{9,8},{10,11... | collective-permute-start | bytes 15728648 | tf_op jit(solution)/shard_map/ppermute | solution.py:49
  253.0 12.3 %collective-permute-start.31 = (bf16[4,40,960]{2,1,0:T(8,128)(2,1)S(1)}, bf16[4,40,960]{2,1,0:T(8,128)(2,1)S(1)}, u32[]{:S(2)}, u32[]{:S(2)}) collective-permute-start(bf16[4,40,960]{2,1,0:T(8,128)(2,1)S(1)} %get-tuple-element.299), channel_id=1, source_target_pairs={{0,2},{1,17},{2,4},{3,19},{4,6},{5,21},{6,0},{7,23},{8,10},{9,25},... | collective-permute-start | bytes 921608 | tf_op jit(solution)/shard_map/ppermute | solution.py:49
  253.1 12.3 %collective-permute-start.32 = (bf16[4,40,960]{2,1,0:T(8,128)(2,1)S(1)}, bf16[4,40,960]{2,1,0:T(8,128)(2,1)S(1)}, u32[]{:S(2)}, u32[]{:S(2)}) collective-permute-start(bf16[4,40,960]{2,1,0:T(8,128)(2,1)S(1)} %get-tuple-element.300), channel_id=1, source_target_pairs={{0,6},{1,49},{2,0},{3,51},{4,2},{5,53},{6,4},{7,55},{8,14},{9,57},... | collective-permute-start | bytes 921608 | tf_op jit(solution)/shard_map/ppermute | solution.py:49
  277.2 13.8 %collective-permute-start.34 = (bf16[4,16,5120]{2,1,0:T(8,128)(2,1)S(1)}, bf16[4,16,5120]{2,1,0:T(8,128)(2,1)S(1)}, u32[]{:S(2)}, u32[]{:S(2)}) collective-permute-start(bf16[4,16,5120]{2,1,0:T(8,128)(2,1)S(1)} %get-tuple-element.308), channel_id=1, source_target_pairs={{0,2},{1,17},{2,4},{3,19},{4,6},{5,21},{6,0},{7,23},{8,10},{9,25},... | collective-permute-start | bytes 1966088 | tf_op jit(solution)/shard_map/ppermute | solution.py:49
  277.5 13.6 %collective-permute-start.35 = (bf16[4,16,5120]{2,1,0:T(8,128)(2,1)S(1)}, bf16[4,16,5120]{2,1,0:T(8,128)(2,1)S(1)}, u32[]{:S(2)}, u32[]{:S(2)}) collective-permute-start(bf16[4,16,5120]{2,1,0:T(8,128)(2,1)S(1)} %get-tuple-element.309), channel_id=1, source_target_pairs={{0,6},{1,49},{2,0},{3,51},{4,2},{5,53},{6,4},{7,55},{8,14},{9,57},... | collective-permute-start | bytes 1966088 | tf_op jit(solution)/shard_map/ppermute | solution.py:49
  283.0 12.3 %collective-permute-start.38 = (bf16[32,16,2688]{2,1,0:T(8,128)(2,1)S(1)}, bf16[32,16,2688]{2,1,0:T(8,128)(2,1)S(1)}, u32[]{:S(2)}, u32[]{:S(2)}) collective-permute-start(bf16[32,16,2688]{2,1,0:T(8,128)(2,1)S(1)} %bitcast.224), channel_id=1, source_target_pairs={{0,1},{1,0},{2,3},{3,2},{4,5},{5,4},{6,7},{7,6},{8,9},{9,8},{10,11... | collective-permute-start | bytes 8257544 | tf_op jit(solution)/shard_map/ppermute | solution.py:49
  285.1 11.8 %collective-permute-start.41 = (bf16[8,40,960]{2,1,0:T(8,128)(2,1)S(1)}, bf16[8,40,960]{2,1,0:T(8,128)(2,1)S(1)}, u32[]{:S(2)}, u32[]{:S(2)}) collective-permute-start(bf16[8,40,960]{2,1,0:T(8,128)(2,1)S(1)} %pad_maximum_fusion.15), channel_id=1, source_target_pairs={{0,2},{1,17},{2,4},{3,19},{4,6},{5,21},{6,0},{7,23},{8,10},{9,25},... | collective-permute-start | bytes 1843208 | tf_op jit(solution)/shard_map/ppermute | solution.py:49
  285.1 11.8 %collective-permute-start.42 = (bf16[8,40,960]{2,1,0:T(8,128)(2,1)S(1)}, bf16[8,40,960]{2,1,0:T(8,128)(2,1)S(1)}, u32[]{:S(2)}, u32[]{:S(2)}) collective-permute-start(bf16[8,40,960]{2,1,0:T(8,128)(2,1)S(1)} %pad_maximum_fusion.16), channel_id=1, source_target_pairs={{0,6},{1,49},{2,0},{3,51},{4,2},{5,53},{6,4},{7,55},{8,14},{9,57},... | collective-permute-start | bytes 1843208 | tf_op jit(solution)/shard_map/ppermute | solution.py:49
  301.0 7.5 %collective-permute-start.43 = (bf16[1,40,960]{2,1,0:T(8,128)(2,1)}, bf16[1,40,960]{2,1,0:T(8,128)(2,1)}, u32[]{:S(2)}, u32[]{:S(2)}) collective-permute-start(bf16[1,40,960]{2,1,0:T(8,128)(2,1)} %get-tuple-element.352), channel_id=1, source_target_pairs={{0,16},{1,3},{2,18},{3,5},{4,20},{5,7},{6,22},{7,1},{8,24},{9,11},... | collective-permute-start | bytes 230408 | tf_op jit(solution)/shard_map/ppermute | solution.py:49
  301.0 10.8 %collective-permute-start.44 = (bf16[1,40,960]{2,1,0:T(8,128)(2,1)S(1)}, bf16[1,40,960]{2,1,0:T(8,128)(2,1)}, u32[]{:S(2)}, u32[]{:S(2)}) collective-permute-start(bf16[1,40,960]{2,1,0:T(8,128)(2,1)S(1)} %get-tuple-element.353), channel_id=1, source_target_pairs={{0,48},{1,7},{2,50},{3,1},{4,52},{5,3},{6,54},{7,5},{8,56},{9,15},... | collective-permute-start | bytes 230408 | tf_op jit(solution)/shard_map/ppermute | solution.py:49
  305.2 26.0 %collective-permute-start.36 = (bf16[8,16,5120]{2,1,0:T(8,128)(2,1)}, bf16[8,16,5120]{2,1,0:T(8,128)(2,1)S(1)}, u32[]{:S(2)}, u32[]{:S(2)}) collective-permute-start(bf16[8,16,5120]{2,1,0:T(8,128)(2,1)} %pad_maximum_fusion.7), channel_id=1, source_target_pairs={{0,2},{1,17},{2,4},{3,19},{4,6},{5,21},{6,0},{7,23},{8,10},{9,25},... | collective-permute-start | bytes 3932168 | tf_op jit(solution)/shard_map/ppermute | solution.py:49
  305.9 25.4 %collective-permute-start.37 = (bf16[8,16,5120]{2,1,0:T(8,128)(2,1)}, bf16[8,16,5120]{2,1,0:T(8,128)(2,1)S(1)}, u32[]{:S(2)}, u32[]{:S(2)}) collective-permute-start(bf16[8,16,5120]{2,1,0:T(8,128)(2,1)} %pad_maximum_fusion.8), channel_id=1, source_target_pairs={{0,6},{1,49},{2,0},{3,51},{4,2},{5,53},{6,4},{7,55},{8,14},{9,57},... | collective-permute-start | bytes 3932168 | tf_op jit(solution)/shard_map/ppermute | solution.py:49
  308.5 21.2 %collective-permute-start.39 = (bf16[4,16,2688]{2,1,0:T(8,128)(2,1)}, bf16[4,16,2688]{2,1,0:T(8,128)(2,1)S(1)}, u32[]{:S(2)}, u32[]{:S(2)}) collective-permute-start(bf16[4,16,2688]{2,1,0:T(8,128)(2,1)} %get-tuple-element.344), channel_id=1, source_target_pairs={{0,2},{1,17},{2,4},{3,19},{4,6},{5,21},{6,0},{7,23},{8,10},{9,25},... | collective-permute-start | bytes 1032200 | tf_op jit(solution)/shard_map/ppermute | solution.py:49
  308.5 21.2 %collective-permute-start.40 = (bf16[4,16,2688]{2,1,0:T(8,128)(2,1)}, bf16[4,16,2688]{2,1,0:T(8,128)(2,1)S(1)}, u32[]{:S(2)}, u32[]{:S(2)}) collective-permute-start(bf16[4,16,2688]{2,1,0:T(8,128)(2,1)} %get-tuple-element.345), channel_id=1, source_target_pairs={{0,6},{1,49},{2,0},{3,51},{4,2},{5,53},{6,4},{7,55},{8,14},{9,57},... | collective-permute-start | bytes 1032200 | tf_op jit(solution)/shard_map/ppermute | solution.py:49
  312.8 24.0 %collective-permute-start.47 = (bf16[2,40,960]{2,1,0:T(8,128)(2,1)S(1)}, bf16[2,40,960]{2,1,0:T(8,128)(2,1)S(1)}, u32[]{:S(2)}, u32[]{:S(2)}) collective-permute-start(bf16[2,40,960]{2,1,0:T(8,128)(2,1)S(1)} %pad_maximum_fusion.26), channel_id=1, source_target_pairs={{0,16},{1,3},{2,18},{3,5},{4,20},{5,7},{6,22},{7,1},{8,24},{9,11},... | collective-permute-start | bytes 460808 | tf_op jit(solution)/shard_map/ppermute | solution.py:49
  329.7 7.2 %collective-permute-start.48 = (bf16[2,40,960]{2,1,0:T(8,128)(2,1)S(1)}, bf16[2,40,960]{2,1,0:T(8,128)(2,1)S(1)}, u32[]{:S(2)}, u32[]{:S(2)}) collective-permute-start(bf16[2,40,960]{2,1,0:T(8,128)(2,1)S(1)} %pad_maximum_fusion.27), channel_id=1, source_target_pairs={{0,48},{1,7},{2,50},{3,1},{4,52},{5,3},{6,54},{7,5},{8,56},{9,15},... | collective-permute-start | bytes 460808 | tf_op jit(solution)/shard_map/ppermute | solution.py:49
  331.3 14.0 %collective-permute-start.50 = (bf16[8,16,2688]{2,1,0:T(8,128)(2,1)S(1)}, bf16[8,16,2688]{2,1,0:T(8,128)(2,1)S(1)}, u32[]{:S(2)}, u32[]{:S(2)}) collective-permute-start(bf16[8,16,2688]{2,1,0:T(8,128)(2,1)S(1)} %pad_maximum_fusion.11), channel_id=1, source_target_pairs={{0,2},{1,17},{2,4},{3,19},{4,6},{5,21},{6,0},{7,23},{8,10},{9,25},... | collective-permute-start | bytes 2064392 | tf_op jit(solution)/shard_map/ppermute | solution.py:49
  331.4 13.9 %collective-permute-start.51 = (bf16[8,16,2688]{2,1,0:T(8,128)(2,1)S(1)}, bf16[8,16,2688]{2,1,0:T(8,128)(2,1)S(1)}, u32[]{:S(2)}, u32[]{:S(2)}) collective-permute-start(bf16[8,16,2688]{2,1,0:T(8,128)(2,1)S(1)} %pad_maximum_fusion.12), channel_id=1, source_target_pairs={{0,6},{1,49},{2,0},{3,51},{4,2},{5,53},{6,4},{7,55},{8,14},{9,57},... | collective-permute-start | bytes 2064392 | tf_op jit(solution)/shard_map/ppermute | solution.py:49
  337.9 8.9 %collective-permute-start.49 = (bf16[40,960]{1,0:T(8,128)(2,1)S(1)}, bf16[40,960]{1,0:T(8,128)(2,1)S(1)}, u32[]{:S(2)}, u32[]{:S(2)}) collective-permute-start(bf16[40,960]{1,0:T(8,128)(2,1)S(1)} %slice_bitcast_fusion.17), channel_id=1, source_target_pairs={{0,8},{1,9},{2,10},{3,11},{4,12},{5,13},{6,14},{7,15},{8,0},{9,1},... | collective-permute-start | bytes 230408 | tf_op jit(solution)/shard_map/ppermute | solution.py:49
  338.5 8.2 %collective-permute-start.45 = (bf16[1,16,5120]{2,1,0:T(8,128)(2,1)S(1)}, bf16[1,16,5120]{2,1,0:T(8,128)(2,1)S(1)}, u32[]{:S(2)}, u32[]{:S(2)}) collective-permute-start(bf16[1,16,5120]{2,1,0:T(8,128)(2,1)S(1)} %get-tuple-element.366), channel_id=1, source_target_pairs={{0,16},{1,3},{2,18},{3,5},{4,20},{5,7},{6,22},{7,1},{8,24},{9,11},... | collective-permute-start | bytes 491528 | tf_op jit(solution)/shard_map/ppermute | solution.py:49
  340.6 6.2 %collective-permute-start.46 = (bf16[1,16,5120]{2,1,0:T(8,128)(2,1)S(1)}, bf16[1,16,5120]{2,1,0:T(8,128)(2,1)S(1)}, u32[]{:S(2)}, u32[]{:S(2)}) collective-permute-start(bf16[1,16,5120]{2,1,0:T(8,128)(2,1)S(1)} %get-tuple-element.367), channel_id=1, source_target_pairs={{0,48},{1,7},{2,50},{3,1},{4,52},{5,3},{6,54},{7,5},{8,56},{9,15},... | collective-permute-start | bytes 491528 | tf_op jit(solution)/shard_map/ppermute | solution.py:49
  346.8 7.0 %collective-permute-start.54 = (bf16[1,16,2688]{2,1,0:T(8,128)(2,1)S(1)}, bf16[1,16,2688]{2,1,0:T(8,128)(2,1)S(1)}, u32[]{:S(2)}, u32[]{:S(2)}) collective-permute-start(bf16[1,16,2688]{2,1,0:T(8,128)(2,1)S(1)} %get-tuple-element.387), channel_id=1, source_target_pairs={{0,16},{1,3},{2,18},{3,5},{4,20},{5,7},{6,22},{7,1},{8,24},{9,11},... | collective-permute-start | bytes 258056 | tf_op jit(solution)/shard_map/ppermute | solution.py:49
  349.1 4.7 %collective-permute-start.55 = (bf16[1,16,2688]{2,1,0:T(8,128)(2,1)S(1)}, bf16[1,16,2688]{2,1,0:T(8,128)(2,1)S(1)}, u32[]{:S(2)}, u32[]{:S(2)}) collective-permute-start(bf16[1,16,2688]{2,1,0:T(8,128)(2,1)S(1)} %get-tuple-element.388), channel_id=1, source_target_pairs={{0,48},{1,7},{2,50},{3,1},{4,52},{5,3},{6,54},{7,5},{8,56},{9,15},... | collective-permute-start | bytes 258056 | tf_op jit(solution)/shard_map/ppermute | solution.py:49
  350.5 8.4 %collective-permute-start.52 = (bf16[2,16,5120]{2,1,0:T(8,128)(2,1)S(1)}, bf16[2,16,5120]{2,1,0:T(8,128)(2,1)S(1)}, u32[]{:S(2)}, u32[]{:S(2)}) collective-permute-start(bf16[2,16,5120]{2,1,0:T(8,128)(2,1)S(1)} %pad_maximum_fusion.22), channel_id=1, source_target_pairs={{0,16},{1,3},{2,18},{3,5},{4,20},{5,7},{6,22},{7,1},{8,24},{9,11},... | collective-permute-start | bytes 983048 | tf_op jit(solution)/shard_map/ppermute | solution.py:49
  351.4 7.5 %collective-permute-start.53 = (bf16[2,16,5120]{2,1,0:T(8,128)(2,1)S(1)}, bf16[2,16,5120]{2,1,0:T(8,128)(2,1)S(1)}, u32[]{:S(2)}, u32[]{:S(2)}) collective-permute-start(bf16[2,16,5120]{2,1,0:T(8,128)(2,1)S(1)} %pad_maximum_fusion.23), channel_id=1, source_target_pairs={{0,48},{1,7},{2,50},{3,1},{4,52},{5,3},{6,54},{7,5},{8,56},{9,15},... | collective-permute-start | bytes 983048 | tf_op jit(solution)/shard_map/ppermute | solution.py:49
  353.9 6.8 %collective-permute-start.57 = (bf16[2,16,2688]{2,1,0:T(8,128)(2,1)S(1)}, bf16[2,16,2688]{2,1,0:T(8,128)(2,1)S(1)}, u32[]{:S(2)}, u32[]{:S(2)}) collective-permute-start(bf16[2,16,2688]{2,1,0:T(8,128)(2,1)S(1)} %pad_maximum_fusion.24), channel_id=1, source_target_pairs={{0,16},{1,3},{2,18},{3,5},{4,20},{5,7},{6,22},{7,1},{8,24},{9,11},... | collective-permute-start | bytes 516104 | tf_op jit(solution)/shard_map/ppermute | solution.py:49
  354.0 6.7 %collective-permute-start.58 = (bf16[2,16,2688]{2,1,0:T(8,128)(2,1)S(1)}, bf16[2,16,2688]{2,1,0:T(8,128)(2,1)S(1)}, u32[]{:S(2)}, u32[]{:S(2)}) collective-permute-start(bf16[2,16,2688]{2,1,0:T(8,128)(2,1)S(1)} %pad_maximum_fusion.25), channel_id=1, source_target_pairs={{0,48},{1,7},{2,50},{3,1},{4,52},{5,3},{6,54},{7,5},{8,56},{9,15},... | collective-permute-start | bytes 516104 | tf_op jit(solution)/shard_map/ppermute | solution.py:49
  360.8 4.6 %collective-permute-start.59 = (bf16[16,2688]{1,0:T(8,128)(2,1)S(1)}, bf16[16,2688]{1,0:T(8,128)(2,1)S(1)}, u32[]{:S(2)}, u32[]{:S(2)}) collective-permute-start(bf16[16,2688]{1,0:T(8,128)(2,1)S(1)} %slice_bitcast_fusion.9), channel_id=1, source_target_pairs={{0,8},{1,9},{2,10},{3,11},{4,12},{5,13},{6,14},{7,15},{8,0},{9,1},... | collective-permute-start | bytes 258056 | tf_op jit(solution)/shard_map/ppermute | solution.py:49
  361.3 5.8 %collective-permute-start.56 = (bf16[16,5120]{1,0:T(8,128)(2,1)S(1)}, bf16[16,5120]{1,0:T(8,128)(2,1)S(1)}, u32[]{:S(2)}, u32[]{:S(2)}) collective-permute-start(bf16[16,5120]{1,0:T(8,128)(2,1)S(1)} %get-tuple-element.397), channel_id=1, source_target_pairs={{0,8},{1,9},{2,10},{3,11},{4,12},{5,13},{6,14},{7,15},{8,0},{9,1},... | collective-permute-start | bytes 491528 | tf_op jit(solution)/shard_map/ppermute | solution.py:49
  (93 other events, 787.7 us)
